TPU v7x, 512 devices: a whole 4x8x8 slice. The times are simulated.
512 devices in a mesh: sib: 2 (over x_hi), row: 16 (over z, core), col: 16 (over y, x_lo).
Axes of the slice: x: 4 (x_hi: 2, x_lo: 2; x = x_hi * 2 + x_lo), y: 8, z: 8, core: 2. Of those that a mesh axis runs over, the one named last changes fastest.
Arguments:
- children: bfloat16 [2, 16384, 16384], P('sib', 'row', 'col'), as said below
- block_map: int32 [2, 128], P('sib'), may hold values from 0 to 127, as said below
- inverse_factor: bfloat16 [512, 512], replicated, as said below
Outputs:
- updated: float32 [16384, 16384], P('row', ('sib', 'col'))
Inputs may be any that keep to these rules, and one draw needn't show every extreme that they name: `block_map`: each child's row is a permutation of 0 to 127, and it orders rows and columns alike. Of each aligned run of 8 child blocks, exactly 1 or none go to each aligned run of 8 parent blocks, and at most 1 go to each set of parent blocks p that agree in (p // 4) modulo the number of row groups. `children`: each child's contribution is symmetric. `inverse_factor`: lower triangular with a positive diagonal.
All inputs are finite; a program needn't handle non-finite values.
Results may differ from a plain program's by a relative error of at most 0.0035.
Values may be sent and summed in bfloat16 or wider, within the bound.
No kernel may reach another device: no remote copies, remote signals or barrier semaphores. Data moves between devices by JAX's collectives and lax.ppermute only.
A program may use at most 64 MiB of HBM per device.

v0:
```python
import jax
import jax.numpy as jnp
from jax import lax
from jax.sharding import PartitionSpec as P

BLOCK = 128


def from_partner(shard, axis, bit):
    return lax.ppermute(shard, axis, [(i, i ^ 1 << bit) for i in range(lax.axis_size(axis))])


def from_root(value, axis, source):
    kept = jnp.where(lax.axis_index(axis) == source, value, 0).astype(value.dtype)
    return lax.psum(kept, axis)


def arrival_rank(targets):
    count = targets.shape[-1]
    same = targets[..., :, None] == targets[..., None, :]
    earlier = jnp.arange(count)[None, :] < jnp.arange(count)[:, None]
    return jnp.sum(jnp.logical_and(same, earlier), axis=-1)


def send_index(targets, groups, capacity):
    rank = arrival_rank(targets)
    slot_key = targets * capacity + rank
    slots = jnp.arange(groups * capacity, dtype=jnp.int32)
    match = slot_key[None, :] == slots[:, None]
    found = jnp.any(match, axis=1)
    source = jnp.sum(
        jnp.where(match, jnp.arange(targets.shape[0], dtype=jnp.int32)[None, :], 0), axis=1
    )
    return (source, found)


def receive_index(targets, places, me_index, capacity, width):
    rank = arrival_rank(targets)
    groups = targets.shape[0]
    slot_value = jnp.arange(groups, dtype=jnp.int32)[:, None] * capacity + rank
    hit = jnp.logical_and(
        (targets == me_index)[:, :, None],
        places[:, :, None] == jnp.arange(width, dtype=jnp.int32)[None, None, :],
    )
    return jnp.sum(jnp.where(hit, slot_value[:, :, None], 0), axis=(0, 1))


def relay_columns(tile, grid, groups, width, capacity):
    half = width // 2
    column_group = grid // half
    targets = column_group % groups
    places = column_group // groups * half + grid % half
    me_index = lax.axis_index("col")
    mine = lax.dynamic_index_in_dim(targets, me_index, 0, keepdims=False)
    source, found = send_index(mine, groups, capacity)
    height = tile.shape[0]
    blocks = tile.reshape(height, width, BLOCK)
    chosen = jnp.take(blocks, source, axis=1)
    chosen = jnp.where(found[None, :, None], chosen, jnp.zeros_like(chosen))
    outgoing = jnp.transpose(chosen.reshape(height, groups, capacity, BLOCK), (1, 0, 2, 3))
    outgoing = outgoing.reshape(groups, height, capacity * BLOCK)
    incoming = lax.all_to_all(outgoing, "col", split_axis=0, concat_axis=0, tiled=True)
    landing = receive_index(targets, places, me_index, capacity, width)
    arrived = jnp.transpose(incoming.reshape(groups, height, capacity, BLOCK), (1, 0, 2, 3))
    arrived = arrived.reshape(height, groups * capacity, BLOCK)
    placed = jnp.take(arrived, landing, axis=1)
    return placed.reshape(height, width * BLOCK)


def relay_rows(tile, grid, groups, width, capacity):
    targets = grid // width
    places = grid % width
    me_index = lax.axis_index("row")
    mine = lax.dynamic_index_in_dim(targets, me_index, 0, keepdims=False)
    source, found = send_index(mine, groups, capacity)
    breadth = tile.shape[1]
    blocks = tile.reshape(width, BLOCK, breadth)
    chosen = jnp.take(blocks, source, axis=0)
    chosen = jnp.where(found[:, None, None], chosen, jnp.zeros_like(chosen))
    outgoing = chosen.reshape(groups, capacity, BLOCK, breadth)
    incoming = lax.all_to_all(outgoing, "row", split_axis=0, concat_axis=0, tiled=True)
    landing = receive_index(targets, places, me_index, capacity, width)
    arrived = incoming.reshape(groups * capacity, BLOCK, breadth)
    placed = jnp.take(arrived, landing, axis=0)
    return placed.reshape(width * BLOCK, breadth)


def shards(children, block_map, inverse_factor):
    groups = lax.axis_size("row")
    tile = children[0]
    parents = block_map[0]
    width = parents.shape[0] // groups
    capacity = width // min(width, groups // 2)
    grid = parents.reshape(groups, width)
    tile = relay_columns(tile, grid, groups, width, capacity)
    tile = relay_rows(tile, grid, groups, width, capacity)
    halfway = tile.shape[1] // 2
    sibling = lax.axis_index("sib")
    kept = lax.dynamic_slice_in_dim(tile, sibling * halfway, halfway, 1)
    handed = lax.dynamic_slice_in_dim(tile, (1 - sibling) * halfway, halfway, 1)
    received = from_partner(handed, "sib", 0)
    summed = kept.astype(jnp.float32) + received.astype(jnp.float32)
    panel = from_root(summed.astype(jnp.bfloat16), ("sib", "col"), 0)
    factor_rows = lax.dot_general(
        panel, inverse_factor, (((1,), (1,)), ((), ())), preferred_element_type=jnp.float32
    ).astype(jnp.bfloat16)
    span = summed.shape[1]
    column_group = lax.axis_index("sib") * lax.axis_size("col") + lax.axis_index("col")
    source_rows = from_root(factor_rows, "row", column_group // 2)
    factor_cols = lax.dynamic_slice_in_dim(source_rows, column_group % 2 * span, span, 0)
    product = lax.dot_general(
        factor_rows, factor_cols, (((1,), (1,)), ((), ())), preferred_element_type=jnp.float32
    )
    return summed - product


def solution(mesh):
    in_specs = (P("sib", "row", "col"), P("sib", None), P())
    out_specs = P("row", ("sib", "col"))
    return jax.shard_map(shards, mesh=mesh, in_specs=in_specs, out_specs=out_specs, check_vma=False)
```

profile of v0, /device:TPU:6, one launch (start us, length us, event | category | flops | bytes accessed | tf_op | source)
XLA Modules:
  0.0 578.6 jit_solution(3931839086848285328)
XLA Ops:
  6.5 0.5 broadcast.561
  7.0 1.3 reduce.11
  8.6 0.2 dynamic-slice_reduce_fusion.1
  8.7 0.2 convert_reduce_fusion.3
  9.0 0.2 add_reduce_fusion.1
  9.3 0.2 dynamic-slice_reduce_fusion
  9.5 0.2 convert_reduce_fusion.2
  9.7 0.2 add_reduce_fusion
  10.1 3.9 copy.39
  14.1 3.0 copy.40
  17.1 3.1 gather_fusion
  20.2 4.7 fusion.1
  24.9 8.6 %all-to-all-start = ((bf16[16,1024,128]{2,1,0:T(8,128)(2,1)}), bf16[16,1024,128]{2,1,0:T(8,128)(2,1)}, u32[]{:S(2)}, u32[]{:S(2)}) async-start(bf16[16,1024,128]{2,1,0:T(8,128)(2,1)} %fusion.1), calls=%async_computation | async-start | bytes 8388608 | tf_op jit(solution)/shard_map/all_to_all | solution.py:62
  34.0 95.6 %all-to-all-done = bf16[16,1024,128]{2,1,0:T(8,128)(2,1)} async-done(((bf16[16,1024,128]{2,1,0:T(8,128)(2,1)}), bf16[16,1024,128]{2,1,0:T(8,128)(2,1)}, u32[]{:S(2)}, u32[]{:S(2)}) %all-to-all-start) | async-done | bytes 4194336 | tf_op jit(solution)/shard_map/all_to_all | solution.py:62
  129.5 3.1 gather_fusion.1
  132.7 2.7 copy.41
  135.3 4.2 gather.27
  139.5 1.8 broadcast_select_fusion
  141.3 2.8 gather_fusion.2
  144.1 4.7 fusion.3
  148.8 10.5 %all-to-all-start.1 = ((bf16[16,1,128,1024]{3,2,1,0:T(8,128)(2,1)}), bf16[16,1,128,1024]{3,2,1,0:T(8,128)(2,1)}, u32[]{:S(2)}, u32[]{:S(2)}) async-start(bf16[16,1,128,1024]{3,2,1,0:T(8,128)(2,1)} %fusion.3), calls=%async_computation.1 | async-start | bytes 8388608 | tf_op jit(solution)/shard_map/all_to_all | solution.py:81
  159.4 94.1 %all-to-all-done.1 = bf16[16,1,128,1024]{3,2,1,0:T(8,128)(2,1)} async-done(((bf16[16,1,128,1024]{3,2,1,0:T(8,128)(2,1)}), bf16[16,1,128,1024]{3,2,1,0:T(8,128)(2,1)}, u32[]{:S(2)}, u32[]{:S(2)}) %all-to-all-start.1) | async-done | bytes 4194336 | tf_op jit(solution)/shard_map/all_to_all | solution.py:81
  253.6 4.2 gather_fusion.3
  257.8 1.9 bitcast_select_fusion.2
  259.6 1.1 constant_dynamic-slice_fusion
  260.7 3.3 collective-permute-start
  264.0 25.1 %collective-permute-done = bf16[1024,512]{1,0:T(8,128)(2,1)} collective-permute-done((bf16[1024,512]{1,0:T(8,128)(2,1)}, bf16[1024,512]{1,0:T(8,128)(2,1)}, u32[]{:S(2)}, u32[]{:S(2)}) %collective-permute-start) | collective-permute-done | bytes 1048608 | tf_op jit(solution)/shard_map/ppermute | solution.py:10
  289.1 2.6 fusion.6
  291.8 155.8 %all-reduce.3.cloned.1.call-done = bf16[1024,512]{1,0:T(8,128)(2,1)} async-done(((bf16[1024,512]{1,0:T(8,128)(2,1)}), bf16[1024,512]{1,0:T(8,128)(2,1)}) %all-reduce.3.cloned.1.call-update) | async-done | bytes 1048592 | tf_op jit(solution)/shard_map/psum | solution.py:15
  447.6 3.3 broadcast_select_fusion.1
  451.0 117.0 %all-reduce.5.cloned.1.call-done = bf16[1024,512]{1,0:T(8,128)(2,1)} async-done(((bf16[1024,512]{1,0:T(8,128)(2,1)}), bf16[1024,512]{1,0:T(8,128)(2,1)}) %all-reduce.5.cloned.1.call-update) | async-done | bytes 1048592 | tf_op jit(solution)/shard_map/psum | solution.py:15
  568.0 3.8 fusion.4
  (33 shorter events, 1.3 us)
Async XLA Ops:
  6.5 441.1 %copy-start = (bf16[512,512]{1,0:T(8,128)(2,1)S(1)}, bf16[512,512]{1,0:T(8,128)(2,1)}, u32[]{:S(2)}) copy-start(bf16[512,512]{1,0:T(8,128)(2,1)} %param.5) | copy-start | bytes 1572868
  24.9 104.7 %all-to-all-start = ((bf16[16,1024,128]{2,1,0:T(8,128)(2,1)}), bf16[16,1024,128]{2,1,0:T(8,128)(2,1)}, u32[]{:S(2)}, u32[]{:S(2)}) async-start(bf16[16,1024,128]{2,1,0:T(8,128)(2,1)} %fusion.1), calls=%async_computation | async-start | bytes 8388608 | tf_op jit(solution)/shard_map/all_to_all | solution.py:62
  148.8 104.8 %all-to-all-start.1 = ((bf16[16,1,128,1024]{3,2,1,0:T(8,128)(2,1)}), bf16[16,1,128,1024]{3,2,1,0:T(8,128)(2,1)}, u32[]{:S(2)}, u32[]{:S(2)}) async-start(bf16[16,1,128,1024]{3,2,1,0:T(8,128)(2,1)} %fusion.3), calls=%async_computation.1 | async-start | bytes 8388608 | tf_op jit(solution)/shard_map/all_to_all | solution.py:81
  159.2 288.4 %all-reduce.3.cloned.1.call-start = ((), (), s32[]{:S(2)}) async-start(), calls=%async_computation.2 | async-start | bytes 2097152 | tf_op jit(solution)/shard_map/psum | solution.py:15
  260.7 28.4 %collective-permute-start = (bf16[1024,512]{1,0:T(8,128)(2,1)}, bf16[1024,512]{1,0:T(8,128)(2,1)}, u32[]{:S(2)}, u32[]{:S(2)}) collective-permute-start(bf16[1024,512]{1,0:T(8,128)(2,1)} %constant_dynamic-slice_fusion), channel_id=1, source_target_pairs={{0,256},{256,0},{1,257},{257,1},{2,258},{258,2},{3,259},{259,3},{4... | collective-permute-start | bytes 3145736 | tf_op jit(solution)/shard_map/ppermute | solution.py:10
  291.7 276.2 %all-reduce.5.cloned.1.call-start = ((), (), s32[]{:S(2)}) async-start(), calls=%async_computation.3 | async-start | bytes 2097152 | tf_op jit(solution)/shard_map/psum | solution.py:15
Sparse Core Ops, SparseCore 0:
  291.9 155.7 all-reduce.2
  451.1 116.8 all-reduce.4
where the time goes:
time: 580 us; the launch traced here: 579 us
  waiting for transfers between devices  488 us (84%)
  local copies, waits for them, and re-layouts  29.4 us (5%)
  starting transfers between devices  22.4 us (4%)
  other arithmetic  18.4 us (3%)
  between operations  13.6 us (2%)
  matrix products  7.05 us (1%)
    psum x2, waiting for transfers between devices, from_root(): return lax.psum(kept, axis)  273 us
    all_to_all x1, waiting for transfers between devices, relay_columns(): lax.all_to_all(outgoing, 'col', split_axis=0, concat_axis=0, tiled=True)  95.6 us
    all_to_all x1, waiting for transfers between devices, relay_rows(): lax.all_to_all(outgoing, 'row', split_axis=0, concat_axis=0, tiled=True)  94.1 us
    ppermute x1, waiting for transfers between devices, from_partner(): lax.ppermute(shard, axis, [(i, i ^ 1 << bit) for i in range(lax.axis_size...  25.1 us
  transfers between devices with their start and end apart: 5, of which 5 were waited for; matrix products, arithmetic and copies ran while one was open for 0% of the time, Pallas kernels for 0%

commit v1 on v0

v1 whole, which is shorter than its diff:
```python
import jax
import jax.numpy as jnp
from jax import lax
from jax.experimental import pallas as pl
from jax.experimental.pallas import tpu as pltpu
from jax.sharding import PartitionSpec as P

B = 128
H = B // 2
W = 8
G = 16
PANEL = 512
SMEM = pl.BlockSpec(memory_space=pltpu.SMEM)
ANY = pl.BlockSpec(memory_space=pl.ANY)
VMEM_LIMIT = 40 * 1024 * 1024


def params(flops=0, moved=0):
    return dict(
        compiler_params=pltpu.CompilerParams(vmem_limit_bytes=VMEM_LIMIT),
        cost_estimate=pl.CostEstimate(flops=flops, bytes_accessed=moved, transcendentals=0),
    )


def bf16(*shape):
    return jax.ShapeDtypeStruct(shape, jnp.bfloat16)


def ring(core, distance):
    return lax.bitwise_and(jnp.where(core == 0, distance, -distance), 7)


def row_slot(map_ref, q):
    row = lax.axis_index("row")
    target = map_ref[row * W + q] // W
    core = target % 2
    return lax.bitwise_xor(core, row % 2), ring(core, target // 2 - row // 2)


def row_landing(inv_ref, i):
    row = lax.axis_index("row")
    source = inv_ref[row * W + i] // W
    return lax.bitwise_xor(source % 2, row % 2), ring(row % 2, row // 2 - source // 2)


def col_slot(map_ref, v):
    return (map_ref[lax.axis_index("col") * W + v] // (W // 2)) % G


def col_landing(inv_ref, half, j):
    return inv_ref[(half * G + lax.axis_index("col")) * (W // 2) + j] // W


def lanes(j):
    return pl.ds(pl.multiple_of(j * B, B), B)


def pack(map_ref, tile, a, ob, sem_a, sem_b):
    for v in range(W):
        pltpu.make_async_copy(tile.at[:, pl.ds(0, H), pl.ds(v * B, B)], a.at[col_slot(map_ref, v)], sem_a).start()
    for q in range(W):
        e, k = row_slot(map_ref, q)
        pltpu.make_async_copy(tile.at[q, pl.ds(H, H), :], ob.at[e, k], sem_b).start()
    pltpu.make_async_copy(a.at[pl.ds(0, W)], a.at[pl.ds(0, W)], sem_a).wait()
    pltpu.make_async_copy(ob.at[0], ob.at[0], sem_b).wait()


def cols_to_rows(map_ref, inv_ref, arrived, ob, sem):
    @pl.loop(0, W)
    def _(q):
        e, k = row_slot(map_ref, q)
        for j in range(W):
            pltpu.make_async_copy(
                arrived.at[col_landing(inv_ref, j // 4, j % 4), q], ob.at[e, k, :, pl.ds(j * B, B)], sem
            ).start()
    pltpu.make_async_copy(ob.at[0], ob.at[0], sem).wait()


def rows_to_cols(map_ref, inv_ref, *refs):
    arrived, a, sem = refs[:8], refs[8], refs[9]

    @pl.loop(0, W)
    def _(i):
        e, k = row_landing(inv_ref, i)
        for step in range(8):
            @pl.when(k == step)
            def _():
                for v in range(W):
                    pltpu.make_async_copy(
                        arrived[step].at[e, :, pl.ds(v * B, B)], a.at[col_slot(map_ref, v), i], sem
                    ).start()
    pltpu.make_async_copy(a.at[pl.ds(0, W)], a.at[pl.ds(0, W)], sem).wait()


def split_rows(inv_ref, *refs):
    arrived, hand, kept, sem_h, sem_k = refs[:8], refs[8], refs[9], refs[10], refs[11]
    sib = lax.axis_index("sib")
    mine = pl.ds(pl.multiple_of(sib * PANEL, PANEL), PANEL)
    other = pl.ds(pl.multiple_of((1 - sib) * PANEL, PANEL), PANEL)

    @pl.loop(0, W)
    def _(i):
        e, k = row_landing(inv_ref, i)
        for step in range(8):
            @pl.when(k == step)
            def _():
                pltpu.make_async_copy(arrived[step].at[e, :, other], hand.at[i], sem_h).start()
                pltpu.make_async_copy(arrived[step].at[e, :, mine], kept.at[i], sem_k).start()
    pltpu.make_async_copy(hand, hand, sem_h).wait()
    pltpu.make_async_copy(kept, kept, sem_k).wait()


def split_cols(inv_ref, arrived, hand, kept, sem_h, sem_k):
    sib = lax.axis_index("sib")
    for j in range(W // 2):
        place = pl.ds(j * B, B)
        pltpu.make_async_copy(arrived.at[col_landing(inv_ref, 1 - sib, j)], hand.at[:, :, place], sem_h).start()
        pltpu.make_async_copy(arrived.at[col_landing(inv_ref, sib, j)], kept.at[:, :, place], sem_k).start()
    pltpu.make_async_copy(hand, hand, sem_h).wait()
    pltpu.make_async_copy(kept, kept, sem_k).wait()


def update(kept_a, kept_b, got_a, got_b, rows, cols, out):
    product = lax.dot_general(rows[...], cols[...], (((1,), (1,)), ((), ())), preferred_element_type=jnp.float32)
    f32 = jnp.float32
    out[0, 0:H] = kept_a[0].astype(f32) + got_a[0].astype(f32) - product[0:H]
    out[0, H:B] = kept_b[0].astype(f32) + got_b[0].astype(f32) - product[H:B]


def rows_permute(ob):
    other = lax.ppermute(ob[1], "row", [(i, i ^ 1) for i in range(G)])
    both = [jnp.stack([ob[0, k], other[k]]) for k in range(8)]
    arrived = [both[0]]
    for k in range(1, 8):
        pairs = [(z * 2 + c, (z + (k if c == 0 else -k)) % 8 * 2 + c) for z in range(8) for c in range(2)]
        arrived.append(lax.ppermute(both[k], "row", pairs))
    return arrived


def panel_piece(tile, maps, inv):
    row, col = lax.axis_index("row"), lax.axis_index("col")
    mine = lax.dynamic_slice_in_dim(maps, col * W, W, 0)
    owned = jnp.sum(jnp.where(mine < 4, jnp.arange(W, dtype=jnp.int32), 0))
    column = lax.dynamic_slice(tile, (0, owned * B), (W * B, B))
    out = jnp.transpose(column.reshape(W, G, 8, B), (1, 0, 2, 3))
    got = lax.all_to_all(out, "col", 0, 0, tiled=True)
    got = jnp.transpose(jnp.take(got, inv[:4] // W, axis=0, mode="clip"), (1, 0, 2, 3))
    targets = lax.dynamic_slice_in_dim(maps, row * W, W, 0) // W
    match = targets[None, :] == jnp.arange(G, dtype=jnp.int32)[:, None]
    source = jnp.sum(jnp.where(match, jnp.arange(W, dtype=jnp.int32)[None, :], 0), axis=1)
    got = lax.all_to_all(jnp.take(got, source, axis=0, mode="clip"), "row", 0, 0, tiled=True)
    landing = lax.dynamic_slice_in_dim(inv, row * W, W, 0) // W
    got = jnp.transpose(jnp.take(got, landing, axis=0, mode="clip"), (0, 2, 1, 3)).reshape(W * 8, PANEL)
    partner = lax.ppermute(got, "sib", [(0, 1), (1, 0)])
    return (got.astype(jnp.float32) + partner.astype(jnp.float32)).astype(jnp.bfloat16)


def panel_parts(piece):
    rows = lax.all_gather(piece, "col", axis=0, tiled=True)
    rows = jnp.transpose(rows.reshape(G, W, 8, PANEL), (1, 0, 2, 3)).reshape(W * B, PANEL)
    sib, row = lax.axis_index("sib"), lax.axis_index("row")
    half = jnp.where(sib == row // 8, 0, 1)
    send = lax.dynamic_slice_in_dim(piece, half * (W * 4), W * 4, 0)
    pairs = []
    for s in range(2):
        for g in range(G):
            for c in range(G):
                x = 0 if s == g // 8 else 1
                pairs.append((s * 256 + g * G + c, (g // 8) * 256 + c * G + (g % 8) * 2 + x))
    got = lax.ppermute(send, ("sib", "row", "col"), pairs)
    cols = lax.all_gather(got, "row", axis=0, tiled=True)
    cols = jnp.transpose(cols.reshape(G, W // 2, 8, PANEL), (1, 0, 2, 3)).reshape(PANEL, PANEL)
    return rows, cols


def factor(panel, inverse_factor):
    return lax.dot_general(
        panel, inverse_factor, (((1,), (1,)), ((), ())), preferred_element_type=jnp.float32
    ).astype(jnp.bfloat16)


def shards(children, block_map, inverse_factor):
    tile = children[0]
    maps = block_map[0]
    blocks = jnp.arange(maps.shape[0], dtype=jnp.int32)
    inv = jnp.sum(jnp.where(maps[None, :] == blocks[:, None], blocks[None, :], 0), axis=1)
    dma = pltpu.SemaphoreType.DMA
    MiB = 1 << 20

    slots, rows = bf16(G, W, H, B), bf16(2, 8, H, W * B)
    half = bf16(W, H, PANEL)
    send_a, send_b = pl.pallas_call(
        pack, out_shape=(slots, rows), in_specs=[SMEM, ANY], out_specs=(ANY, ANY), scratch_shapes=[dma, dma],
        **params(moved=4 * MiB),
    )(maps, tile.reshape(W, B, W * B))

    piece = panel_piece(tile, maps, inv)

    got_a = lax.all_to_all(send_a, "col", 0, 0, tiled=True)
    got_b = rows_permute(send_b)

    panel_rows, panel_cols = panel_parts(piece)

    send_a = pl.pallas_call(
        cols_to_rows, out_shape=rows, in_specs=[SMEM, SMEM, ANY], out_specs=ANY, scratch_shapes=[dma],
        **params(moved=2 * MiB),
    )(maps, inv, got_a)
    send_b = pl.pallas_call(
        rows_to_cols, out_shape=slots, in_specs=[SMEM, SMEM] + [ANY] * 8, out_specs=ANY, scratch_shapes=[dma],
        **params(moved=2 * MiB),
    )(maps, inv, *got_b)

    got_a = rows_permute(send_a)
    got_b = lax.all_to_all(send_b, "col", 0, 0, tiled=True)

    hand_a, kept_a = pl.pallas_call(
        split_rows, out_shape=(half, half), in_specs=[SMEM] + [ANY] * 8, out_specs=(ANY, ANY), scratch_shapes=[dma, dma],
        **params(moved=2 * MiB),
    )(inv, *got_a)
    hand_b, kept_b = pl.pallas_call(
        split_cols, out_shape=(half, half), in_specs=[SMEM, ANY], out_specs=(ANY, ANY), scratch_shapes=[dma, dma],
        **params(moved=2 * MiB),
    )(inv, got_b)
    swap = [(0, 1), (1, 0)]
    hand_a = lax.ppermute(hand_a, "sib", swap)
    hand_b = lax.ppermute(hand_b, "sib", swap)

    factor_rows = factor(panel_rows, inverse_factor)
    factor_cols = factor(panel_cols, inverse_factor)
    piece_spec = pl.BlockSpec((1, H, PANEL), lambda i: (i, 0, 0))
    out = pl.pallas_call(
        update, grid=(W,), out_shape=jax.ShapeDtypeStruct((W, B, PANEL), jnp.float32),
        in_specs=[piece_spec] * 4 + [
            pl.BlockSpec((B, PANEL), lambda i: (i, 0)), pl.BlockSpec((PANEL, PANEL), lambda i: (0, 0))],
        out_specs=pl.BlockSpec((1, B, PANEL), lambda i: (i, 0, 0)),
        **params(flops=2 * W * B * PANEL * PANEL, moved=6 * MiB),
    )(kept_a, kept_b, hand_a, hand_b, factor_rows, factor_cols)
    return out.reshape(W * B, PANEL)


def solution(mesh):
    in_specs = (P("sib", "row", "col"), P("sib", None), P())
    out_specs = P("row", ("sib", "col"))
    return jax.shard_map(shards, mesh=mesh, in_specs=in_specs, out_specs=out_specs, check_vma=False)
```

time: 580 us -> 275 us (0.47)
  waiting for transfers between devices: 488 us -> 47 us
  starting transfers between devices: 22.4 us -> 128 us
  Pallas kernels: 0 us -> 30.2 us
  blocking collectives: 0 us -> 25.9 us
  local copies, waits for them, and re-layouts: 29.4 us -> 17.5 us
  other arithmetic: 18.4 us -> 7.8 us
  matrix products: 7.05 us -> 1.21 us
    psum x2 -> x0, waiting for transfers between devices: 273 us -> none  [from_root(): return lax.psum(kept, axis)]
    all_to_all x2 -> x4, waiting for transfers between devices: 190 us -> 12.6 us  [the longest x1 8.94 us: panel_piece(): got = lax.all_to_all(out, 'col', 0, 0, tiled=True)]
    ppermute x1 -> x20, starting transfers between devices: 3.3 us -> 95.6 us  [the longest x14 77.4 us: rows_permute(): arrived.append(lax.ppermute(both[k], 'row', pairs))]
    pallas_call x0 -> x6, Pallas kernels: none -> 30.2 us  [the longest x1 17.6 us: shards(): pl.pallas_call(split_cols, out_shape=(half, half), in_specs=[SMEM, ANY],...]
    all_gather x0 -> x1, blocking collectives: none -> 25.9 us  [panel_parts(): cols = lax.all_gather(got, 'row', axis=0, tiled=True)]
    gather x6 -> x3, local copies, waits for them, and re-layouts: 20 us -> 2.39 us  [the longest x1 1.26 us: panel_piece(): jnp.take(got, source, axis=0, mode='clip')]
    all_to_all x2 -> x4, starting transfers between devices: 19 us -> 32.2 us  [the longest x1 10.4 us: panel_piece(): lax.all_to_all(jnp.take(got, source, axis=0, mode='clip'), 'row', 0, 0, t...]
    select_n x8 -> x2, other arithmetic: 11 us -> 0.1 us  [the longest x1 0.09 us: panel_piece(): landing = lax.dynamic_slice_in_dim(inv, row * W, W, 0) // W]
  transfers between devices with their start and end apart: 5 -> 25, of which waited for: 5 -> 10; matrix products, arithmetic and copies ran while one was open for 0% -> 5% of each run, Pallas kernels for 0% -> 10%
where the time goes in v1:
time: 275 us; the launch traced here: 272 us
  starting transfers between devices  128 us (47%)
  waiting for transfers between devices  47 us (17%)
  Pallas kernels  30.2 us (11%)
  blocking collectives  25.9 us (9%)
  local copies, waits for them, and re-layouts  17.5 us (6%)
  between operations  14.6 us (5%)
  other arithmetic  7.8 us (3%)
    ppermute x14, starting transfers between devices, rows_permute(): arrived.append(lax.ppermute(both[k], 'row', pairs))  77.4 us
    all_gather x1, blocking collectives, panel_parts(): cols = lax.all_gather(got, 'row', axis=0, tiled=True)  25.9 us
    pallas_call x1, Pallas kernels, shards(): pl.pallas_call(split_cols, out_shape=(half, half), in_specs=[SMEM, ANY],...  17.6 us
    ppermute x14, waiting for transfers between devices, rows_permute(): arrived.append(lax.ppermute(both[k], 'row', pairs))  14 us
    ppermute x1, waiting for transfers between devices, shards(): hand_a = lax.ppermute(hand_a, 'sib', swap)  11.1 us
    all_to_all x1, starting transfers between devices, panel_piece(): lax.all_to_all(jnp.take(got, source, axis=0, mode='clip'), 'row', 0, 0, t...  10.4 us
    all_to_all x1, waiting for transfers between devices, panel_piece(): got = lax.all_to_all(out, 'col', 0, 0, tiled=True)  8.94 us
    all_to_all x1, starting transfers between devices, panel_piece(): got = lax.all_to_all(out, 'col', 0, 0, tiled=True)  8.57 us
  transfers between devices with their start and end apart: 25, of which 10 were waited for; matrix products, arithmetic and copies ran while one was open for 5% of the time, Pallas kernels for 10%

profile of v1, /device:TPU:6, one launch (start us, length us, event | category | flops | bytes accessed | tf_op | source)
XLA Modules:
  0.0 272.2 jit_solution(5066211381085184727)
XLA Ops:
  10.5 8.6 %all-to-all-start.2 = ((bf16[16,8,8,128]{3,2,1,0:T(8,128)(2,1)}), bf16[16,8,8,128]{3,2,1,0:T(8,128)(2,1)S(1)}, u32[]{:S(2)}, u32[]{:S(2)}) async-start(bf16[16,8,8,128]{3,2,1,0:T(8,128)(2,1)} %copy.11), calls=%async_computation.2 | async-start | bytes 524288 | tf_op jit(solution)/shard_map/all_to_all | solution.py:146
  20.7 8.9 %all-to-all-done.2 = bf16[16,8,8,128]{3,2,1,0:T(8,128)(2,1)S(1)} async-done(((bf16[16,8,8,128]{3,2,1,0:T(8,128)(2,1)}), bf16[16,8,8,128]{3,2,1,0:T(8,128)(2,1)S(1)}, u32[]{:S(2)}, u32[]{:S(2)}) %all-to-all-start.2) | async-done | bytes 262176 | tf_op jit(solution)/shard_map/all_to_all | solution.py:146
  31.4 10.4 %all-to-all-start.3 = ((bf16[16,4,8,128]{3,2,1,0:T(8,128)(2,1)}), bf16[16,4,8,128]{3,2,1,0:T(8,128)(2,1)S(1)}, u32[]{:S(2)}, u32[]{:S(2)}) async-start(bf16[16,4,8,128]{3,2,1,0:T(8,128)(2,1)} %gather_fusion.1), calls=%async_computation.3 | async-start | bytes 262144 | tf_op jit(solution)/shard_map/all_to_all | solution.py:151
  46.9 3.7 %all-to-all-done.3 = bf16[16,4,8,128]{3,2,1,0:T(8,128)(2,1)S(1)} async-done(((bf16[16,4,8,128]{3,2,1,0:T(8,128)(2,1)}), bf16[16,4,8,128]{3,2,1,0:T(8,128)(2,1)S(1)}, u32[]{:S(2)}, u32[]{:S(2)}) %all-to-all-start.3) | async-done | bytes 131104 | tf_op jit(solution)/shard_map/all_to_all | solution.py:151
  50.6 5.1 %all-to-all-start = ((bf16[16,8,64,128]{3,2,1,0:T(8,128)(2,1)}), bf16[16,8,64,128]{3,2,1,0:T(8,128)(2,1)S(1)}, u32[]{:S(2)}, u32[]{:S(2)}) async-start(bf16[16,8,64,128]{3,2,1,0:T(8,128)(2,1)} %copy-done.3), calls=%async_computation | async-start | bytes 4194304 | tf_op jit(solution)/shard_map/all_to_all | solution.py:199
  57.2 2.5 collective-permute-start.8
  62.0 2.5 collective-permute-start.10
  64.6 4.2 %collective-permute-start.11 = (bf16[2,64,1024]{2,1,0:T(8,128)(2,1)S(1)}, bf16[2,64,1024]{2,1,0:T(8,128)(2,1)S(1)}, u32[]{:S(2)}, u32[]{:S(2)}) collective-permute-start(bf16[2,64,1024]{2,1,0:T(8,128)(2,1)S(1)} %pad_maximum_fusion.11), channel_id=1, source_target_pairs={{0,96},{16,176},{32,128},{48,208},{64,160},{80,240},{96,192},{112,... | collective-permute-start | bytes 786440 | tf_op jit(solution)/shard_map/ppermute | solution.py:136
  68.9 5.3 %collective-permute-start.12 = (bf16[2,64,1024]{2,1,0:T(8,128)(2,1)S(1)}, bf16[2,64,1024]{2,1,0:T(8,128)(2,1)S(1)}, u32[]{:S(2)}, u32[]{:S(2)}) collective-permute-start(bf16[2,64,1024]{2,1,0:T(8,128)(2,1)S(1)} %pad_maximum_fusion.12), channel_id=1, source_target_pairs={{0,128},{16,144},{32,160},{48,176},{64,192},{80,208},{96,224},{112... | collective-permute-start | bytes 786440 | tf_op jit(solution)/shard_map/ppermute | solution.py:136
  74.2 4.0 %collective-permute-start.13 = (bf16[2,64,1024]{2,1,0:T(8,128)(2,1)S(1)}, bf16[2,64,1024]{2,1,0:T(8,128)(2,1)S(1)}, u32[]{:S(2)}, u32[]{:S(2)}) collective-permute-start(bf16[2,64,1024]{2,1,0:T(8,128)(2,1)S(1)} %pad_maximum_fusion.13), channel_id=1, source_target_pairs={{0,160},{16,112},{32,192},{48,144},{64,224},{80,176},{96,0},{112,2... | collective-permute-start | bytes 786440 | tf_op jit(solution)/shard_map/ppermute | solution.py:136
  78.2 4.6 %collective-permute-start.14 = (bf16[2,64,1024]{2,1,0:T(8,128)(2,1)S(1)}, bf16[2,64,1024]{2,1,0:T(8,128)(2,1)S(1)}, u32[]{:S(2)}, u32[]{:S(2)}) collective-permute-start(bf16[2,64,1024]{2,1,0:T(8,128)(2,1)S(1)} %pad_maximum_fusion.14), channel_id=1, source_target_pairs={{0,192},{16,80},{32,224},{48,112},{64,0},{80,144},{96,32},{112,176... | collective-permute-start | bytes 786440 | tf_op jit(solution)/shard_map/ppermute | solution.py:136
  83.0 2.6 collective-permute-start.15
  85.6 12.2 %collective-permute-start.9 = (bf16[2,64,1024]{2,1,0:T(8,128)(2,1)S(1)}, bf16[2,64,1024]{2,1,0:T(8,128)(2,1)S(1)}, u32[]{:S(2)}, u32[]{:S(2)}) collective-permute-start(bf16[2,64,1024]{2,1,0:T(8,128)(2,1)S(1)} %pad_maximum_fusion.9), channel_id=1, source_target_pairs={{0,32},{16,240},{32,64},{48,16},{64,96},{80,48},{96,128},{112,80},... | collective-permute-start | bytes 786440 | tf_op jit(solution)/shard_map/ppermute | solution.py:136
  98.7 3.7 %collective-permute-done.13.refs_5_ = bf16[2,64,1024]{2,1,0:T(8,128)(2,1)S(1)} collective-permute-done((bf16[2,64,1024]{2,1,0:T(8,128)(2,1)S(1)}, bf16[2,64,1024]{2,1,0:T(8,128)(2,1)S(1)}, u32[]{:S(2)}, u32[]{:S(2)}) %collective-permute-start.13) | collective-permute-done | bytes 262176 | tf_op jit(solution)/shard_map/ppermute | solution.py:136
  102.4 7.4 %collective-permute-done.14.refs_6_ = bf16[2,64,1024]{2,1,0:T(8,128)(2,1)S(1)} collective-permute-done((bf16[2,64,1024]{2,1,0:T(8,128)(2,1)S(1)}, bf16[2,64,1024]{2,1,0:T(8,128)(2,1)S(1)}, u32[]{:S(2)}, u32[]{:S(2)}) %collective-permute-start.14) | collective-permute-done | bytes 262176 | tf_op jit(solution)/shard_map/ppermute | solution.py:136
  114.2 8.2 %all-to-all-start.1 = ((bf16[16,8,64,128]{3,2,1,0:T(8,128)(2,1)}), bf16[16,8,64,128]{3,2,1,0:T(8,128)(2,1)}, u32[]{:S(2)}, u32[]{:S(2)}) async-start(bf16[16,8,64,128]{3,2,1,0:T(8,128)(2,1)} %shard_map.40), calls=%async_computation.1 | async-start | bytes 4194304 | tf_op jit(solution)/shard_map/all_to_all | solution.py:214
  125.6 2.9 %collective-permute-start = (bf16[8,64,1024]{2,1,0:T(8,128)(2,1)S(1)}, bf16[8,64,1024]{2,1,0:T(8,128)(2,1)S(1)}, u32[]{:S(2)}, u32[]{:S(2)}) collective-permute-start(bf16[8,64,1024]{2,1,0:T(8,128)(2,1)S(1)} %slice_bitcast_fusion), channel_id=1, source_target_pairs={{0,16},{16,0},{32,48},{48,32},{64,80},{80,64},{96,112},{112,96},{1... | collective-permute-start | bytes 3145736 | tf_op jit(solution)/shard_map/ppermute | solution.py:131
  129.1 3.3 %collective-permute-start.18 = (bf16[64,512]{1,0:T(8,128)(2,1)S(1)}, bf16[64,512]{1,0:T(8,128)(2,1)S(1)}, u32[]{:S(2)}, u32[]{:S(2)}) collective-permute-start(bf16[64,512]{1,0:T(8,128)(2,1)S(1)} %bitcast.76), channel_id=1, source_target_pairs={{0,256},{256,0},{1,257},{257,1},{2,258},{258,2},{3,259},{259,3},{4... | collective-permute-start | bytes 196616 | tf_op jit(solution)/shard_map/ppermute | solution.py:154
  132.5 4.3 %collective-permute-done.18 = bf16[64,512]{1,0:T(8,128)(2,1)S(1)} collective-permute-done((bf16[64,512]{1,0:T(8,128)(2,1)S(1)}, bf16[64,512]{1,0:T(8,128)(2,1)S(1)}, u32[]{:S(2)}, u32[]{:S(2)}) %collective-permute-start.18) | collective-permute-done | bytes 65568 | tf_op jit(solution)/shard_map/ppermute | solution.py:154
  141.9 6.7 %collective-permute-start.7 = (bf16[2,64,1024]{2,1,0:T(8,128)(2,1)S(1)}, bf16[2,64,1024]{2,1,0:T(8,128)(2,1)S(1)}, u32[]{:S(2)}, u32[]{:S(2)}) collective-permute-start(bf16[2,64,1024]{2,1,0:T(8,128)(2,1)S(1)} %pad_maximum_fusion.7), channel_id=1, source_target_pairs={{0,224},{16,48},{32,0},{48,80},{64,32},{80,112},{96,64},{112,144},... | collective-permute-start | bytes 786440 | tf_op jit(solution)/shard_map/ppermute | solution.py:136
  148.7 4.6 %collective-permute-start.6 = (bf16[2,64,1024]{2,1,0:T(8,128)(2,1)S(1)}, bf16[2,64,1024]{2,1,0:T(8,128)(2,1)S(1)}, u32[]{:S(2)}, u32[]{:S(2)}) collective-permute-start(bf16[2,64,1024]{2,1,0:T(8,128)(2,1)S(1)} %pad_maximum_fusion.6), channel_id=1, source_target_pairs={{0,192},{16,80},{32,224},{48,112},{64,0},{80,144},{96,32},{112,176... | collective-permute-start | bytes 786440 | tf_op jit(solution)/shard_map/ppermute | solution.py:136
  154.0 5.7 %collective-permute-start.5 = (bf16[2,64,1024]{2,1,0:T(8,128)(2,1)}, bf16[2,64,1024]{2,1,0:T(8,128)(2,1)S(1)}, u32[]{:S(2)}, u32[]{:S(2)}) collective-permute-start(bf16[2,64,1024]{2,1,0:T(8,128)(2,1)} %pad_maximum_fusion.5), channel_id=1, source_target_pairs={{0,160},{16,112},{32,192},{48,144},{64,224},{80,176},{96,0},{112,2... | collective-permute-start | bytes 786440 | tf_op jit(solution)/shard_map/ppermute | solution.py:136
  160.4 4.6 %collective-permute-start.4 = (bf16[2,64,1024]{2,1,0:T(8,128)(2,1)}, bf16[2,64,1024]{2,1,0:T(8,128)(2,1)S(1)}, u32[]{:S(2)}, u32[]{:S(2)}) collective-permute-start(bf16[2,64,1024]{2,1,0:T(8,128)(2,1)} %pad_maximum_fusion.4), channel_id=1, source_target_pairs={{0,128},{16,144},{32,160},{48,176},{64,192},{80,208},{96,224},{112... | collective-permute-start | bytes 786440 | tf_op jit(solution)/shard_map/ppermute | solution.py:136
  167.2 15.9 %collective-permute-start.3 = (bf16[2,64,1024]{2,1,0:T(8,128)(2,1)}, bf16[2,64,1024]{2,1,0:T(8,128)(2,1)S(1)}, u32[]{:S(2)}, u32[]{:S(2)}) collective-permute-start(bf16[2,64,1024]{2,1,0:T(8,128)(2,1)} %pad_maximum_fusion.3), channel_id=1, source_target_pairs={{0,96},{16,176},{32,128},{48,208},{64,160},{80,240},{96,192},{112,... | collective-permute-start | bytes 786440 | tf_op jit(solution)/shard_map/ppermute | solution.py:136
  185.1 2.5 collective-permute-start.1
  187.6 25.9 %all_gather.7 = bf16[512,512]{1,0:T(8,128)(2,1)S(1)} all-gather(bf16[32,512]{1,0:T(8,128)(2,1)S(1)} %collective-permute-done.19), channel_id=1, replica_groups=mesh['sib'=2,'row'=16,'col'=16] {'row'}, dimensions={0}, use_global_device_ids=true | all-gather | bytes 557056 | tf_op jit(solution)/shard_map/all_gather | solution.py:171
  214.4 17.6 %shard_map.41 = (bf16[8,64,512]{2,1,0:T(8,128)(2,1)}, bf16[8,64,512]{2,1,0:T(8,128)(2,1)S(1)}) custom-call(s32[128]{0:T(128)S(1)} %select_reduce_fusion.inv_ref, bf16[16,8,64,128]{3,2,1,0:T(8,128)(2,1)} %all-to-all-done.1.arrived), custom_call_target="tpu_custom_call" | custom-call | bytes 2097152 | tf_op jit(solution)/shard_map/pallas_call | solution.py:220
  231.9 3.8 %collective-permute-start.17 = (bf16[8,64,512]{2,1,0:T(8,128)(2,1)}, bf16[8,64,512]{2,1,0:T(8,128)(2,1)S(1)}, u32[]{:S(2)}, u32[]{:S(2)}) collective-permute-start(bf16[8,64,512]{2,1,0:T(8,128)(2,1)} %get-tuple-element.16), channel_id=1, source_target_pairs={{0,256},{256,0},{1,257},{257,1},{2,258},{258,2},{3,259},{259,3},{4... | collective-permute-start | bytes 1572872 | tf_op jit(solution)/shard_map/ppermute | solution.py:226
  241.0 3.5 %collective-permute-start.16 = (bf16[8,64,512]{2,1,0:T(8,128)(2,1)}, bf16[8,64,512]{2,1,0:T(8,128)(2,1)S(1)}, u32[]{:S(2)}, u32[]{:S(2)}) collective-permute-start(bf16[8,64,512]{2,1,0:T(8,128)(2,1)} %get-tuple-element.15), channel_id=1, source_target_pairs={{0,256},{256,0},{1,257},{257,1},{2,258},{258,2},{3,259},{259,3},{4... | collective-permute-start | bytes 1572872 | tf_op jit(solution)/shard_map/ppermute | solution.py:225
  247.1 2.8 %collective-permute-done.17.got_b = bf16[8,64,512]{2,1,0:T(8,128)(2,1)S(1)} collective-permute-done((bf16[8,64,512]{2,1,0:T(8,128)(2,1)}, bf16[8,64,512]{2,1,0:T(8,128)(2,1)S(1)}, u32[]{:S(2)}, u32[]{:S(2)}) %collective-permute-start.17) | collective-permute-done | bytes 524320 | tf_op jit(solution)/shard_map/ppermute | solution.py:226
  249.9 11.1 %collective-permute-done.16.got_a = bf16[8,64,512]{2,1,0:T(8,128)(2,1)S(1)} collective-permute-done((bf16[8,64,512]{2,1,0:T(8,128)(2,1)}, bf16[8,64,512]{2,1,0:T(8,128)(2,1)S(1)}, u32[]{:S(2)}, u32[]{:S(2)}) %collective-permute-start.16) | collective-permute-done | bytes 524320 | tf_op jit(solution)/shard_map/ppermute | solution.py:225
  261.0 4.4 %shard_map.42 = f32[8,128,512]{2,1,0:T(8,128)} custom-call(bf16[8,64,512]{2,1,0:T(8,128)(2,1)S(1)} %get-tuple-element.12.kept_a, bf16[8,64,512]{2,1,0:T(8,128)(2,1)S(1)} %get-tuple-element.14.kept_b, bf16[8,64,512]{2,1,0:T(8,128)(2,1)S(1)} %collective-permute-done.16.got_a, bf16[8,64,512]{2,1,0:T(8,128)(2,1)S(1)} %collective-permute-done.17.got_b, ...), custom_call_target="tpu_custom_call" | custom-call | flops 536870912 | bytes 6291456 | tf_op jit(solution)/shard_map/pallas_call | solution.py:231
  (92 shorter events, 44.1 us)
Async XLA Ops:
  6.5 238.0 %copy-start = (bf16[512,512]{1,0:T(8,128)(2,1)S(1)}, bf16[512,512]{1,0:T(8,128)(2,1)}, u32[]{:S(2)}) copy-start(bf16[512,512]{1,0:T(8,128)(2,1)} %param.5) | copy-start | bytes 1572868
  6.5 35.3 %copy-start.10 = (s32[1,128]{1,0:T(1,128)S(1)}, s32[1,128]{1,0:T(1,128)}, u32[]{:S(2)}) copy-start(s32[1,128]{1,0:T(1,128)} %param.4) | copy-start | bytes 1540
  6.5 35.3 %copy-start.2 = (bf16[1,1024,1024]{2,1,0:T(8,128)(2,1)S(1)}, bf16[1,1024,1024]{2,1,0:T(8,128)(2,1)}, u32[]{:S(2)}) copy-start(bf16[1,1024,1024]{2,1,0:T(8,128)(2,1)} %param.3) | copy-start | bytes 6291460
  10.5 19.1 %all-to-all-start.2 = ((bf16[16,8,8,128]{3,2,1,0:T(8,128)(2,1)}), bf16[16,8,8,128]{3,2,1,0:T(8,128)(2,1)S(1)}, u32[]{:S(2)}, u32[]{:S(2)}) async-start(bf16[16,8,8,128]{3,2,1,0:T(8,128)(2,1)} %copy.11), calls=%async_computation.2 | async-start | bytes 524288 | tf_op jit(solution)/shard_map/all_to_all | solution.py:146
  31.4 19.2 %all-to-all-start.3 = ((bf16[16,4,8,128]{3,2,1,0:T(8,128)(2,1)}), bf16[16,4,8,128]{3,2,1,0:T(8,128)(2,1)S(1)}, u32[]{:S(2)}, u32[]{:S(2)}) async-start(bf16[16,4,8,128]{3,2,1,0:T(8,128)(2,1)} %gather_fusion.1), calls=%async_computation.3 | async-start | bytes 262144 | tf_op jit(solution)/shard_map/all_to_all | solution.py:151
  44.2 1.3 copy-start.3
  45.6 1.4 copy-start.4
  50.6 63.6 %all-to-all-start = ((bf16[16,8,64,128]{3,2,1,0:T(8,128)(2,1)}), bf16[16,8,64,128]{3,2,1,0:T(8,128)(2,1)S(1)}, u32[]{:S(2)}, u32[]{:S(2)}) async-start(bf16[16,8,64,128]{3,2,1,0:T(8,128)(2,1)} %copy-done.3), calls=%async_computation | async-start | bytes 4194304 | tf_op jit(solution)/shard_map/all_to_all | solution.py:199
  55.7 4.0 %copy-start.5 = (bf16[2,8,64,1024]{3,2,1,0:T(8,128)(2,1)S(1)}, bf16[2,8,64,1024]{3,2,1,0:T(8,128)(2,1)}, u32[]{:S(2)}) copy-start(bf16[2,8,64,1024]{3,2,1,0:T(8,128)(2,1)} %copy-done.4) | copy-start | bytes 6291460
  57.2 4.7 %collective-permute-start.8 = (bf16[8,64,1024]{2,1,0:T(8,128)(2,1)S(1)}, bf16[8,64,1024]{2,1,0:T(8,128)(2,1)S(1)}, u32[]{:S(2)}, u32[]{:S(2)}) collective-permute-start(bf16[8,64,1024]{2,1,0:T(8,128)(2,1)S(1)} %slice_bitcast_fusion.1), channel_id=1, source_target_pairs={{0,16},{16,0},{32,48},{48,32},{64,80},{80,64},{96,112},{112,96},{1... | collective-permute-start | bytes 3145736 | tf_op jit(solution)/shard_map/ppermute | solution.py:131
  62.0 20.9 %collective-permute-start.10 = (bf16[2,64,1024]{2,1,0:T(8,128)(2,1)S(1)}, bf16[2,64,1024]{2,1,0:T(8,128)(2,1)S(1)}, u32[]{:S(2)}, u32[]{:S(2)}) collective-permute-start(bf16[2,64,1024]{2,1,0:T(8,128)(2,1)S(1)} %pad_maximum_fusion.10), channel_id=1, source_target_pairs={{0,64},{16,208},{32,96},{48,240},{64,128},{80,16},{96,160},{112,48... | collective-permute-start | bytes 786440 | tf_op jit(solution)/shard_map/ppermute | solution.py:136
  64.6 21.0 %collective-permute-start.11 = (bf16[2,64,1024]{2,1,0:T(8,128)(2,1)S(1)}, bf16[2,64,1024]{2,1,0:T(8,128)(2,1)S(1)}, u32[]{:S(2)}, u32[]{:S(2)}) collective-permute-start(bf16[2,64,1024]{2,1,0:T(8,128)(2,1)S(1)} %pad_maximum_fusion.11), channel_id=1, source_target_pairs={{0,96},{16,176},{32,128},{48,208},{64,160},{80,240},{96,192},{112,... | collective-permute-start | bytes 786440 | tf_op jit(solution)/shard_map/ppermute | solution.py:136
  68.9 29.9 %collective-permute-start.12 = (bf16[2,64,1024]{2,1,0:T(8,128)(2,1)S(1)}, bf16[2,64,1024]{2,1,0:T(8,128)(2,1)S(1)}, u32[]{:S(2)}, u32[]{:S(2)}) collective-permute-start(bf16[2,64,1024]{2,1,0:T(8,128)(2,1)S(1)} %pad_maximum_fusion.12), channel_id=1, source_target_pairs={{0,128},{16,144},{32,160},{48,176},{64,192},{80,208},{96,224},{112... | collective-permute-start | bytes 786440 | tf_op jit(solution)/shard_map/ppermute | solution.py:136
  74.2 28.3 %collective-permute-start.13 = (bf16[2,64,1024]{2,1,0:T(8,128)(2,1)S(1)}, bf16[2,64,1024]{2,1,0:T(8,128)(2,1)S(1)}, u32[]{:S(2)}, u32[]{:S(2)}) collective-permute-start(bf16[2,64,1024]{2,1,0:T(8,128)(2,1)S(1)} %pad_maximum_fusion.13), channel_id=1, source_target_pairs={{0,160},{16,112},{32,192},{48,144},{64,224},{80,176},{96,0},{112,2... | collective-permute-start | bytes 786440 | tf_op jit(solution)/shard_map/ppermute | solution.py:136
  78.2 31.6 %collective-permute-start.14 = (bf16[2,64,1024]{2,1,0:T(8,128)(2,1)S(1)}, bf16[2,64,1024]{2,1,0:T(8,128)(2,1)S(1)}, u32[]{:S(2)}, u32[]{:S(2)}) collective-permute-start(bf16[2,64,1024]{2,1,0:T(8,128)(2,1)S(1)} %pad_maximum_fusion.14), channel_id=1, source_target_pairs={{0,192},{16,80},{32,224},{48,112},{64,0},{80,144},{96,32},{112,176... | collective-permute-start | bytes 786440 | tf_op jit(solution)/shard_map/ppermute | solution.py:136
  83.0 28.8 %collective-permute-start.15 = (bf16[2,64,1024]{2,1,0:T(8,128)(2,1)S(1)}, bf16[2,64,1024]{2,1,0:T(8,128)(2,1)S(1)}, u32[]{:S(2)}, u32[]{:S(2)}) collective-permute-start(bf16[2,64,1024]{2,1,0:T(8,128)(2,1)S(1)} %pad_maximum_fusion.15), channel_id=1, source_target_pairs={{0,224},{16,48},{32,0},{48,80},{64,32},{80,112},{96,64},{112,144},... | collective-permute-start | bytes 786440 | tf_op jit(solution)/shard_map/ppermute | solution.py:136
  85.6 26.2 %collective-permute-start.9 = (bf16[2,64,1024]{2,1,0:T(8,128)(2,1)S(1)}, bf16[2,64,1024]{2,1,0:T(8,128)(2,1)S(1)}, u32[]{:S(2)}, u32[]{:S(2)}) collective-permute-start(bf16[2,64,1024]{2,1,0:T(8,128)(2,1)S(1)} %pad_maximum_fusion.9), channel_id=1, source_target_pairs={{0,32},{16,240},{32,64},{48,16},{64,96},{80,48},{96,128},{112,80},... | collective-permute-start | bytes 786440 | tf_op jit(solution)/shard_map/ppermute | solution.py:136
  114.2 100.1 %all-to-all-start.1 = ((bf16[16,8,64,128]{3,2,1,0:T(8,128)(2,1)}), bf16[16,8,64,128]{3,2,1,0:T(8,128)(2,1)}, u32[]{:S(2)}, u32[]{:S(2)}) async-start(bf16[16,8,64,128]{3,2,1,0:T(8,128)(2,1)} %shard_map.40), calls=%async_computation.1 | async-start | bytes 4194304 | tf_op jit(solution)/shard_map/all_to_all | solution.py:214
  122.4 122.7 %all-gather.2.cloned.1.call-start = ((), (), s32[]{:S(2)}) async-start(), calls=%async_computation.4 | async-start | bytes 1114112 | tf_op jit(solution)/shard_map/all_gather | solution.py:159
  125.6 16.2 %collective-permute-start = (bf16[8,64,1024]{2,1,0:T(8,128)(2,1)S(1)}, bf16[8,64,1024]{2,1,0:T(8,128)(2,1)S(1)}, u32[]{:S(2)}, u32[]{:S(2)}) collective-permute-start(bf16[8,64,1024]{2,1,0:T(8,128)(2,1)S(1)} %slice_bitcast_fusion), channel_id=1, source_target_pairs={{0,16},{16,0},{32,48},{48,32},{64,80},{80,64},{96,112},{112,96},{1... | collective-permute-start | bytes 3145736 | tf_op jit(solution)/shard_map/ppermute | solution.py:131
  129.1 7.7 %collective-permute-start.18 = (bf16[64,512]{1,0:T(8,128)(2,1)S(1)}, bf16[64,512]{1,0:T(8,128)(2,1)S(1)}, u32[]{:S(2)}, u32[]{:S(2)}) collective-permute-start(bf16[64,512]{1,0:T(8,128)(2,1)S(1)} %bitcast.76), channel_id=1, source_target_pairs={{0,256},{256,0},{1,257},{257,1},{2,258},{258,2},{3,259},{259,3},{4... | collective-permute-start | bytes 196616 | tf_op jit(solution)/shard_map/ppermute | solution.py:154
  138.2 29.1 %collective-permute-start.19 = (bf16[32,512]{1,0:T(8,128)(2,1)S(1)}, bf16[32,512]{1,0:T(8,128)(2,1)S(1)}, u32[]{:S(2)}, u32[]{:S(2)}) collective-permute-start(bf16[32,512]{1,0:T(8,128)(2,1)S(1)} %constant_dynamic-slice_fusion.3), channel_id=1, source_target_pairs={{0,0},{1,16},{2,32},{3,48},{4,64},{5,80},{6,96},{7,112},{8,128},{9... | collective-permute-start | bytes 98312 | tf_op jit(solution)/shard_map/ppermute | solution.py:170
  141.9 41.3 %collective-permute-start.7 = (bf16[2,64,1024]{2,1,0:T(8,128)(2,1)S(1)}, bf16[2,64,1024]{2,1,0:T(8,128)(2,1)S(1)}, u32[]{:S(2)}, u32[]{:S(2)}) collective-permute-start(bf16[2,64,1024]{2,1,0:T(8,128)(2,1)S(1)} %pad_maximum_fusion.7), channel_id=1, source_target_pairs={{0,224},{16,48},{32,0},{48,80},{64,32},{80,112},{96,64},{112,144},... | collective-permute-start | bytes 786440 | tf_op jit(solution)/shard_map/ppermute | solution.py:136
  148.7 36.4 %collective-permute-start.6 = (bf16[2,64,1024]{2,1,0:T(8,128)(2,1)S(1)}, bf16[2,64,1024]{2,1,0:T(8,128)(2,1)S(1)}, u32[]{:S(2)}, u32[]{:S(2)}) collective-permute-start(bf16[2,64,1024]{2,1,0:T(8,128)(2,1)S(1)} %pad_maximum_fusion.6), channel_id=1, source_target_pairs={{0,192},{16,80},{32,224},{48,112},{64,0},{80,144},{96,32},{112,176... | collective-permute-start | bytes 786440 | tf_op jit(solution)/shard_map/ppermute | solution.py:136
  154.0 77.9 %collective-permute-start.5 = (bf16[2,64,1024]{2,1,0:T(8,128)(2,1)}, bf16[2,64,1024]{2,1,0:T(8,128)(2,1)S(1)}, u32[]{:S(2)}, u32[]{:S(2)}) collective-permute-start(bf16[2,64,1024]{2,1,0:T(8,128)(2,1)} %pad_maximum_fusion.5), channel_id=1, source_target_pairs={{0,160},{16,112},{32,192},{48,144},{64,224},{80,176},{96,0},{112,2... | collective-permute-start | bytes 786440 | tf_op jit(solution)/shard_map/ppermute | solution.py:136
  160.4 75.3 %collective-permute-start.4 = (bf16[2,64,1024]{2,1,0:T(8,128)(2,1)}, bf16[2,64,1024]{2,1,0:T(8,128)(2,1)S(1)}, u32[]{:S(2)}, u32[]{:S(2)}) collective-permute-start(bf16[2,64,1024]{2,1,0:T(8,128)(2,1)} %pad_maximum_fusion.4), channel_id=1, source_target_pairs={{0,128},{16,144},{32,160},{48,176},{64,192},{80,208},{96,224},{112... | collective-permute-start | bytes 786440 | tf_op jit(solution)/shard_map/ppermute | solution.py:136
  167.2 68.5 %collective-permute-start.3 = (bf16[2,64,1024]{2,1,0:T(8,128)(2,1)}, bf16[2,64,1024]{2,1,0:T(8,128)(2,1)S(1)}, u32[]{:S(2)}, u32[]{:S(2)}) collective-permute-start(bf16[2,64,1024]{2,1,0:T(8,128)(2,1)} %pad_maximum_fusion.3), channel_id=1, source_target_pairs={{0,96},{16,176},{32,128},{48,208},{64,160},{80,240},{96,192},{112,... | collective-permute-start | bytes 786440 | tf_op jit(solution)/shard_map/ppermute | solution.py:136
  183.2 53.3 %collective-permute-start.2 = (bf16[2,64,1024]{2,1,0:T(8,128)(2,1)}, bf16[2,64,1024]{2,1,0:T(8,128)(2,1)S(1)}, u32[]{:S(2)}, u32[]{:S(2)}) collective-permute-start(bf16[2,64,1024]{2,1,0:T(8,128)(2,1)} %pad_maximum_fusion.2), channel_id=1, source_target_pairs={{0,64},{16,208},{32,96},{48,240},{64,128},{80,16},{96,160},{112,48... | collective-permute-start | bytes 786440 | tf_op jit(solution)/shard_map/ppermute | solution.py:136
  185.1 52.1 %collective-permute-start.1 = (bf16[2,64,1024]{2,1,0:T(8,128)(2,1)}, bf16[2,64,1024]{2,1,0:T(8,128)(2,1)}, u32[]{:S(2)}, u32[]{:S(2)}) collective-permute-start(bf16[2,64,1024]{2,1,0:T(8,128)(2,1)} %pad_maximum_fusion.1), channel_id=1, source_target_pairs={{0,32},{16,240},{32,64},{48,16},{64,96},{80,48},{96,128},{112,80},... | collective-permute-start | bytes 786440 | tf_op jit(solution)/shard_map/ppermute | solution.py:136
  214.3 30.2 %copy-start.11 = (bf16[4,16,8,512]{3,2,1,0:T(8,128)(2,1)S(1)}, bf16[4,16,8,512]{3,2,1,0:T(8,128)(2,1)}, u32[]{:S(2)}) copy-start(bf16[4,16,8,512]{3,2,1,0:T(8,128)(2,1)} %copy.13) | copy-start | bytes 1572868
  231.9 17.9 %collective-permute-start.17 = (bf16[8,64,512]{2,1,0:T(8,128)(2,1)}, bf16[8,64,512]{2,1,0:T(8,128)(2,1)S(1)}, u32[]{:S(2)}, u32[]{:S(2)}) collective-permute-start(bf16[8,64,512]{2,1,0:T(8,128)(2,1)} %get-tuple-element.16), channel_id=1, source_target_pairs={{0,256},{256,0},{1,257},{257,1},{2,258},{258,2},{3,259},{259,3},{4... | collective-permute-start | bytes 1572872 | tf_op jit(solution)/shard_map/ppermute | solution.py:226
  241.0 20.0 %collective-permute-start.16 = (bf16[8,64,512]{2,1,0:T(8,128)(2,1)}, bf16[8,64,512]{2,1,0:T(8,128)(2,1)S(1)}, u32[]{:S(2)}, u32[]{:S(2)}) collective-permute-start(bf16[8,64,512]{2,1,0:T(8,128)(2,1)} %get-tuple-element.15), channel_id=1, source_target_pairs={{0,256},{256,0},{1,257},{257,1},{2,258},{258,2},{3,259},{259,3},{4... | collective-permute-start | bytes 1572872 | tf_op jit(solution)/shard_map/ppermute | solution.py:225
  (5 other events, 4.6 us)
Sparse Core Ops, SparseCore 0:
  137.5 82.0 all-gather.1

commit v2 on v1

v2 whole, which is shorter than its diff:
```python
import jax
import jax.numpy as jnp
from jax import lax
from jax.experimental import pallas as pl
from jax.experimental.pallas import tpu as pltpu
from jax.sharding import PartitionSpec as P

B = 128
HA = 64
HB = B - HA
W = 8
G = 16
PANEL = 512
TAIL = 16
SMEM = pl.BlockSpec(memory_space=pltpu.SMEM)
ANY = pl.BlockSpec(memory_space=pl.ANY)
VMEM = pl.BlockSpec(memory_space=pltpu.VMEM)
VMEM_LIMIT = 40 * 1024 * 1024


def params(flops=0, moved=0):
    return dict(
        compiler_params=pltpu.CompilerParams(vmem_limit_bytes=VMEM_LIMIT),
        cost_estimate=pl.CostEstimate(flops=flops, bytes_accessed=moved, transcendentals=0),
    )


def bf16(*shape):
    return jax.ShapeDtypeStruct(shape, jnp.bfloat16)


def ring(core, distance):
    return lax.bitwise_and(jnp.where(core == 0, distance, -distance), 7)


def row_slot(map_ref, q):
    row = lax.axis_index("row")
    target = map_ref[row * W + q] // W
    core = target % 2
    return lax.bitwise_xor(core, row % 2), ring(core, target // 2 - row // 2)


def row_landing(inv_ref, i):
    row = lax.axis_index("row")
    source = inv_ref[row * W + i] // W
    return lax.bitwise_xor(source % 2, row % 2), ring(row % 2, row // 2 - source // 2)


def col_slot(map_ref, v):
    return (map_ref[lax.axis_index("col") * W + v] // (W // 2)) % G


def col_landing(inv_ref, half, j):
    return inv_ref[(half * G + lax.axis_index("col")) * (W // 2) + j] // W


def lanes(j):
    return pl.ds(pl.multiple_of(j * B, B), B)


def pack(map_ref, tile, column, a, own, swap, sem_a, sem_b, sem_c):
    for v in range(W):
        pltpu.make_async_copy(
            tile.at[:, pl.ds(0, HA), pl.ds(v * B, B)], a.at[col_slot(map_ref, v), pl.ds(0, W)], sem_a
        ).start()
    sixteenths = pltpu.make_async_copy(column, a.at[:, W], sem_c)
    sixteenths.start()
    for q in range(W):
        e, k = row_slot(map_ref, q)
        for side, ob in enumerate((own, swap)):
            @pl.when(e == side)
            def _():
                pltpu.make_async_copy(tile.at[q, pl.ds(HA, HB), :], ob.at[k], sem_b).start()
    done = a.at[pl.ds(0, W), pl.ds(0, W)]
    pltpu.make_async_copy(done, done, sem_a).wait()
    pltpu.make_async_copy(own, own, sem_b).wait()
    sixteenths.wait()


def cols_to_rows(map_ref, map2_ref, inv_ref, arrived, taken, tail, own, swap, sem, sem_t):
    sib = lax.axis_index("sib")

    @pl.loop(0, W)
    def _(q):
        e, k = row_slot(map_ref, q)
        e2, k2 = row_slot(map2_ref, q)
        for side, ob in enumerate((own, swap)):
            @pl.when(e == side)
            def _():
                for j in range(W // 2):
                    pltpu.make_async_copy(
                        arrived.at[col_landing(inv_ref, sib, j), q],
                        ob.at[k, pl.ds(0, HA), pl.ds(j * B, B)], sem
                    ).start()

            @pl.when(e2 == side)
            def _():
                pltpu.make_async_copy(taken.at[q], ob.at[k2, pl.ds(0, HA), pl.ds(PANEL, PANEL)], sem).start()
            pltpu.make_async_copy(tail, ob.at[q, pl.ds(HA, TAIL), :], sem_t).start()
    done = own.at[:, pl.ds(0, HA), :]
    pltpu.make_async_copy(done, done, sem).wait()
    for ob in (own, swap):
        done = ob.at[:, pl.ds(HA, TAIL), :]
        pltpu.make_async_copy(done, done, sem_t).wait()


def rows_to_cols(map_ref, inv_ref, piece, *refs):
    arrived, a, sem, sem_p = refs[:8], refs[8], refs[9], refs[10]

    @pl.loop(0, W)
    def _(i):
        e, k = row_landing(inv_ref, i)
        for step in range(8):
            @pl.when(k == step)
            def _():
                for v in range(W):
                    pltpu.make_async_copy(
                        arrived[step].at[e, :, pl.ds(v * B, B)], a.at[col_slot(map_ref, v), i], sem
                    ).start()
    for t in range(G):
        pltpu.make_async_copy(piece, a.at[t, pl.ds(W, 4)], sem_p).start()
    done = a.at[pl.ds(0, W), pl.ds(0, W)]
    pltpu.make_async_copy(done, done, sem).wait()
    done = a.at[:, pl.ds(W, 4)]
    pltpu.make_async_copy(done, done, sem_p).wait()


def hand_cols(inv_ref, arrived, hand, sem):
    sib = lax.axis_index("sib")
    for j in range(W // 2):
        pltpu.make_async_copy(
            arrived.at[col_landing(inv_ref, 1 - sib, j), pl.ds(0, W)], hand.at[:, :, pl.ds(j * B, B)], sem
        ).start()
    pltpu.make_async_copy(hand, hand, sem).wait()


DIMS = (((1,), (1,)), ((), ()))


def factor_of(arrived, inverse, out, parts, panel, sem):
    copy = pltpu.make_async_copy(arrived.at[:, pl.ds(W, 4)], parts, sem)
    copy.start()
    copy.wait()
    for c in range(G):
        for j in range(4):
            part = parts[c, j].astype(jnp.float32)
            panel[:, c * 8:c * 8 + 8, j * B:j * B + B] = part.reshape(W, 8, B)

    @pl.loop(0, W)
    def _(p):
        out[pl.ds(pl.multiple_of(p * B, B), B), :] = lax.dot_general(
            panel[p].astype(jnp.bfloat16), inverse[...], DIMS, preferred_element_type=jnp.float32
        ).astype(jnp.bfloat16)


def keep(inv_ref, inv2_ref, *refs):
    arrived_a, refs = refs[:8], refs[8:]
    arrived_b, rows, inverse, base, kept_a, kept_b, pieces, panel, sem_a, sem_b, sem_p = refs
    sib, row = lax.axis_index("sib"), lax.axis_index("row")

    for step in range(8):
        z = lax.bitwise_and(row // 2 - jnp.where(row % 2 == 0, step, -step), 7)
        for e in range(2):
            origin = z * 2 + lax.bitwise_xor(row % 2, e)
            for h in range(2):
                pltpu.make_async_copy(
                    arrived_a[step].at[e, pl.ds(HA, TAIL), pl.ds(h * PANEL, PANEL)], pieces.at[origin, h], sem_p
                ).start()

    @pl.loop(0, W)
    def _(i):
        for child, ref in enumerate((inv_ref, inv2_ref)):
            e, k = row_landing(ref, i)
            for step in range(8):
                @pl.when(k == step)
                def _():
                    pltpu.make_async_copy(
                        arrived_a[step].at[e, pl.ds(0, HA), pl.ds(child * PANEL, PANEL)], kept_a.at[child, i], sem_a
                    ).start()
    for j in range(W // 2):
        pltpu.make_async_copy(
            arrived_b.at[col_landing(inv_ref, sib, j), pl.ds(0, W)], kept_b.at[:, :, pl.ds(j * B, B)], sem_b
        ).start()
    pltpu.make_async_copy(pieces, pieces, sem_p).wait()
    f32 = jnp.float32
    for p in range(W // 2):
        for r in range(G):
            low = (p % 2) * 8
            panel[p * B + r * 8:p * B + r * 8 + 8, :] = pieces[r, p // 2].astype(f32)[low:low + 8]
    cols = lax.dot_general(panel[...].astype(jnp.bfloat16), inverse[...], DIMS, preferred_element_type=f32)
    panel[...] = cols.astype(jnp.bfloat16).astype(f32)
    pltpu.make_async_copy(kept_a, kept_a, sem_a).wait()
    pltpu.make_async_copy(kept_b, kept_b, sem_b).wait()

    @pl.loop(0, W)
    def _(i):
        block = rows[pl.ds(pl.multiple_of(i * B, B), B), :]
        product = lax.dot_general(block, panel[...].astype(jnp.bfloat16), DIMS, preferred_element_type=f32)
        base[i, 0:HA] = kept_a[0, i].astype(f32) + kept_a[1, i].astype(f32) - product[0:HA]
        base[i, HA:B] = kept_b[i].astype(f32) - product[HA:B]


def join(base, got_b, out):
    out[:, 0:HA] = base[:, 0:HA]
    out[:, HA:B] = base[:, HA:B] + got_b[...].astype(jnp.float32)


def core_exchange(swap):
    return lax.ppermute(swap, "row", [(i, i ^ 1) for i in range(G)])


def pairs_of(own, other):
    return [jnp.stack([own[k], other[k]]) for k in range(8)]


def z_ring(both):
    arrived = [both[0]] + [None] * 7
    for k in (4, 3, 5, 2, 6, 1, 7):
        pairs = [(z * 2 + c, (z + (k if c == 0 else -k)) % 8 * 2 + c) for z in range(8) for c in range(2)]
        arrived[k] = lax.ppermute(both[k], "row", pairs)
    return arrived


def inverse_of(maps):
    blocks = jnp.arange(maps.shape[0], dtype=jnp.int32)
    return jnp.sum(jnp.where(maps[None, :] == blocks[:, None], blocks[None, :], 0), axis=1)


def panel_column(tile, maps):
    mine = lax.dynamic_slice_in_dim(maps, lax.axis_index("col") * W, W, 0)
    owned = jnp.sum(jnp.where(mine < 4, jnp.arange(W, dtype=jnp.int32), 0))
    column = lax.dynamic_slice(tile, (0, owned * B), (W * B, B))
    return jnp.transpose(column.reshape(W, G, 8, B), (1, 0, 2, 3)).reshape(G, W * 8, B)


def panel_piece(got, maps, inv, inv2, early):
    sib, row = lax.axis_index("sib"), lax.axis_index("row")
    got = jnp.transpose(jnp.take(got, inv[:4] // W, axis=0, mode="clip"), (1, 0, 2, 3))
    targets = lax.dynamic_slice_in_dim(maps, row * W, W, 0) // W
    match = targets[None, :] == (jnp.arange(2 * G, dtype=jnp.int32) % G)[:, None]
    source = jnp.sum(jnp.where(match, jnp.arange(W, dtype=jnp.int32)[None, :], 0), axis=1)
    got = lax.all_to_all(jnp.take(got, source, axis=0, mode="clip"), ("sib", "row"), 0, 0, tiled=True)
    got, early = lax.optimization_barrier((got, early))
    parts = [
        jnp.take(got, child * G + lax.dynamic_slice_in_dim(ref, row * W, W, 0) // W, axis=0, mode="clip").astype(jnp.float32)
        for child, ref in ((sib, inv), (1 - sib, inv2))
    ]
    return (parts[0] + parts[1]).astype(jnp.bfloat16), early


def tail_piece(piece):
    sib, row = lax.axis_index("sib"), lax.axis_index("row")
    half = jnp.where(sib == row // 8, 0, 1)
    send = lax.dynamic_slice_in_dim(jnp.transpose(piece, (0, 2, 1, 3)).reshape(W * 8, PANEL), half * (W * 4), W * 4, 0)
    pairs = []
    for s in range(2):
        for g in range(G):
            for c in range(G):
                x = 0 if s == g // 8 else 1
                pairs.append((s * 256 + g * G + c, (g // 8) * 256 + c * G + (g % 8) * 2 + x))
    got = lax.ppermute(send, ("sib", "row", "col"), pairs)
    return jnp.concatenate([got[:16], got[16:]], axis=1)


def shards(children, block_map, inverse_factor):
    tile = children[0]
    maps = block_map[0]
    dma = pltpu.SemaphoreType.DMA
    MiB = 1 << 20
    exchange = [(0, 1), (1, 0)]
    maps2 = lax.ppermute(maps, "sib", exchange)
    inv = inverse_of(maps)
    blocks = tile.reshape(W, B, W * B)

    rows_a, rows_b = bf16(8, HA + TAIL, W * B), bf16(8, HB, W * B)
    send_a, own, swap = pl.pallas_call(
        pack, out_shape=(bf16(G, W + 1, HA, B), rows_b, rows_b), in_specs=[SMEM, ANY, ANY], out_specs=(ANY, ANY, ANY),
        scratch_shapes=[dma, dma, dma], **params(moved=4 * MiB),
    )(maps, blocks, panel_column(tile, maps))
    got_a = lax.all_to_all(send_a, "col", 0, 0, tiled=True)
    got_b = z_ring(pairs_of(own, core_exchange(swap)))
    got_a, maps2, got_b[7], got_b[6], got_b[5], got_b[4], got_b[3] = lax.optimization_barrier(
        (got_a, maps2, got_b[7], got_b[6], got_b[5], got_b[4], got_b[3]))

    inv2 = inverse_of(maps2)
    hand_a = pl.pallas_call(
        hand_cols, out_shape=bf16(W, HA, PANEL), in_specs=[SMEM, ANY], out_specs=VMEM, scratch_shapes=[dma],
        **params(moved=MiB),
    )(inv, got_a)
    taken_a = lax.ppermute(hand_a, "sib", exchange)
    piece, taken_a = panel_piece(got_a[:, W].reshape(G, W, 8, B), maps, inv, inv2, taken_a)
    tail = tail_piece(piece)
    send_b = pl.pallas_call(
        rows_to_cols, out_shape=bf16(G, W + 4, HB, B), in_specs=[SMEM, SMEM] + [ANY] * 9, out_specs=ANY,
        scratch_shapes=[dma, dma], **params(moved=3 * MiB),
    )(maps, inv, jnp.transpose(piece, (1, 0, 2, 3)).reshape(4, W * 8, B), *got_b)
    send_b, tail = lax.optimization_barrier((send_b, tail))
    got_b = lax.all_to_all(send_b, "col", 0, 0, tiled=True)
    own, swap = pl.pallas_call(
        cols_to_rows, out_shape=(rows_a, rows_a), in_specs=[SMEM] * 3 + [ANY] * 3, out_specs=(ANY, ANY),
        scratch_shapes=[dma, dma], **params(moved=2 * MiB),
    )(maps, maps2, inv, got_a, taken_a, tail)
    got_a = z_ring(pairs_of(own, core_exchange(swap)))
    got_b, got_a = lax.optimization_barrier((got_b, got_a))

    hand_b = pl.pallas_call(
        hand_cols, out_shape=bf16(W, HB, PANEL), in_specs=[SMEM, ANY], out_specs=VMEM, scratch_shapes=[dma],
        **params(moved=MiB),
    )(inv, got_b)
    taken_b = lax.ppermute(hand_b, "sib", exchange)
    factor_rows = pl.pallas_call(
        factor_of, out_shape=bf16(W * B, PANEL), in_specs=[ANY, VMEM], out_specs=VMEM,
        scratch_shapes=[pltpu.VMEM((G, 4, W * 8, B), jnp.bfloat16), pltpu.VMEM((W, B, PANEL), jnp.float32), dma],
        **params(flops=2 * W * B * PANEL * PANEL, moved=2 * MiB),
    )(got_b, inverse_factor)
    full = jax.ShapeDtypeStruct((W, B, PANEL), jnp.float32)
    base = pl.pallas_call(
        keep, out_shape=full, in_specs=[SMEM] * 2 + [ANY] * 9 + [VMEM] * 2, out_specs=VMEM,
        scratch_shapes=[pltpu.VMEM((2, W, HA, PANEL), jnp.bfloat16), pltpu.VMEM((W, HB, PANEL), jnp.bfloat16),
                        pltpu.VMEM((G, 2, 16, PANEL), jnp.bfloat16), pltpu.VMEM((PANEL, PANEL), jnp.float32), dma, dma, dma],
        **params(flops=3 * W * B * PANEL * PANEL, moved=6 * MiB),
    )(inv, inv2, *got_a, got_b, factor_rows, inverse_factor)
    full_spec = pl.BlockSpec((2, B, PANEL), lambda i: (i, 0, 0))
    out = pl.pallas_call(
        join, grid=(W // 2,), out_shape=full, in_specs=[full_spec, pl.BlockSpec((2, HB, PANEL), lambda i: (i, 0, 0))],
        out_specs=full_spec, **params(moved=5 * MiB),
    )(base, taken_b)
    return out.reshape(W * B, PANEL)


def solution(mesh):
    in_specs = (P("sib", "row", "col"), P("sib", None), P())
    out_specs = P("row", ("sib", "col"))
    return jax.shard_map(shards, mesh=mesh, in_specs=in_specs, out_specs=out_specs, check_vma=False)
```

time: 275 us -> 228 us (0.83)
  blocking collectives: 25.9 us -> 0 us
  starting transfers between devices: 128 us -> 104 us
  waiting for transfers between devices: 47 us -> 66.7 us
  between operations: 14.6 us -> 1.4 us
  Pallas kernels: 30.2 us -> 19.5 us
  local copies, waits for them, and re-layouts: 17.5 us -> 25.1 us
    ppermute x20, waiting for transfers between devices: 34.3 us -> 65.5 us  [the longest x14 52.9 us: z_ring(): arrived[k] = lax.ppermute(both[k], 'row', pairs)]
    all_gather x1 -> x0, blocking collectives: 25.9 us -> none  [panel_parts(): cols = lax.all_gather(got, 'row', axis=0, tiled=True)]
    ppermute x20, starting transfers between devices: 95.6 us -> 75 us  [the longest x14 57.3 us: z_ring(): arrived[k] = lax.ppermute(both[k], 'row', pairs)]
    all_to_all x2 -> x1, waiting for transfers between devices: 12.6 us -> 1.17 us  [panel_piece(): lax.all_to_all(jnp.take(got, source, axis=0, mode='clip'), ('sib', 'row')...]
    pallas_call x6 -> x8, Pallas kernels: 30.2 us -> 19.5 us  [the longest x1 5.33 us: shards(): pl.pallas_call(keep, out_shape=full, in_specs=[SMEM] * 2 + [ANY] * 9 + [V...]
    all_to_all x2 -> x1, starting transfers between devices: 19 us -> 10.1 us  [panel_piece(): lax.all_to_all(jnp.take(got, source, axis=0, mode='clip'), ('sib', 'row')...]
    unnamed x24 -> x68, local copies, waits for them, and re-layouts: 7.29 us -> 14.1 us
    another operation x16, other arithmetic: 3.96 us -> 7.67 us  [pairs_of(): return [jnp.stack([own[k], other[k]]) for k in range(8)]]
  transfers between devices with their start and end apart: 25 -> 23, of which waited for: 10 -> 13; matrix products, arithmetic and copies ran while one was open for 5% -> 8% of each run, Pallas kernels for 10% -> 6%
where the time goes in v2:
time: 228 us; the launch traced here: 226 us
  starting transfers between devices  104 us (46%)
  waiting for transfers between devices  66.7 us (29%)
  local copies, waits for them, and re-layouts  25.1 us (11%)
  Pallas kernels  19.5 us (9%)
  other arithmetic  9.65 us (4%)
    ppermute x14, starting transfers between devices, z_ring(): arrived[k] = lax.ppermute(both[k], 'row', pairs)  57.3 us
    ppermute x14, waiting for transfers between devices, z_ring(): arrived[k] = lax.ppermute(both[k], 'row', pairs)  52.9 us
    unnamed x68, local copies, waits for them, and re-layouts  14.1 us
    all_to_all x1, starting transfers between devices, shards(): got_b = lax.all_to_all(send_b, 'col', 0, 0, tiled=True)  10.3 us
    all_to_all x1, starting transfers between devices, panel_piece(): lax.all_to_all(jnp.take(got, source, axis=0, mode='clip'), ('sib', 'row')...  10.1 us
    all_to_all x1, starting transfers between devices, shards(): got_a = lax.all_to_all(send_a, 'col', 0, 0, tiled=True)  8.71 us
    another operation x16, other arithmetic, pairs_of(): return [jnp.stack([own[k], other[k]]) for k in range(8)]  7.67 us
    ppermute x1, waiting for transfers between devices, shards(): taken_b = lax.ppermute(hand_b, 'sib', exchange)  7.05 us
  transfers between devices with their start and end apart: 23, of which 13 were waited for; matrix products, arithmetic and copies ran while one was open for 8% of the time, Pallas kernels for 6%

profile of v2, /device:TPU:6, one launch (start us, length us, event | category | flops | bytes accessed | tf_op | source)
XLA Modules:
  0.0 226.4 jit_solution(11873883499612516184)
XLA Ops:
  5.3 2.4 %shard_map.37 = (bf16[16,9,64,128]{3,2,1,0:T(8,128)(2,1)S(1)}, bf16[8,64,1024]{2,1,0:T(8,128)(2,1)S(1)}, bf16[8,64,1024]{2,1,0:T(8,128)(2,1)S(1)}) custom-call(s32[128]{0:T(128)S(1)} %bitcast.30, bf16[8,128,1024]{2,1,0:T(8,128)(2,1)S(1)} %bitcast.27, bf16[16,64,128]{2,1,0:T(8,128)(2,1)S(1)} %bitcast.28), custom_call_target="tpu_custom_call" | custom-call | bytes 4194304 | tf_op jit(solution)/shard_map/pallas_call | solution.py:276
  10.1 8.7 %all-to-all-start = ((bf16[16,9,64,128]{3,2,1,0:T(8,128)(2,1)}), bf16[16,9,64,128]{3,2,1,0:T(8,128)(2,1)S(1)}, u32[]{:S(2)}, u32[]{:S(2)}) async-start(bf16[16,9,64,128]{3,2,1,0:T(8,128)(2,1)} %copy-done.4), calls=%async_computation | async-start | bytes 4718592 | tf_op jit(solution)/shard_map/all_to_all | solution.py:280
  20.7 4.2 %collective-permute-start = (s32[128]{0:T(128)S(1)}, s32[128]{0:T(128)S(1)}, u32[]{:S(2)}, u32[]{:S(2)}) collective-permute-start(s32[128]{0:T(128)S(1)} %bitcast.31), channel_id=1, source_target_pairs={{0,256},{256,0},{1,257},{257,1},{2,258},{258,2},{3,259},{259,3},{4... | collective-permute-start | bytes 1544 | tf_op jit(solution)/shard_map/ppermute | solution.py:271
  28.8 7.0 %collective-permute-start.6 = (bf16[2,64,1024]{2,1,0:T(8,128)(2,1)}, bf16[2,64,1024]{2,1,0:T(8,128)(2,1)S(1)}, u32[]{:S(2)}, u32[]{:S(2)}) collective-permute-start(bf16[2,64,1024]{2,1,0:T(8,128)(2,1)} %pad_maximum_fusion.12), channel_id=1, source_target_pairs={{0,96},{16,176},{32,128},{48,208},{64,160},{80,240},{96,192},{112,... | collective-permute-start | bytes 786440 | tf_op jit(solution)/shard_map/ppermute | solution.py:220
  36.6 8.2 %collective-permute-start.5 = (bf16[2,64,1024]{2,1,0:T(8,128)(2,1)}, bf16[2,64,1024]{2,1,0:T(8,128)(2,1)S(1)}, u32[]{:S(2)}, u32[]{:S(2)}) collective-permute-start(bf16[2,64,1024]{2,1,0:T(8,128)(2,1)} %pad_maximum_fusion.11), channel_id=1, source_target_pairs={{0,128},{16,144},{32,160},{48,176},{64,192},{80,208},{96,224},{112... | collective-permute-start | bytes 786440 | tf_op jit(solution)/shard_map/ppermute | solution.py:220
  45.6 3.6 %collective-permute-start.4 = (bf16[2,64,1024]{2,1,0:T(8,128)(2,1)}, bf16[2,64,1024]{2,1,0:T(8,128)(2,1)S(1)}, u32[]{:S(2)}, u32[]{:S(2)}) collective-permute-start(bf16[2,64,1024]{2,1,0:T(8,128)(2,1)} %pad_maximum_fusion.10), channel_id=1, source_target_pairs={{0,160},{16,112},{32,192},{48,144},{64,224},{80,176},{96,0},{112,2... | collective-permute-start | bytes 786440 | tf_op jit(solution)/shard_map/ppermute | solution.py:220
  50.0 2.8 %collective-permute-start.3 = (bf16[2,64,1024]{2,1,0:T(8,128)(2,1)}, bf16[2,64,1024]{2,1,0:T(8,128)(2,1)S(1)}, u32[]{:S(2)}, u32[]{:S(2)}) collective-permute-start(bf16[2,64,1024]{2,1,0:T(8,128)(2,1)} %pad_maximum_fusion.9), channel_id=1, source_target_pairs={{0,192},{16,80},{32,224},{48,112},{64,0},{80,144},{96,32},{112,176... | collective-permute-start | bytes 786440 | tf_op jit(solution)/shard_map/ppermute | solution.py:220
  53.6 2.5 %collective-permute-start.2 = (bf16[2,64,1024]{2,1,0:T(8,128)(2,1)}, bf16[2,64,1024]{2,1,0:T(8,128)(2,1)}, u32[]{:S(2)}, u32[]{:S(2)}) collective-permute-start(bf16[2,64,1024]{2,1,0:T(8,128)(2,1)} %pad_maximum_fusion.8), channel_id=1, source_target_pairs={{0,224},{16,48},{32,0},{48,80},{64,32},{80,112},{96,64},{112,144},... | collective-permute-start | bytes 786440 | tf_op jit(solution)/shard_map/ppermute | solution.py:220
  57.2 13.3 %collective-permute-done.4.refs_5_ = bf16[2,64,1024]{2,1,0:T(8,128)(2,1)S(1)} collective-permute-done((bf16[2,64,1024]{2,1,0:T(8,128)(2,1)}, bf16[2,64,1024]{2,1,0:T(8,128)(2,1)S(1)}, u32[]{:S(2)}, u32[]{:S(2)}) %collective-permute-start.4) | collective-permute-done | bytes 262176 | tf_op jit(solution)/shard_map/ppermute | solution.py:220
  71.2 2.1 collective-permute-done.3.refs_6_
  74.0 2.1 collective-permute-done.2.refs_7_
  77.6 4.0 %collective-permute-start.7 = (bf16[8,64,512]{2,1,0:T(8,128)(2,1)S(1)}, bf16[8,64,512]{2,1,0:T(8,128)(2,1)S(1)}, u32[]{:S(2)}, u32[]{:S(2)}) collective-permute-start(bf16[8,64,512]{2,1,0:T(8,128)(2,1)S(1)} %shard_map.38), channel_id=1, source_target_pairs={{0,256},{256,0},{1,257},{257,1},{2,258},{258,2},{3,259},{259,3},{4... | collective-permute-start | bytes 1572872 | tf_op jit(solution)/shard_map/ppermute | solution.py:290
  84.5 10.1 %all-to-all-start.1 = ((bf16[32,4,8,128]{3,2,1,0:T(8,128)(2,1)}), bf16[32,4,8,128]{3,2,1,0:T(8,128)(2,1)}, u32[]{:S(2)}, u32[]{:S(2)}) async-start(bf16[32,4,8,128]{3,2,1,0:T(8,128)(2,1)} %gather_fusion.1), calls=%async_computation.1 | async-start | bytes 524288 | tf_op jit(solution)/shard_map/all_to_all | solution.py:242
  95.7 4.3 %collective-permute-start.9 = (bf16[2,64,1024]{2,1,0:T(8,128)(2,1)S(1)}, bf16[2,64,1024]{2,1,0:T(8,128)(2,1)S(1)}, u32[]{:S(2)}, u32[]{:S(2)}) collective-permute-start(bf16[2,64,1024]{2,1,0:T(8,128)(2,1)S(1)} %pad_maximum_fusion.15), channel_id=1, source_target_pairs={{0,64},{16,208},{32,96},{48,240},{64,128},{80,16},{96,160},{112,48... | collective-permute-start | bytes 786440 | tf_op jit(solution)/shard_map/ppermute | solution.py:220
  101.7 3.4 %collective-permute-start.8 = (bf16[2,64,1024]{2,1,0:T(8,128)(2,1)}, bf16[2,64,1024]{2,1,0:T(8,128)(2,1)S(1)}, u32[]{:S(2)}, u32[]{:S(2)}) collective-permute-start(bf16[2,64,1024]{2,1,0:T(8,128)(2,1)} %pad_maximum_fusion.14), channel_id=1, source_target_pairs={{0,32},{16,240},{32,64},{48,16},{64,96},{80,48},{96,128},{112,80},... | collective-permute-start | bytes 786440 | tf_op jit(solution)/shard_map/ppermute | solution.py:220
  109.7 3.6 %collective-permute-start.10 = (bf16[32,512]{1,0:T(8,128)(2,1)S(1)}, bf16[32,512]{1,0:T(8,128)(2,1)S(1)}, u32[]{:S(2)}, u32[]{:S(2)}) collective-permute-start(bf16[32,512]{1,0:T(8,128)(2,1)S(1)} %constant_dynamic-slice_fusion.3), channel_id=1, source_target_pairs={{0,0},{1,16},{2,32},{3,48},{4,64},{5,80},{6,96},{7,112},{8,128},{9... | collective-permute-start | bytes 98312 | tf_op jit(solution)/shard_map/ppermute | solution.py:261
  114.4 3.6 %shard_map.39 = bf16[16,12,64,128]{3,2,1,0:T(8,128)(2,1)S(1)} custom-call(s32[128]{0:T(128)S(1)} %bitcast.33, s32[128]{0:T(128)S(1)} %select_reduce_fusion.1.inv_ref, bf16[4,64,128]{2,1,0:T(8,128)(2,1)S(1)} %bitcast.29, bf16[2,64,1024]{2,1,0:T(8,128)(2,1)S(1)} %pad_maximum_fusion.13.refs_0_, bf16[2,64,1024]{2,1,0:T(8,128)(2,1)S(1)} %collective-permute-done.8.refs_1_, ...), custom_call_target="tpu_custom_call" | custom-call | bytes 3145728 | tf_op jit(solution)/shard_map/pallas_call | solution.py:293
  119.6 2.6 %collective-permute-done.10 = bf16[32,512]{1,0:T(8,128)(2,1)S(1)} collective-permute-done((bf16[32,512]{1,0:T(8,128)(2,1)S(1)}, bf16[32,512]{1,0:T(8,128)(2,1)S(1)}, u32[]{:S(2)}, u32[]{:S(2)}) %collective-permute-start.10) | collective-permute-done | bytes 32800 | tf_op jit(solution)/shard_map/ppermute | solution.py:261
  122.3 10.3 %all-to-all-start.2 = ((bf16[16,12,64,128]{3,2,1,0:T(8,128)(2,1)}), bf16[16,12,64,128]{3,2,1,0:T(8,128)(2,1)S(1)}, u32[]{:S(2)}, u32[]{:S(2)}) async-start(bf16[16,12,64,128]{3,2,1,0:T(8,128)(2,1)} %copy-done.2), calls=%async_computation.2 | async-start | bytes 6291456 | tf_op jit(solution)/shard_map/all_to_all | solution.py:298
  135.3 2.3 %shard_map.40 = (bf16[8,80,1024]{2,1,0:T(8,128)(2,1)S(1)}, bf16[8,80,1024]{2,1,0:T(8,128)(2,1)S(1)}) custom-call(s32[128]{0:T(128)S(1)} %bitcast.34, s32[128]{0:T(128)S(1)} %collective-permute-done.map2_ref, s32[128]{0:T(128)S(1)} %select_reduce_fusion.1.inv_ref, bf16[16,9,64,128]{3,2,1,0:T(8,128)(2,1)S(1)} %copy-done.1, bf16[8,64,512]{2,1,0:T(8,128)(2,1)S(1)} %copy-done.7, ...), custom_call_target="tpu_custom_call" | custom-call | bytes 2097152 | tf_op jit(solution)/shard_map/pallas_call | solution.py:299
  139.7 2.9 %collective-permute-done.11 = bf16[8,80,1024]{2,1,0:T(8,128)(2,1)S(1)} collective-permute-done((bf16[8,80,1024]{2,1,0:T(8,128)(2,1)S(1)}, bf16[8,80,1024]{2,1,0:T(8,128)(2,1)S(1)}, u32[]{:S(2)}, u32[]{:S(2)}) %collective-permute-start.11) | collective-permute-done | bytes 1310752 | tf_op jit(solution)/shard_map/ppermute | solution.py:209
  146.6 7.7 %collective-permute-start.16 = (bf16[2,80,1024]{2,1,0:T(8,128)(2,1)S(1)}, bf16[2,80,1024]{2,1,0:T(8,128)(2,1)S(1)}, u32[]{:S(2)}, u32[]{:S(2)}) collective-permute-start(bf16[2,80,1024]{2,1,0:T(8,128)(2,1)S(1)} %pad_maximum_fusion.5), channel_id=1, source_target_pairs={{0,160},{16,112},{32,192},{48,144},{64,224},{80,176},{96,0},{112,2... | collective-permute-start | bytes 983048 | tf_op jit(solution)/shard_map/ppermute | solution.py:220
  154.4 4.4 %collective-permute-start.15 = (bf16[2,80,1024]{2,1,0:T(8,128)(2,1)S(1)}, bf16[2,80,1024]{2,1,0:T(8,128)(2,1)S(1)}, u32[]{:S(2)}, u32[]{:S(2)}) collective-permute-start(bf16[2,80,1024]{2,1,0:T(8,128)(2,1)S(1)} %pad_maximum_fusion.4), channel_id=1, source_target_pairs={{0,128},{16,144},{32,160},{48,176},{64,192},{80,208},{96,224},{112... | collective-permute-start | bytes 983048 | tf_op jit(solution)/shard_map/ppermute | solution.py:220
  158.8 5.7 %collective-permute-start.14 = (bf16[2,80,1024]{2,1,0:T(8,128)(2,1)S(1)}, bf16[2,80,1024]{2,1,0:T(8,128)(2,1)S(1)}, u32[]{:S(2)}, u32[]{:S(2)}) collective-permute-start(bf16[2,80,1024]{2,1,0:T(8,128)(2,1)S(1)} %pad_maximum_fusion.3), channel_id=1, source_target_pairs={{0,96},{16,176},{32,128},{48,208},{64,160},{80,240},{96,192},{112,... | collective-permute-start | bytes 983048 | tf_op jit(solution)/shard_map/ppermute | solution.py:220
  166.6 9.7 %collective-permute-done.17.refs_6_ = bf16[2,80,1024]{2,1,0:T(8,128)(2,1)S(1)} collective-permute-done((bf16[2,80,1024]{2,1,0:T(8,128)(2,1)S(1)}, bf16[2,80,1024]{2,1,0:T(8,128)(2,1)S(1)}, u32[]{:S(2)}, u32[]{:S(2)}) %collective-permute-start.17) | collective-permute-done | bytes 327712 | tf_op jit(solution)/shard_map/ppermute | solution.py:220
  179.0 3.1 %collective-permute-done.15.refs_4_ = bf16[2,80,1024]{2,1,0:T(8,128)(2,1)S(1)} collective-permute-done((bf16[2,80,1024]{2,1,0:T(8,128)(2,1)S(1)}, bf16[2,80,1024]{2,1,0:T(8,128)(2,1)S(1)}, u32[]{:S(2)}, u32[]{:S(2)}) %collective-permute-start.15) | collective-permute-done | bytes 327712 | tf_op jit(solution)/shard_map/ppermute | solution.py:220
  182.8 11.6 %collective-permute-done.14.refs_3_ = bf16[2,80,1024]{2,1,0:T(8,128)(2,1)S(1)} collective-permute-done((bf16[2,80,1024]{2,1,0:T(8,128)(2,1)S(1)}, bf16[2,80,1024]{2,1,0:T(8,128)(2,1)S(1)}, u32[]{:S(2)}, u32[]{:S(2)}) %collective-permute-start.14) | collective-permute-done | bytes 327712 | tf_op jit(solution)/shard_map/ppermute | solution.py:220
  195.1 7.3 %collective-permute-done.13.refs_2_ = bf16[2,80,1024]{2,1,0:T(8,128)(2,1)S(1)} collective-permute-done((bf16[2,80,1024]{2,1,0:T(8,128)(2,1)S(1)}, bf16[2,80,1024]{2,1,0:T(8,128)(2,1)S(1)}, u32[]{:S(2)}, u32[]{:S(2)}) %collective-permute-start.13) | collective-permute-done | bytes 327712 | tf_op jit(solution)/shard_map/ppermute | solution.py:220
  203.2 2.7 %collective-permute-done.12.refs_1_ = bf16[2,80,1024]{2,1,0:T(8,128)(2,1)S(1)} collective-permute-done((bf16[2,80,1024]{2,1,0:T(8,128)(2,1)S(1)}, bf16[2,80,1024]{2,1,0:T(8,128)(2,1)S(1)}, u32[]{:S(2)}, u32[]{:S(2)}) %collective-permute-start.12) | collective-permute-done | bytes 327712 | tf_op jit(solution)/shard_map/ppermute | solution.py:220
  209.4 2.7 %shard_map.41.refs_9_ = bf16[1024,512]{1,0:T(8,128)(2,1)S(1)} custom-call(bf16[16,12,64,128]{3,2,1,0:T(8,128)(2,1)S(1)} %all-to-all-done.2.arrived.refs_8_, bf16[512,512]{1,0:T(8,128)(2,1)S(1)} %copy-done.5), custom_call_target="tpu_custom_call" | custom-call | flops 536870912 | bytes 2097152 | tf_op jit(solution)/shard_map/pallas_call | solution.py:311
  212.2 5.3 %shard_map.42.base = f32[8,128,512]{2,1,0:T(8,128)S(1)} custom-call(s32[128]{0:T(128)S(1)} %select_reduce_fusion.1.inv_ref, s32[128]{0:T(128)S(1)} %select_reduce_fusion.inv2_ref, bf16[2,80,1024]{2,1,0:T(8,128)(2,1)S(1)} %pad_maximum_fusion.refs_0_, bf16[2,80,1024]{2,1,0:T(8,128)(2,1)S(1)} %copy-done.21, bf16[2,80,1024]{2,1,0:T(8,128)(2,1)S(1)} %copy-done.19, ...), custom_call_target="tpu_custom_call" | custom-call | flops 805306368 | bytes 6291456 | tf_op jit(solution)/shard_map/pallas_call | solution.py:317
  217.5 7.1 %collective-permute-done.19.got_b = bf16[8,64,512]{2,1,0:T(8,128)(2,1)S(1)} collective-permute-done((bf16[8,64,512]{2,1,0:T(8,128)(2,1)S(1)}, bf16[8,64,512]{2,1,0:T(8,128)(2,1)S(1)}, u32[]{:S(2)}, u32[]{:S(2)}) %collective-permute-start.19) | collective-permute-done | bytes 524320 | tf_op jit(solution)/shard_map/ppermute | solution.py:310
  (135 shorter events, 53.7 us)
Async XLA Ops:
  10.1 66.0 %all-to-all-start = ((bf16[16,9,64,128]{3,2,1,0:T(8,128)(2,1)}), bf16[16,9,64,128]{3,2,1,0:T(8,128)(2,1)S(1)}, u32[]{:S(2)}, u32[]{:S(2)}) async-start(bf16[16,9,64,128]{3,2,1,0:T(8,128)(2,1)} %copy-done.4), calls=%async_computation | async-start | bytes 4718592 | tf_op jit(solution)/shard_map/all_to_all | solution.py:280
  18.8 7.2 %collective-permute-start.1 = (bf16[8,64,1024]{2,1,0:T(8,128)(2,1)}, bf16[8,64,1024]{2,1,0:T(8,128)(2,1)}, u32[]{:S(2)}, u32[]{:S(2)}) collective-permute-start(bf16[8,64,1024]{2,1,0:T(8,128)(2,1)} %copy-done.32), channel_id=1, source_target_pairs={{0,16},{16,0},{32,48},{48,32},{64,80},{80,64},{96,112},{112,96},{1... | collective-permute-start | bytes 3145736 | tf_op jit(solution)/shard_map/ppermute | solution.py:209
  20.7 32.8 %collective-permute-start = (s32[128]{0:T(128)S(1)}, s32[128]{0:T(128)S(1)}, u32[]{:S(2)}, u32[]{:S(2)}) collective-permute-start(s32[128]{0:T(128)S(1)} %bitcast.31), channel_id=1, source_target_pairs={{0,256},{256,0},{1,257},{257,1},{2,258},{258,2},{3,259},{259,3},{4... | collective-permute-start | bytes 1544 | tf_op jit(solution)/shard_map/ppermute | solution.py:271
  28.8 27.3 %collective-permute-start.6 = (bf16[2,64,1024]{2,1,0:T(8,128)(2,1)}, bf16[2,64,1024]{2,1,0:T(8,128)(2,1)S(1)}, u32[]{:S(2)}, u32[]{:S(2)}) collective-permute-start(bf16[2,64,1024]{2,1,0:T(8,128)(2,1)} %pad_maximum_fusion.12), channel_id=1, source_target_pairs={{0,96},{16,176},{32,128},{48,208},{64,160},{80,240},{96,192},{112,... | collective-permute-start | bytes 786440 | tf_op jit(solution)/shard_map/ppermute | solution.py:220
  36.6 20.6 %collective-permute-start.5 = (bf16[2,64,1024]{2,1,0:T(8,128)(2,1)}, bf16[2,64,1024]{2,1,0:T(8,128)(2,1)S(1)}, u32[]{:S(2)}, u32[]{:S(2)}) collective-permute-start(bf16[2,64,1024]{2,1,0:T(8,128)(2,1)} %pad_maximum_fusion.11), channel_id=1, source_target_pairs={{0,128},{16,144},{32,160},{48,176},{64,192},{80,208},{96,224},{112... | collective-permute-start | bytes 786440 | tf_op jit(solution)/shard_map/ppermute | solution.py:220
  45.6 24.9 %collective-permute-start.4 = (bf16[2,64,1024]{2,1,0:T(8,128)(2,1)}, bf16[2,64,1024]{2,1,0:T(8,128)(2,1)S(1)}, u32[]{:S(2)}, u32[]{:S(2)}) collective-permute-start(bf16[2,64,1024]{2,1,0:T(8,128)(2,1)} %pad_maximum_fusion.10), channel_id=1, source_target_pairs={{0,160},{16,112},{32,192},{48,144},{64,224},{80,176},{96,0},{112,2... | collective-permute-start | bytes 786440 | tf_op jit(solution)/shard_map/ppermute | solution.py:220
  50.0 23.3 %collective-permute-start.3 = (bf16[2,64,1024]{2,1,0:T(8,128)(2,1)}, bf16[2,64,1024]{2,1,0:T(8,128)(2,1)S(1)}, u32[]{:S(2)}, u32[]{:S(2)}) collective-permute-start(bf16[2,64,1024]{2,1,0:T(8,128)(2,1)} %pad_maximum_fusion.9), channel_id=1, source_target_pairs={{0,192},{16,80},{32,224},{48,112},{64,0},{80,144},{96,32},{112,176... | collective-permute-start | bytes 786440 | tf_op jit(solution)/shard_map/ppermute | solution.py:220
  53.6 22.6 %collective-permute-start.2 = (bf16[2,64,1024]{2,1,0:T(8,128)(2,1)}, bf16[2,64,1024]{2,1,0:T(8,128)(2,1)}, u32[]{:S(2)}, u32[]{:S(2)}) collective-permute-start(bf16[2,64,1024]{2,1,0:T(8,128)(2,1)} %pad_maximum_fusion.8), channel_id=1, source_target_pairs={{0,224},{16,48},{32,0},{48,80},{64,32},{80,112},{96,64},{112,144},... | collective-permute-start | bytes 786440 | tf_op jit(solution)/shard_map/ppermute | solution.py:220
  56.1 20.7 %copy-start.22 = (bf16[2,64,1024]{2,1,0:T(8,128)(2,1)}, bf16[2,64,1024]{2,1,0:T(8,128)(2,1)S(1)}, u32[]{:S(2)}) copy-start(bf16[2,64,1024]{2,1,0:T(8,128)(2,1)S(1)} %collective-permute-done.6.refs_3_) | copy-start | bytes 786436
  57.2 19.7 %copy-start.24 = (bf16[2,64,1024]{2,1,0:T(8,128)(2,1)}, bf16[2,64,1024]{2,1,0:T(8,128)(2,1)S(1)}, u32[]{:S(2)}) copy-start(bf16[2,64,1024]{2,1,0:T(8,128)(2,1)S(1)} %collective-permute-done.5.refs_4_) | copy-start | bytes 786436
  77.6 28.9 %collective-permute-start.7 = (bf16[8,64,512]{2,1,0:T(8,128)(2,1)S(1)}, bf16[8,64,512]{2,1,0:T(8,128)(2,1)S(1)}, u32[]{:S(2)}, u32[]{:S(2)}) collective-permute-start(bf16[8,64,512]{2,1,0:T(8,128)(2,1)S(1)} %shard_map.38), channel_id=1, source_target_pairs={{0,256},{256,0},{1,257},{257,1},{2,258},{258,2},{3,259},{259,3},{4... | collective-permute-start | bytes 1572872 | tf_op jit(solution)/shard_map/ppermute | solution.py:290
  84.5 28.8 %copy-start.33 = (bf16[1,64,1024]{2,1,0:T(8,128)(2,1)S(1)}, bf16[1,64,1024]{2,1,0:T(8,128)(2,1)}, u32[]{:S(2)}) copy-start(bf16[1,64,1024]{2,1,0:T(8,128)(2,1)} %get-tuple-element.73) | copy-start | bytes 393220
  84.5 21.9 %all-to-all-start.1 = ((bf16[32,4,8,128]{3,2,1,0:T(8,128)(2,1)}), bf16[32,4,8,128]{3,2,1,0:T(8,128)(2,1)}, u32[]{:S(2)}, u32[]{:S(2)}) async-start(bf16[32,4,8,128]{3,2,1,0:T(8,128)(2,1)} %gather_fusion.1), calls=%async_computation.1 | async-start | bytes 524288 | tf_op jit(solution)/shard_map/all_to_all | solution.py:242
  94.6 19.7 %copy-start.23 = (bf16[2,64,1024]{2,1,0:T(8,128)(2,1)S(1)}, bf16[2,64,1024]{2,1,0:T(8,128)(2,1)}, u32[]{:S(2)}) copy-start(bf16[2,64,1024]{2,1,0:T(8,128)(2,1)} %copy-done.22) | copy-start | bytes 786436
  94.6 19.7 %copy-start.25 = (bf16[2,64,1024]{2,1,0:T(8,128)(2,1)S(1)}, bf16[2,64,1024]{2,1,0:T(8,128)(2,1)}, u32[]{:S(2)}) copy-start(bf16[2,64,1024]{2,1,0:T(8,128)(2,1)} %copy-done.24) | copy-start | bytes 786436
  94.6 19.7 %copy-start.27 = (bf16[2,64,1024]{2,1,0:T(8,128)(2,1)S(1)}, bf16[2,64,1024]{2,1,0:T(8,128)(2,1)}, u32[]{:S(2)}) copy-start(bf16[2,64,1024]{2,1,0:T(8,128)(2,1)} %copy-done.26) | copy-start | bytes 786436
  94.6 19.7 %copy-start.29 = (bf16[2,64,1024]{2,1,0:T(8,128)(2,1)S(1)}, bf16[2,64,1024]{2,1,0:T(8,128)(2,1)}, u32[]{:S(2)}) copy-start(bf16[2,64,1024]{2,1,0:T(8,128)(2,1)} %copy-done.28) | copy-start | bytes 786436
  95.7 18.6 %collective-permute-start.9 = (bf16[2,64,1024]{2,1,0:T(8,128)(2,1)S(1)}, bf16[2,64,1024]{2,1,0:T(8,128)(2,1)S(1)}, u32[]{:S(2)}, u32[]{:S(2)}) collective-permute-start(bf16[2,64,1024]{2,1,0:T(8,128)(2,1)S(1)} %pad_maximum_fusion.15), channel_id=1, source_target_pairs={{0,64},{16,208},{32,96},{48,240},{64,128},{80,16},{96,160},{112,48... | collective-permute-start | bytes 786440 | tf_op jit(solution)/shard_map/ppermute | solution.py:220
  101.7 12.6 %collective-permute-start.8 = (bf16[2,64,1024]{2,1,0:T(8,128)(2,1)}, bf16[2,64,1024]{2,1,0:T(8,128)(2,1)S(1)}, u32[]{:S(2)}, u32[]{:S(2)}) collective-permute-start(bf16[2,64,1024]{2,1,0:T(8,128)(2,1)} %pad_maximum_fusion.14), channel_id=1, source_target_pairs={{0,32},{16,240},{32,64},{48,16},{64,96},{80,48},{96,128},{112,80},... | collective-permute-start | bytes 786440 | tf_op jit(solution)/shard_map/ppermute | solution.py:220
  109.7 12.6 %collective-permute-start.10 = (bf16[32,512]{1,0:T(8,128)(2,1)S(1)}, bf16[32,512]{1,0:T(8,128)(2,1)S(1)}, u32[]{:S(2)}, u32[]{:S(2)}) collective-permute-start(bf16[32,512]{1,0:T(8,128)(2,1)S(1)} %constant_dynamic-slice_fusion.3), channel_id=1, source_target_pairs={{0,0},{1,16},{2,32},{3,48},{4,64},{5,80},{6,96},{7,112},{8,128},{9... | collective-permute-start | bytes 98312 | tf_op jit(solution)/shard_map/ppermute | solution.py:261
  122.3 84.3 %all-to-all-start.2 = ((bf16[16,12,64,128]{3,2,1,0:T(8,128)(2,1)}), bf16[16,12,64,128]{3,2,1,0:T(8,128)(2,1)S(1)}, u32[]{:S(2)}, u32[]{:S(2)}) async-start(bf16[16,12,64,128]{3,2,1,0:T(8,128)(2,1)} %copy-done.2), calls=%async_computation.2 | async-start | bytes 6291456 | tf_op jit(solution)/shard_map/all_to_all | solution.py:298
  137.6 4.9 %collective-permute-start.11 = (bf16[8,80,1024]{2,1,0:T(8,128)(2,1)S(1)}, bf16[8,80,1024]{2,1,0:T(8,128)(2,1)S(1)}, u32[]{:S(2)}, u32[]{:S(2)}) collective-permute-start(bf16[8,80,1024]{2,1,0:T(8,128)(2,1)S(1)} %get-tuple-element.45), channel_id=1, source_target_pairs={{0,16},{16,0},{32,48},{48,32},{64,80},{80,64},{96,112},{112,96},{1... | collective-permute-start | bytes 3932168 | tf_op jit(solution)/shard_map/ppermute | solution.py:209
  142.7 21.9 %collective-permute-start.18 = (bf16[2,80,1024]{2,1,0:T(8,128)(2,1)S(1)}, bf16[2,80,1024]{2,1,0:T(8,128)(2,1)S(1)}, u32[]{:S(2)}, u32[]{:S(2)}) collective-permute-start(bf16[2,80,1024]{2,1,0:T(8,128)(2,1)S(1)} %pad_maximum_fusion.7), channel_id=1, source_target_pairs={{0,224},{16,48},{32,0},{48,80},{64,32},{80,112},{96,64},{112,144},... | collective-permute-start | bytes 983048 | tf_op jit(solution)/shard_map/ppermute | solution.py:220
  144.7 31.6 %collective-permute-start.17 = (bf16[2,80,1024]{2,1,0:T(8,128)(2,1)S(1)}, bf16[2,80,1024]{2,1,0:T(8,128)(2,1)S(1)}, u32[]{:S(2)}, u32[]{:S(2)}) collective-permute-start(bf16[2,80,1024]{2,1,0:T(8,128)(2,1)S(1)} %pad_maximum_fusion.6), channel_id=1, source_target_pairs={{0,192},{16,80},{32,224},{48,112},{64,0},{80,144},{96,32},{112,176... | collective-permute-start | bytes 983048 | tf_op jit(solution)/shard_map/ppermute | solution.py:220
  146.6 31.6 %collective-permute-start.16 = (bf16[2,80,1024]{2,1,0:T(8,128)(2,1)S(1)}, bf16[2,80,1024]{2,1,0:T(8,128)(2,1)S(1)}, u32[]{:S(2)}, u32[]{:S(2)}) collective-permute-start(bf16[2,80,1024]{2,1,0:T(8,128)(2,1)S(1)} %pad_maximum_fusion.5), channel_id=1, source_target_pairs={{0,160},{16,112},{32,192},{48,144},{64,224},{80,176},{96,0},{112,2... | collective-permute-start | bytes 983048 | tf_op jit(solution)/shard_map/ppermute | solution.py:220
  154.4 27.7 %collective-permute-start.15 = (bf16[2,80,1024]{2,1,0:T(8,128)(2,1)S(1)}, bf16[2,80,1024]{2,1,0:T(8,128)(2,1)S(1)}, u32[]{:S(2)}, u32[]{:S(2)}) collective-permute-start(bf16[2,80,1024]{2,1,0:T(8,128)(2,1)S(1)} %pad_maximum_fusion.4), channel_id=1, source_target_pairs={{0,128},{16,144},{32,160},{48,176},{64,192},{80,208},{96,224},{112... | collective-permute-start | bytes 983048 | tf_op jit(solution)/shard_map/ppermute | solution.py:220
  158.8 35.6 %collective-permute-start.14 = (bf16[2,80,1024]{2,1,0:T(8,128)(2,1)S(1)}, bf16[2,80,1024]{2,1,0:T(8,128)(2,1)S(1)}, u32[]{:S(2)}, u32[]{:S(2)}) collective-permute-start(bf16[2,80,1024]{2,1,0:T(8,128)(2,1)S(1)} %pad_maximum_fusion.3), channel_id=1, source_target_pairs={{0,96},{16,176},{32,128},{48,208},{64,160},{80,240},{96,192},{112,... | collective-permute-start | bytes 983048 | tf_op jit(solution)/shard_map/ppermute | solution.py:220
  164.6 37.8 %copy-start.8 = (bf16[2,80,1024]{2,1,0:T(8,128)(2,1)}, bf16[2,80,1024]{2,1,0:T(8,128)(2,1)S(1)}, u32[]{:S(2)}) copy-start(bf16[2,80,1024]{2,1,0:T(8,128)(2,1)S(1)} %collective-permute-done.18.refs_7_) | copy-start | bytes 983044
  164.6 37.8 %collective-permute-start.13 = (bf16[2,80,1024]{2,1,0:T(8,128)(2,1)S(1)}, bf16[2,80,1024]{2,1,0:T(8,128)(2,1)S(1)}, u32[]{:S(2)}, u32[]{:S(2)}) collective-permute-start(bf16[2,80,1024]{2,1,0:T(8,128)(2,1)S(1)} %pad_maximum_fusion.2), channel_id=1, source_target_pairs={{0,64},{16,208},{32,96},{48,240},{64,128},{80,16},{96,160},{112,48... | collective-permute-start | bytes 983048 | tf_op jit(solution)/shard_map/ppermute | solution.py:220
  176.3 26.2 %copy-start.10 = (bf16[2,80,1024]{2,1,0:T(8,128)(2,1)}, bf16[2,80,1024]{2,1,0:T(8,128)(2,1)S(1)}, u32[]{:S(2)}) copy-start(bf16[2,80,1024]{2,1,0:T(8,128)(2,1)S(1)} %collective-permute-done.17.refs_6_) | copy-start | bytes 983044
  176.3 29.6 %collective-permute-start.12 = (bf16[2,80,1024]{2,1,0:T(8,128)(2,1)S(1)}, bf16[2,80,1024]{2,1,0:T(8,128)(2,1)S(1)}, u32[]{:S(2)}, u32[]{:S(2)}) collective-permute-start(bf16[2,80,1024]{2,1,0:T(8,128)(2,1)S(1)} %pad_maximum_fusion.1), channel_id=1, source_target_pairs={{0,32},{16,240},{32,64},{48,16},{64,96},{80,48},{96,128},{112,80},... | collective-permute-start | bytes 983048 | tf_op jit(solution)/shard_map/ppermute | solution.py:220
  207.4 17.2 %collective-permute-start.19 = (bf16[8,64,512]{2,1,0:T(8,128)(2,1)S(1)}, bf16[8,64,512]{2,1,0:T(8,128)(2,1)S(1)}, u32[]{:S(2)}, u32[]{:S(2)}) collective-permute-start(bf16[8,64,512]{2,1,0:T(8,128)(2,1)S(1)} %shard_map.43), channel_id=1, source_target_pairs={{0,256},{256,0},{1,257},{257,1},{2,258},{258,2},{3,259},{259,3},{4... | collective-permute-start | bytes 1572872 | tf_op jit(solution)/shard_map/ppermute | solution.py:310
  (25 other events, 81.3 us)

commit v3 on v2

--- a/solution.py
+++ b/solution.py
@@ -58,23 +58,26 @@
     return pl.ds(pl.multiple_of(j * B, B), B)
 
 
-def pack(map_ref, tile, column, a, own, swap, sem_a, sem_b, sem_c):
+def pack_cols(map_ref, tile, column, a, sem_a, sem_c):
     for v in range(W):
         pltpu.make_async_copy(
             tile.at[:, pl.ds(0, HA), pl.ds(v * B, B)], a.at[col_slot(map_ref, v), pl.ds(0, W)], sem_a
         ).start()
     sixteenths = pltpu.make_async_copy(column, a.at[:, W], sem_c)
     sixteenths.start()
+    done = a.at[pl.ds(0, W), pl.ds(0, W)]
+    pltpu.make_async_copy(done, done, sem_a).wait()
+    sixteenths.wait()
+
+
+def pack_rows(map_ref, tile, own, swap, sem):
     for q in range(W):
         e, k = row_slot(map_ref, q)
         for side, ob in enumerate((own, swap)):
             @pl.when(e == side)
             def _():
-                pltpu.make_async_copy(tile.at[q, pl.ds(HA, HB), :], ob.at[k], sem_b).start()
-    done = a.at[pl.ds(0, W), pl.ds(0, W)]
-    pltpu.make_async_copy(done, done, sem_a).wait()
-    pltpu.make_async_copy(own, own, sem_b).wait()
-    sixteenths.wait()
+                pltpu.make_async_copy(tile.at[q, pl.ds(HA, HB), :], ob.at[k], sem).start()
+    pltpu.make_async_copy(own, own, sem).wait()
 
 
 def cols_to_rows(map_ref, map2_ref, inv_ref, arrived, taken, tail, own, swap, sem, sem_t):
@@ -104,8 +107,8 @@
         pltpu.make_async_copy(done, done, sem_t).wait()
 
 
-def rows_to_cols(map_ref, inv_ref, piece, *refs):
-    arrived, a, sem, sem_p = refs[:8], refs[8], refs[9], refs[10]
+def rows_to_cols(map_ref, inv_ref, *refs):
+    arrived, a, sem = refs[:8], refs[8], refs[9]
 
     @pl.loop(0, W)
     def _(i):
@@ -117,12 +120,15 @@
                     pltpu.make_async_copy(
                         arrived[step].at[e, :, pl.ds(v * B, B)], a.at[col_slot(map_ref, v), i], sem
                     ).start()
-    for t in range(G):
-        pltpu.make_async_copy(piece, a.at[t, pl.ds(W, 4)], sem_p).start()
     done = a.at[pl.ds(0, W), pl.ds(0, W)]
     pltpu.make_async_copy(done, done, sem).wait()
-    done = a.at[:, pl.ds(W, 4)]
-    pltpu.make_async_copy(done, done, sem_p).wait()
+
+
+def add_piece(piece, a, filled, sem):
+    for t in range(G):
+        pltpu.make_async_copy(piece, filled.at[t, pl.ds(W, 4)], sem).start()
+    done = filled.at[:, pl.ds(W, 4)]
+    pltpu.make_async_copy(done, done, sem).wait()
 
 
 def hand_cols(inv_ref, arrived, hand, sem):
@@ -233,19 +239,21 @@
     return jnp.transpose(column.reshape(W, G, 8, B), (1, 0, 2, 3)).reshape(G, W * 8, B)
 
 
-def panel_piece(got, maps, inv, inv2, early):
-    sib, row = lax.axis_index("sib"), lax.axis_index("row")
+def panel_slots(got, maps, inv):
     got = jnp.transpose(jnp.take(got, inv[:4] // W, axis=0, mode="clip"), (1, 0, 2, 3))
-    targets = lax.dynamic_slice_in_dim(maps, row * W, W, 0) // W
+    targets = lax.dynamic_slice_in_dim(maps, lax.axis_index("row") * W, W, 0) // W
     match = targets[None, :] == (jnp.arange(2 * G, dtype=jnp.int32) % G)[:, None]
     source = jnp.sum(jnp.where(match, jnp.arange(W, dtype=jnp.int32)[None, :], 0), axis=1)
-    got = lax.all_to_all(jnp.take(got, source, axis=0, mode="clip"), ("sib", "row"), 0, 0, tiled=True)
-    got, early = lax.optimization_barrier((got, early))
+    return jnp.take(got, source, axis=0, mode="clip")
+
+
+def panel_piece(got, inv, inv2):
+    sib, row = lax.axis_index("sib"), lax.axis_index("row")
     parts = [
         jnp.take(got, child * G + lax.dynamic_slice_in_dim(ref, row * W, W, 0) // W, axis=0, mode="clip").astype(jnp.float32)
         for child, ref in ((sib, inv), (1 - sib, inv2))
     ]
-    return (parts[0] + parts[1]).astype(jnp.bfloat16), early
+    return (parts[0] + parts[1]).astype(jnp.bfloat16)
 
 
 def tail_piece(piece):
@@ -273,27 +281,38 @@
     blocks = tile.reshape(W, B, W * B)
 
     rows_a, rows_b = bf16(8, HA + TAIL, W * B), bf16(8, HB, W * B)
-    send_a, own, swap = pl.pallas_call(
-        pack, out_shape=(bf16(G, W + 1, HA, B), rows_b, rows_b), in_specs=[SMEM, ANY, ANY], out_specs=(ANY, ANY, ANY),
-        scratch_shapes=[dma, dma, dma], **params(moved=4 * MiB),
+    send_a = pl.pallas_call(
+        pack_cols, out_shape=bf16(G, W + 1, HA, B), in_specs=[SMEM, ANY, ANY], out_specs=ANY,
+        scratch_shapes=[dma, dma], **params(moved=2 * MiB),
     )(maps, blocks, panel_column(tile, maps))
+    own, swap = pl.pallas_call(
+        pack_rows, out_shape=(rows_b, rows_b), in_specs=[SMEM, ANY], out_specs=(ANY, ANY), scratch_shapes=[dma],
+        **params(moved=2 * MiB),
+    )(maps, blocks)
     got_a = lax.all_to_all(send_a, "col", 0, 0, tiled=True)
     got_b = z_ring(pairs_of(own, core_exchange(swap)))
-    got_a, maps2, got_b[7], got_b[6], got_b[5], got_b[4], got_b[3] = lax.optimization_barrier(
-        (got_a, maps2, got_b[7], got_b[6], got_b[5], got_b[4], got_b[3]))
+    got_a, maps2, got_b[7], got_b[6], got_b[5] = lax.optimization_barrier(
+        (got_a, maps2, got_b[7], got_b[6], got_b[5]))
 
     inv2 = inverse_of(maps2)
+    pieces, got_a = lax.optimization_barrier((panel_slots(got_a[:, W].reshape(G, W, 8, B), maps, inv), got_a))
     hand_a = pl.pallas_call(
         hand_cols, out_shape=bf16(W, HA, PANEL), in_specs=[SMEM, ANY], out_specs=VMEM, scratch_shapes=[dma],
         **params(moved=MiB),
     )(inv, got_a)
     taken_a = lax.ppermute(hand_a, "sib", exchange)
-    piece, taken_a = panel_piece(got_a[:, W].reshape(G, W, 8, B), maps, inv, inv2, taken_a)
+    send_b = pl.pallas_call(
+        rows_to_cols, out_shape=bf16(G, W + 4, HB, B), in_specs=[SMEM, SMEM] + [ANY] * 8, out_specs=ANY,
+        scratch_shapes=[dma], **params(moved=2 * MiB),
+    )(maps, inv, *got_b)
+    pieces = lax.all_to_all(pieces, ("sib", "row"), 0, 0, tiled=True)
+    pieces, taken_a, send_b = lax.optimization_barrier((pieces, taken_a, send_b))
+    piece = panel_piece(pieces, inv, inv2)
     tail = tail_piece(piece)
     send_b = pl.pallas_call(
-        rows_to_cols, out_shape=bf16(G, W + 4, HB, B), in_specs=[SMEM, SMEM] + [ANY] * 9, out_specs=ANY,
-        scratch_shapes=[dma, dma], **params(moved=3 * MiB),
-    )(maps, inv, jnp.transpose(piece, (1, 0, 2, 3)).reshape(4, W * 8, B), *got_b)
+        add_piece, out_shape=bf16(G, W + 4, HB, B), in_specs=[ANY, ANY], out_specs=ANY, scratch_shapes=[dma],
+        input_output_aliases={1: 0}, **params(moved=MiB),
+    )(jnp.transpose(piece, (1, 0, 2, 3)).reshape(4, W * 8, B), send_b)
     send_b, tail = lax.optimization_barrier((send_b, tail))
     got_b = lax.all_to_all(send_b, "col", 0, 0, tiled=True)
     own, swap = pl.pallas_call(

time: 228 us -> 221 us (0.969)
  waiting for transfers between devices: 66.7 us -> 59.2 us
  other arithmetic: 9.65 us -> 6.26 us
    ppermute x14, waiting for transfers between devices: 52.9 us -> 33.2 us  [z_ring(): arrived[k] = lax.ppermute(both[k], 'row', pairs)]
    all_to_all x1, waiting for transfers between devices: 0.01 us -> 5.1 us  [shards(): got_a = lax.all_to_all(send_a, 'col', 0, 0, tiled=True)]
    another operation x16, other arithmetic: 7.67 us -> 4.28 us  [pairs_of(): return [jnp.stack([own[k], other[k]]) for k in range(8)]]
    all_to_all x1, starting transfers between devices: 10.1 us -> 13.4 us  [shards(): pieces = lax.all_to_all(pieces, ('sib', 'row'), 0, 0, tiled=True)]
    all_to_all x1, waiting for transfers between devices: 1.17 us -> 4.45 us  [shards(): pieces = lax.all_to_all(pieces, ('sib', 'row'), 0, 0, tiled=True)]
    ppermute x1, waiting for transfers between devices: 2.63 us -> 5.64 us  [tail_piece(): got = lax.ppermute(send, ('sib', 'row', 'col'), pairs)]
    all_to_all x1, starting transfers between devices: 10.3 us -> 7.63 us  [shards(): got_b = lax.all_to_all(send_b, 'col', 0, 0, tiled=True)]
    unnamed x68 -> x58, local copies, waits for them, and re-layouts: 14.1 us -> 15.8 us
  transfers between devices with their start and end apart: 23 -> 23, of which waited for: 13 -> 11; matrix products, arithmetic and copies ran while one was open for 8% -> 5% of each run, Pallas kernels for 6% -> 8%
where the time goes in v3:
time: 221 us; the launch traced here: 220 us
  starting transfers between devices  105 us (48%)
  waiting for transfers between devices  59.2 us (27%)
  local copies, waits for them, and re-layouts  26.6 us (12%)
  Pallas kernels  21.5 us (10%)
  other arithmetic  6.26 us (3%)
    ppermute x14, starting transfers between devices, z_ring(): arrived[k] = lax.ppermute(both[k], 'row', pairs)  57.4 us
    ppermute x14, waiting for transfers between devices, z_ring(): arrived[k] = lax.ppermute(both[k], 'row', pairs)  33.2 us
    unnamed x58, local copies, waits for them, and re-layouts  15.8 us
    all_to_all x1, starting transfers between devices, shards(): pieces = lax.all_to_all(pieces, ('sib', 'row'), 0, 0, tiled=True)  13.4 us
    all_to_all x1, starting transfers between devices, shards(): got_a = lax.all_to_all(send_a, 'col', 0, 0, tiled=True)  8.71 us
    all_to_all x1, starting transfers between devices, shards(): got_b = lax.all_to_all(send_b, 'col', 0, 0, tiled=True)  7.63 us
    ppermute x1, waiting for transfers between devices, shards(): taken_b = lax.ppermute(hand_b, 'sib', exchange)  6.07 us
    ppermute x1, waiting for transfers between devices, tail_piece(): got = lax.ppermute(send, ('sib', 'row', 'col'), pairs)  5.64 us
  transfers between devices with their start and end apart: 23, of which 11 were waited for; matrix products, arithmetic and copies ran while one was open for 5% of the time, Pallas kernels for 8%

profile of v3, /device:TPU:6, one launch (start us, length us, event | category | flops | bytes accessed | tf_op | source)
XLA Modules:
  0.0 220.1 jit_solution(41259409347214120)
XLA Ops:
  7.6 8.7 %all-to-all-start = ((bf16[16,9,64,128]{3,2,1,0:T(8,128)(2,1)}), bf16[16,9,64,128]{3,2,1,0:T(8,128)(2,1)S(1)}, u32[]{:S(2)}, u32[]{:S(2)}) async-start(bf16[16,9,64,128]{3,2,1,0:T(8,128)(2,1)} %copy-done.5), calls=%async_computation | async-start | bytes 4718592 | tf_op jit(solution)/shard_map/all_to_all | solution.py:292
  16.3 4.2 %collective-permute-start = (s32[128]{0:T(128)S(1)}, s32[128]{0:T(128)S(1)}, u32[]{:S(2)}, u32[]{:S(2)}) collective-permute-start(s32[128]{0:T(128)S(1)} %bitcast.32), channel_id=1, source_target_pairs={{0,256},{256,0},{1,257},{257,1},{2,258},{258,2},{3,259},{259,3},{4... | collective-permute-start | bytes 1544 | tf_op jit(solution)/shard_map/ppermute | solution.py:279
  28.6 2.0 fusion.9
  30.7 10.1 %collective-permute-start.2 = (bf16[2,64,1024]{2,1,0:T(8,128)(2,1)S(1)}, bf16[2,64,1024]{2,1,0:T(8,128)(2,1)S(1)}, u32[]{:S(2)}, u32[]{:S(2)}) collective-permute-start(bf16[2,64,1024]{2,1,0:T(8,128)(2,1)S(1)} %pad_maximum_fusion.8), channel_id=1, source_target_pairs={{0,224},{16,48},{32,0},{48,80},{64,32},{80,112},{96,64},{112,144},... | collective-permute-start | bytes 786440 | tf_op jit(solution)/shard_map/ppermute | solution.py:226
  40.8 2.8 %collective-permute-start.3 = (bf16[2,64,1024]{2,1,0:T(8,128)(2,1)S(1)}, bf16[2,64,1024]{2,1,0:T(8,128)(2,1)S(1)}, u32[]{:S(2)}, u32[]{:S(2)}) collective-permute-start(bf16[2,64,1024]{2,1,0:T(8,128)(2,1)S(1)} %pad_maximum_fusion.9), channel_id=1, source_target_pairs={{0,192},{16,80},{32,224},{48,112},{64,0},{80,144},{96,32},{112,176... | collective-permute-start | bytes 786440 | tf_op jit(solution)/shard_map/ppermute | solution.py:226
  46.4 3.4 %collective-permute-start.6 = (bf16[2,64,1024]{2,1,0:T(8,128)(2,1)}, bf16[2,64,1024]{2,1,0:T(8,128)(2,1)S(1)}, u32[]{:S(2)}, u32[]{:S(2)}) collective-permute-start(bf16[2,64,1024]{2,1,0:T(8,128)(2,1)} %pad_maximum_fusion.12), channel_id=1, source_target_pairs={{0,32},{16,240},{32,64},{48,16},{64,96},{80,48},{96,128},{112,80},... | collective-permute-start | bytes 786440 | tf_op jit(solution)/shard_map/ppermute | solution.py:226
  52.0 4.8 %collective-permute-start.7 = (bf16[2,64,1024]{2,1,0:T(8,128)(2,1)}, bf16[2,64,1024]{2,1,0:T(8,128)(2,1)}, u32[]{:S(2)}, u32[]{:S(2)}) collective-permute-start(bf16[2,64,1024]{2,1,0:T(8,128)(2,1)} %pad_maximum_fusion.13), channel_id=1, source_target_pairs={{0,64},{16,208},{32,96},{48,240},{64,128},{80,16},{96,160},{112,48... | collective-permute-start | bytes 786440 | tf_op jit(solution)/shard_map/ppermute | solution.py:226
  56.8 4.6 %collective-permute-start.8 = (bf16[2,64,1024]{2,1,0:T(8,128)(2,1)}, bf16[2,64,1024]{2,1,0:T(8,128)(2,1)}, u32[]{:S(2)}, u32[]{:S(2)}) collective-permute-start(bf16[2,64,1024]{2,1,0:T(8,128)(2,1)} %pad_maximum_fusion.14), channel_id=1, source_target_pairs={{0,96},{16,176},{32,128},{48,208},{64,160},{80,240},{96,192},{112,... | collective-permute-start | bytes 786440 | tf_op jit(solution)/shard_map/ppermute | solution.py:226
  61.4 4.3 %collective-permute-start.9 = (bf16[2,64,1024]{2,1,0:T(8,128)(2,1)}, bf16[2,64,1024]{2,1,0:T(8,128)(2,1)}, u32[]{:S(2)}, u32[]{:S(2)}) collective-permute-start(bf16[2,64,1024]{2,1,0:T(8,128)(2,1)} %pad_maximum_fusion.15), channel_id=1, source_target_pairs={{0,128},{16,144},{32,160},{48,176},{64,192},{80,208},{96,224},{112... | collective-permute-start | bytes 786440 | tf_op jit(solution)/shard_map/ppermute | solution.py:226
  65.7 5.1 %all-to-all-done.arrived = bf16[16,9,64,128]{3,2,1,0:T(8,128)(2,1)S(1)} async-done(((bf16[16,9,64,128]{3,2,1,0:T(8,128)(2,1)}), bf16[16,9,64,128]{3,2,1,0:T(8,128)(2,1)S(1)}, u32[]{:S(2)}, u32[]{:S(2)}) %all-to-all-start) | async-done | bytes 2359328 | tf_op jit(solution)/shard_map/all_to_all | solution.py:292
  76.1 3.5 %collective-permute-start.5 = (bf16[8,64,512]{2,1,0:T(8,128)(2,1)}, bf16[8,64,512]{2,1,0:T(8,128)(2,1)}, u32[]{:S(2)}, u32[]{:S(2)}) collective-permute-start(bf16[8,64,512]{2,1,0:T(8,128)(2,1)} %shard_map.39), channel_id=1, source_target_pairs={{0,256},{256,0},{1,257},{257,1},{2,258},{258,2},{3,259},{259,3},{4... | collective-permute-start | bytes 1572872 | tf_op jit(solution)/shard_map/ppermute | solution.py:303
  79.6 13.4 %all-to-all-start.1 = ((bf16[32,4,8,128]{3,2,1,0:T(8,128)(2,1)}), bf16[32,4,8,128]{3,2,1,0:T(8,128)(2,1)}, u32[]{:S(2)}, u32[]{:S(2)}) async-start(bf16[32,4,8,128]{3,2,1,0:T(8,128)(2,1)} %gather_fusion.1), calls=%async_computation.1 | async-start | bytes 524288 | tf_op jit(solution)/shard_map/all_to_all | solution.py:308
  97.5 2.6 %shard_map.40.a = bf16[16,12,64,128]{3,2,1,0:T(8,128)(2,1)S(1)} custom-call(s32[128]{0:T(128)S(1)} %bitcast.35, s32[128]{0:T(128)S(1)} %select_reduce_fusion.1.inv_ref, bf16[2,64,1024]{2,1,0:T(8,128)(2,1)S(1)} %pad_maximum_fusion.11.refs_0_, bf16[2,64,1024]{2,1,0:T(8,128)(2,1)S(1)} %copy-done.26, bf16[2,64,1024]{2,1,0:T(8,128)(2,1)} %collective-permute-done.7.refs_2_, ...), custom_call_target="tpu_custom_call" | custom-call | bytes 2097152 | tf_op jit(solution)/shard_map/pallas_call | solution.py:304
  100.4 4.4 %all-to-all-done.1 = bf16[32,4,8,128]{3,2,1,0:T(8,128)(2,1)} async-done(((bf16[32,4,8,128]{3,2,1,0:T(8,128)(2,1)}), bf16[32,4,8,128]{3,2,1,0:T(8,128)(2,1)}, u32[]{:S(2)}, u32[]{:S(2)}) %all-to-all-start.1) | async-done | bytes 262176 | tf_op jit(solution)/shard_map/all_to_all | solution.py:308
  107.9 3.6 %collective-permute-start.10 = (bf16[32,512]{1,0:T(8,128)(2,1)S(1)}, bf16[32,512]{1,0:T(8,128)(2,1)S(1)}, u32[]{:S(2)}, u32[]{:S(2)}) collective-permute-start(bf16[32,512]{1,0:T(8,128)(2,1)S(1)} %constant_dynamic-slice_fusion.3), channel_id=1, source_target_pairs={{0,0},{1,16},{2,32},{3,48},{4,64},{5,80},{6,96},{7,112},{8,128},{9... | collective-permute-start | bytes 98312 | tf_op jit(solution)/shard_map/ppermute | solution.py:269
  114.6 5.6 %collective-permute-done.10 = bf16[32,512]{1,0:T(8,128)(2,1)S(1)} collective-permute-done((bf16[32,512]{1,0:T(8,128)(2,1)S(1)}, bf16[32,512]{1,0:T(8,128)(2,1)S(1)}, u32[]{:S(2)}, u32[]{:S(2)}) %collective-permute-start.10) | collective-permute-done | bytes 32800 | tf_op jit(solution)/shard_map/ppermute | solution.py:269
  120.3 7.6 %all-to-all-start.2 = ((bf16[16,12,64,128]{3,2,1,0:T(8,128)(2,1)}), bf16[16,12,64,128]{3,2,1,0:T(8,128)(2,1)S(1)}, u32[]{:S(2)}, u32[]{:S(2)}) async-start(bf16[16,12,64,128]{3,2,1,0:T(8,128)(2,1)} %copy-done), calls=%async_computation.2 | async-start | bytes 6291456 | tf_op jit(solution)/shard_map/all_to_all | solution.py:317
  129.5 2.9 %shard_map.42 = (bf16[8,80,1024]{2,1,0:T(8,128)(2,1)S(1)}, bf16[8,80,1024]{2,1,0:T(8,128)(2,1)S(1)}) custom-call(s32[128]{0:T(128)S(1)} %bitcast.36, s32[128]{0:T(128)S(1)} %collective-permute-done.map2_ref, s32[128]{0:T(128)S(1)} %select_reduce_fusion.1.inv_ref, bf16[16,9,64,128]{3,2,1,0:T(8,128)(2,1)S(1)} %copy-done.2, ...), custom_call_target="tpu_custom_call" | custom-call | bytes 2097152 | tf_op jit(solution)/shard_map/pallas_call | solution.py:318
  134.6 2.9 %collective-permute-done.11 = bf16[8,80,1024]{2,1,0:T(8,128)(2,1)S(1)} collective-permute-done((bf16[8,80,1024]{2,1,0:T(8,128)(2,1)S(1)}, bf16[8,80,1024]{2,1,0:T(8,128)(2,1)S(1)}, u32[]{:S(2)}, u32[]{:S(2)}) %collective-permute-start.11) | collective-permute-done | bytes 1310752 | tf_op jit(solution)/shard_map/ppermute | solution.py:215
  141.5 7.5 %collective-permute-start.16 = (bf16[2,80,1024]{2,1,0:T(8,128)(2,1)S(1)}, bf16[2,80,1024]{2,1,0:T(8,128)(2,1)S(1)}, u32[]{:S(2)}, u32[]{:S(2)}) collective-permute-start(bf16[2,80,1024]{2,1,0:T(8,128)(2,1)S(1)} %pad_maximum_fusion.5), channel_id=1, source_target_pairs={{0,160},{16,112},{32,192},{48,144},{64,224},{80,176},{96,0},{112,2... | collective-permute-start | bytes 983048 | tf_op jit(solution)/shard_map/ppermute | solution.py:226
  149.0 2.8 %collective-permute-start.15 = (bf16[2,80,1024]{2,1,0:T(8,128)(2,1)S(1)}, bf16[2,80,1024]{2,1,0:T(8,128)(2,1)S(1)}, u32[]{:S(2)}, u32[]{:S(2)}) collective-permute-start(bf16[2,80,1024]{2,1,0:T(8,128)(2,1)S(1)} %pad_maximum_fusion.4), channel_id=1, source_target_pairs={{0,128},{16,144},{32,160},{48,176},{64,192},{80,208},{96,224},{112... | collective-permute-start | bytes 983048 | tf_op jit(solution)/shard_map/ppermute | solution.py:226
  151.9 5.4 %collective-permute-start.14 = (bf16[2,80,1024]{2,1,0:T(8,128)(2,1)S(1)}, bf16[2,80,1024]{2,1,0:T(8,128)(2,1)S(1)}, u32[]{:S(2)}, u32[]{:S(2)}) collective-permute-start(bf16[2,80,1024]{2,1,0:T(8,128)(2,1)S(1)} %pad_maximum_fusion.3), channel_id=1, source_target_pairs={{0,96},{16,176},{32,128},{48,208},{64,160},{80,240},{96,192},{112,... | collective-permute-start | bytes 983048 | tf_op jit(solution)/shard_map/ppermute | solution.py:226
  157.4 4.1 %collective-permute-start.13 = (bf16[2,80,1024]{2,1,0:T(8,128)(2,1)S(1)}, bf16[2,80,1024]{2,1,0:T(8,128)(2,1)S(1)}, u32[]{:S(2)}, u32[]{:S(2)}) collective-permute-start(bf16[2,80,1024]{2,1,0:T(8,128)(2,1)S(1)} %pad_maximum_fusion.2), channel_id=1, source_target_pairs={{0,64},{16,208},{32,96},{48,240},{64,128},{80,16},{96,160},{112,48... | collective-permute-start | bytes 983048 | tf_op jit(solution)/shard_map/ppermute | solution.py:226
  163.5 5.7 %collective-permute-done.16.refs_5_ = bf16[2,80,1024]{2,1,0:T(8,128)(2,1)S(1)} collective-permute-done((bf16[2,80,1024]{2,1,0:T(8,128)(2,1)S(1)}, bf16[2,80,1024]{2,1,0:T(8,128)(2,1)S(1)}, u32[]{:S(2)}, u32[]{:S(2)}) %collective-permute-start.16) | collective-permute-done | bytes 327712 | tf_op jit(solution)/shard_map/ppermute | solution.py:226
  169.9 6.2 %collective-permute-done.15.refs_4_ = bf16[2,80,1024]{2,1,0:T(8,128)(2,1)S(1)} collective-permute-done((bf16[2,80,1024]{2,1,0:T(8,128)(2,1)S(1)}, bf16[2,80,1024]{2,1,0:T(8,128)(2,1)S(1)}, u32[]{:S(2)}, u32[]{:S(2)}) %collective-permute-start.15) | collective-permute-done | bytes 327712 | tf_op jit(solution)/shard_map/ppermute | solution.py:226
  176.9 11.8 %collective-permute-done.14.refs_3_ = bf16[2,80,1024]{2,1,0:T(8,128)(2,1)S(1)} collective-permute-done((bf16[2,80,1024]{2,1,0:T(8,128)(2,1)S(1)}, bf16[2,80,1024]{2,1,0:T(8,128)(2,1)S(1)}, u32[]{:S(2)}, u32[]{:S(2)}) %collective-permute-start.14) | collective-permute-done | bytes 327712 | tf_op jit(solution)/shard_map/ppermute | solution.py:226
  189.4 7.0 %collective-permute-done.13.refs_2_ = bf16[2,80,1024]{2,1,0:T(8,128)(2,1)S(1)} collective-permute-done((bf16[2,80,1024]{2,1,0:T(8,128)(2,1)S(1)}, bf16[2,80,1024]{2,1,0:T(8,128)(2,1)S(1)}, u32[]{:S(2)}, u32[]{:S(2)}) %collective-permute-start.13) | collective-permute-done | bytes 327712 | tf_op jit(solution)/shard_map/ppermute | solution.py:226
  197.1 2.5 %collective-permute-done.12.refs_1_ = bf16[2,80,1024]{2,1,0:T(8,128)(2,1)S(1)} collective-permute-done((bf16[2,80,1024]{2,1,0:T(8,128)(2,1)S(1)}, bf16[2,80,1024]{2,1,0:T(8,128)(2,1)S(1)}, u32[]{:S(2)}, u32[]{:S(2)}) %collective-permute-start.12) | collective-permute-done | bytes 327712 | tf_op jit(solution)/shard_map/ppermute | solution.py:226
  201.1 2.9 %collective-permute-start.19 = (bf16[8,64,512]{2,1,0:T(8,128)(2,1)S(1)}, bf16[8,64,512]{2,1,0:T(8,128)(2,1)S(1)}, u32[]{:S(2)}, u32[]{:S(2)}) collective-permute-start(bf16[8,64,512]{2,1,0:T(8,128)(2,1)S(1)} %shard_map.45), channel_id=1, source_target_pairs={{0,256},{256,0},{1,257},{257,1},{2,258},{258,2},{3,259},{259,3},{4... | collective-permute-start | bytes 1572872 | tf_op jit(solution)/shard_map/ppermute | solution.py:329
  204.1 2.7 %shard_map.43.refs_9_ = bf16[1024,512]{1,0:T(8,128)(2,1)S(1)} custom-call(bf16[16,12,64,128]{3,2,1,0:T(8,128)(2,1)S(1)} %all-to-all-done.2.arrived.refs_8_, bf16[512,512]{1,0:T(8,128)(2,1)S(1)} %copy-done.6), custom_call_target="tpu_custom_call" | custom-call | flops 536870912 | bytes 2097152 | tf_op jit(solution)/shard_map/pallas_call | solution.py:330
  206.9 5.3 %shard_map.44.base = f32[8,128,512]{2,1,0:T(8,128)S(1)} custom-call(s32[128]{0:T(128)S(1)} %select_reduce_fusion.1.inv_ref, s32[128]{0:T(128)S(1)} %select_reduce_fusion.inv2_ref, bf16[2,80,1024]{2,1,0:T(8,128)(2,1)S(1)} %pad_maximum_fusion.refs_0_, bf16[2,80,1024]{2,1,0:T(8,128)(2,1)S(1)} %copy-done.20, bf16[2,80,1024]{2,1,0:T(8,128)(2,1)S(1)} %copy-done.18, ...), custom_call_target="tpu_custom_call" | custom-call | flops 805306368 | bytes 6291456 | tf_op jit(solution)/shard_map/pallas_call | solution.py:336
  212.2 6.1 %collective-permute-done.19.got_b = bf16[8,64,512]{2,1,0:T(8,128)(2,1)S(1)} collective-permute-done((bf16[8,64,512]{2,1,0:T(8,128)(2,1)S(1)}, bf16[8,64,512]{2,1,0:T(8,128)(2,1)S(1)}, u32[]{:S(2)}, u32[]{:S(2)}) %collective-permute-start.19) | collective-permute-done | bytes 524320 | tf_op jit(solution)/shard_map/ppermute | solution.py:329
  (127 shorter events, 52.1 us)
Async XLA Ops:
  7.6 8.7 %copy-start.28 = (s32[1,128]{1,0:T(1,128)S(1)}, s32[1,128]{1,0:T(1,128)}, u32[]{:S(2)}) copy-start(s32[1,128]{1,0:T(1,128)} %param.4) | copy-start | bytes 1540
  7.6 63.2 %all-to-all-start = ((bf16[16,9,64,128]{3,2,1,0:T(8,128)(2,1)}), bf16[16,9,64,128]{3,2,1,0:T(8,128)(2,1)S(1)}, u32[]{:S(2)}, u32[]{:S(2)}) async-start(bf16[16,9,64,128]{3,2,1,0:T(8,128)(2,1)} %copy-done.5), calls=%async_computation | async-start | bytes 4718592 | tf_op jit(solution)/shard_map/all_to_all | solution.py:292
  16.3 35.6 %collective-permute-start = (s32[128]{0:T(128)S(1)}, s32[128]{0:T(128)S(1)}, u32[]{:S(2)}, u32[]{:S(2)}) collective-permute-start(s32[128]{0:T(128)S(1)} %bitcast.32), channel_id=1, source_target_pairs={{0,256},{256,0},{1,257},{257,1},{2,258},{258,2},{3,259},{259,3},{4... | collective-permute-start | bytes 1544 | tf_op jit(solution)/shard_map/ppermute | solution.py:279
  23.8 4.9 %collective-permute-start.1 = (bf16[8,64,1024]{2,1,0:T(8,128)(2,1)}, bf16[8,64,1024]{2,1,0:T(8,128)(2,1)}, u32[]{:S(2)}, u32[]{:S(2)}) collective-permute-start(bf16[8,64,1024]{2,1,0:T(8,128)(2,1)} %get-tuple-element.31), channel_id=1, source_target_pairs={{0,16},{16,0},{32,48},{48,32},{64,80},{80,64},{96,112},{112,96},{1... | collective-permute-start | bytes 3145736 | tf_op jit(solution)/shard_map/ppermute | solution.py:215
  30.7 26.1 %collective-permute-start.2 = (bf16[2,64,1024]{2,1,0:T(8,128)(2,1)S(1)}, bf16[2,64,1024]{2,1,0:T(8,128)(2,1)S(1)}, u32[]{:S(2)}, u32[]{:S(2)}) collective-permute-start(bf16[2,64,1024]{2,1,0:T(8,128)(2,1)S(1)} %pad_maximum_fusion.8), channel_id=1, source_target_pairs={{0,224},{16,48},{32,0},{48,80},{64,32},{80,112},{96,64},{112,144},... | collective-permute-start | bytes 786440 | tf_op jit(solution)/shard_map/ppermute | solution.py:226
  40.8 20.5 %collective-permute-start.3 = (bf16[2,64,1024]{2,1,0:T(8,128)(2,1)S(1)}, bf16[2,64,1024]{2,1,0:T(8,128)(2,1)S(1)}, u32[]{:S(2)}, u32[]{:S(2)}) collective-permute-start(bf16[2,64,1024]{2,1,0:T(8,128)(2,1)S(1)} %pad_maximum_fusion.9), channel_id=1, source_target_pairs={{0,192},{16,80},{32,224},{48,112},{64,0},{80,144},{96,32},{112,176... | collective-permute-start | bytes 786440 | tf_op jit(solution)/shard_map/ppermute | solution.py:226
  43.7 21.9 %collective-permute-start.4 = (bf16[2,64,1024]{2,1,0:T(8,128)(2,1)S(1)}, bf16[2,64,1024]{2,1,0:T(8,128)(2,1)S(1)}, u32[]{:S(2)}, u32[]{:S(2)}) collective-permute-start(bf16[2,64,1024]{2,1,0:T(8,128)(2,1)S(1)} %pad_maximum_fusion.10), channel_id=1, source_target_pairs={{0,160},{16,112},{32,192},{48,144},{64,224},{80,176},{96,0},{112,2... | collective-permute-start | bytes 786440 | tf_op jit(solution)/shard_map/ppermute | solution.py:226
  46.4 47.6 %collective-permute-start.6 = (bf16[2,64,1024]{2,1,0:T(8,128)(2,1)}, bf16[2,64,1024]{2,1,0:T(8,128)(2,1)S(1)}, u32[]{:S(2)}, u32[]{:S(2)}) collective-permute-start(bf16[2,64,1024]{2,1,0:T(8,128)(2,1)} %pad_maximum_fusion.12), channel_id=1, source_target_pairs={{0,32},{16,240},{32,64},{48,16},{64,96},{80,48},{96,128},{112,80},... | collective-permute-start | bytes 786440 | tf_op jit(solution)/shard_map/ppermute | solution.py:226
  52.0 42.7 %collective-permute-start.7 = (bf16[2,64,1024]{2,1,0:T(8,128)(2,1)}, bf16[2,64,1024]{2,1,0:T(8,128)(2,1)}, u32[]{:S(2)}, u32[]{:S(2)}) collective-permute-start(bf16[2,64,1024]{2,1,0:T(8,128)(2,1)} %pad_maximum_fusion.13), channel_id=1, source_target_pairs={{0,64},{16,208},{32,96},{48,240},{64,128},{80,16},{96,160},{112,48... | collective-permute-start | bytes 786440 | tf_op jit(solution)/shard_map/ppermute | solution.py:226
  56.8 37.9 %collective-permute-start.8 = (bf16[2,64,1024]{2,1,0:T(8,128)(2,1)}, bf16[2,64,1024]{2,1,0:T(8,128)(2,1)}, u32[]{:S(2)}, u32[]{:S(2)}) collective-permute-start(bf16[2,64,1024]{2,1,0:T(8,128)(2,1)} %pad_maximum_fusion.14), channel_id=1, source_target_pairs={{0,96},{16,176},{32,128},{48,208},{64,160},{80,240},{96,192},{112,... | collective-permute-start | bytes 786440 | tf_op jit(solution)/shard_map/ppermute | solution.py:226
  61.4 18.2 %copy-start.21 = (bf16[2,64,1024]{2,1,0:T(8,128)(2,1)}, bf16[2,64,1024]{2,1,0:T(8,128)(2,1)S(1)}, u32[]{:S(2)}) copy-start(bf16[2,64,1024]{2,1,0:T(8,128)(2,1)S(1)} %collective-permute-done.3.refs_6_) | copy-start | bytes 786436
  61.4 33.3 %collective-permute-start.9 = (bf16[2,64,1024]{2,1,0:T(8,128)(2,1)}, bf16[2,64,1024]{2,1,0:T(8,128)(2,1)}, u32[]{:S(2)}, u32[]{:S(2)}) collective-permute-start(bf16[2,64,1024]{2,1,0:T(8,128)(2,1)} %pad_maximum_fusion.15), channel_id=1, source_target_pairs={{0,128},{16,144},{32,160},{48,176},{64,192},{80,208},{96,224},{112... | collective-permute-start | bytes 786440 | tf_op jit(solution)/shard_map/ppermute | solution.py:226
  65.7 13.9 %copy-start.23 = (bf16[2,64,1024]{2,1,0:T(8,128)(2,1)}, bf16[2,64,1024]{2,1,0:T(8,128)(2,1)S(1)}, u32[]{:S(2)}) copy-start(bf16[2,64,1024]{2,1,0:T(8,128)(2,1)S(1)} %collective-permute-done.4.refs_5_) | copy-start | bytes 786436
  70.8 8.8 %copy-start.1 = (bf16[16,9,64,128]{3,2,1,0:T(8,128)(2,1)}, bf16[16,9,64,128]{3,2,1,0:T(8,128)(2,1)S(1)}, u32[]{:S(2)}) copy-start(bf16[16,9,64,128]{3,2,1,0:T(8,128)(2,1)S(1)} %all-to-all-done.arrived) | copy-start | bytes 7077892
  76.1 28.7 %collective-permute-start.5 = (bf16[8,64,512]{2,1,0:T(8,128)(2,1)}, bf16[8,64,512]{2,1,0:T(8,128)(2,1)}, u32[]{:S(2)}, u32[]{:S(2)}) collective-permute-start(bf16[8,64,512]{2,1,0:T(8,128)(2,1)} %shard_map.39), channel_id=1, source_target_pairs={{0,256},{256,0},{1,257},{257,1},{2,258},{258,2},{3,259},{259,3},{4... | collective-permute-start | bytes 1572872 | tf_op jit(solution)/shard_map/ppermute | solution.py:303
  79.6 25.2 %all-to-all-start.1 = ((bf16[32,4,8,128]{3,2,1,0:T(8,128)(2,1)}), bf16[32,4,8,128]{3,2,1,0:T(8,128)(2,1)}, u32[]{:S(2)}, u32[]{:S(2)}) async-start(bf16[32,4,8,128]{3,2,1,0:T(8,128)(2,1)} %gather_fusion.1), calls=%async_computation.1 | async-start | bytes 524288 | tf_op jit(solution)/shard_map/all_to_all | solution.py:308
  107.9 12.3 %collective-permute-start.10 = (bf16[32,512]{1,0:T(8,128)(2,1)S(1)}, bf16[32,512]{1,0:T(8,128)(2,1)S(1)}, u32[]{:S(2)}, u32[]{:S(2)}) collective-permute-start(bf16[32,512]{1,0:T(8,128)(2,1)S(1)} %constant_dynamic-slice_fusion.3), channel_id=1, source_target_pairs={{0,0},{1,16},{2,32},{3,48},{4,64},{5,80},{6,96},{7,112},{8,128},{9... | collective-permute-start | bytes 98312 | tf_op jit(solution)/shard_map/ppermute | solution.py:269
  120.3 80.1 %all-to-all-start.2 = ((bf16[16,12,64,128]{3,2,1,0:T(8,128)(2,1)}), bf16[16,12,64,128]{3,2,1,0:T(8,128)(2,1)S(1)}, u32[]{:S(2)}, u32[]{:S(2)}) async-start(bf16[16,12,64,128]{3,2,1,0:T(8,128)(2,1)} %copy-done), calls=%async_computation.2 | async-start | bytes 6291456 | tf_op jit(solution)/shard_map/all_to_all | solution.py:317
  132.5 4.9 %collective-permute-start.11 = (bf16[8,80,1024]{2,1,0:T(8,128)(2,1)S(1)}, bf16[8,80,1024]{2,1,0:T(8,128)(2,1)S(1)}, u32[]{:S(2)}, u32[]{:S(2)}) collective-permute-start(bf16[8,80,1024]{2,1,0:T(8,128)(2,1)S(1)} %get-tuple-element.45), channel_id=1, source_target_pairs={{0,16},{16,0},{32,48},{48,32},{64,80},{80,64},{96,112},{112,96},{1... | collective-permute-start | bytes 3932168 | tf_op jit(solution)/shard_map/ppermute | solution.py:215
  137.6 19.8 %collective-permute-start.18 = (bf16[2,80,1024]{2,1,0:T(8,128)(2,1)S(1)}, bf16[2,80,1024]{2,1,0:T(8,128)(2,1)S(1)}, u32[]{:S(2)}, u32[]{:S(2)}) collective-permute-start(bf16[2,80,1024]{2,1,0:T(8,128)(2,1)S(1)} %pad_maximum_fusion.7), channel_id=1, source_target_pairs={{0,224},{16,48},{32,0},{48,80},{64,32},{80,112},{96,64},{112,144},... | collective-permute-start | bytes 983048 | tf_op jit(solution)/shard_map/ppermute | solution.py:226
  139.5 22.0 %collective-permute-start.17 = (bf16[2,80,1024]{2,1,0:T(8,128)(2,1)S(1)}, bf16[2,80,1024]{2,1,0:T(8,128)(2,1)S(1)}, u32[]{:S(2)}, u32[]{:S(2)}) collective-permute-start(bf16[2,80,1024]{2,1,0:T(8,128)(2,1)S(1)} %pad_maximum_fusion.6), channel_id=1, source_target_pairs={{0,192},{16,80},{32,224},{48,112},{64,0},{80,144},{96,32},{112,176... | collective-permute-start | bytes 983048 | tf_op jit(solution)/shard_map/ppermute | solution.py:226
  141.5 27.7 %collective-permute-start.16 = (bf16[2,80,1024]{2,1,0:T(8,128)(2,1)S(1)}, bf16[2,80,1024]{2,1,0:T(8,128)(2,1)S(1)}, u32[]{:S(2)}, u32[]{:S(2)}) collective-permute-start(bf16[2,80,1024]{2,1,0:T(8,128)(2,1)S(1)} %pad_maximum_fusion.5), channel_id=1, source_target_pairs={{0,160},{16,112},{32,192},{48,144},{64,224},{80,176},{96,0},{112,2... | collective-permute-start | bytes 983048 | tf_op jit(solution)/shard_map/ppermute | solution.py:226
  149.0 27.1 %collective-permute-start.15 = (bf16[2,80,1024]{2,1,0:T(8,128)(2,1)S(1)}, bf16[2,80,1024]{2,1,0:T(8,128)(2,1)S(1)}, u32[]{:S(2)}, u32[]{:S(2)}) collective-permute-start(bf16[2,80,1024]{2,1,0:T(8,128)(2,1)S(1)} %pad_maximum_fusion.4), channel_id=1, source_target_pairs={{0,128},{16,144},{32,160},{48,176},{64,192},{80,208},{96,224},{112... | collective-permute-start | bytes 983048 | tf_op jit(solution)/shard_map/ppermute | solution.py:226
  151.9 36.7 %collective-permute-start.14 = (bf16[2,80,1024]{2,1,0:T(8,128)(2,1)S(1)}, bf16[2,80,1024]{2,1,0:T(8,128)(2,1)S(1)}, u32[]{:S(2)}, u32[]{:S(2)}) collective-permute-start(bf16[2,80,1024]{2,1,0:T(8,128)(2,1)S(1)} %pad_maximum_fusion.3), channel_id=1, source_target_pairs={{0,96},{16,176},{32,128},{48,208},{64,160},{80,240},{96,192},{112,... | collective-permute-start | bytes 983048 | tf_op jit(solution)/shard_map/ppermute | solution.py:226
  157.4 39.0 %copy-start.7 = (bf16[2,80,1024]{2,1,0:T(8,128)(2,1)}, bf16[2,80,1024]{2,1,0:T(8,128)(2,1)S(1)}, u32[]{:S(2)}) copy-start(bf16[2,80,1024]{2,1,0:T(8,128)(2,1)S(1)} %collective-permute-done.18.refs_7_) | copy-start | bytes 983044
  157.4 39.0 %collective-permute-start.13 = (bf16[2,80,1024]{2,1,0:T(8,128)(2,1)S(1)}, bf16[2,80,1024]{2,1,0:T(8,128)(2,1)S(1)}, u32[]{:S(2)}, u32[]{:S(2)}) collective-permute-start(bf16[2,80,1024]{2,1,0:T(8,128)(2,1)S(1)} %pad_maximum_fusion.2), channel_id=1, source_target_pairs={{0,64},{16,208},{32,96},{48,240},{64,128},{80,16},{96,160},{112,48... | collective-permute-start | bytes 983048 | tf_op jit(solution)/shard_map/ppermute | solution.py:226
  161.5 34.9 %copy-start.9 = (bf16[2,80,1024]{2,1,0:T(8,128)(2,1)}, bf16[2,80,1024]{2,1,0:T(8,128)(2,1)S(1)}, u32[]{:S(2)}) copy-start(bf16[2,80,1024]{2,1,0:T(8,128)(2,1)S(1)} %collective-permute-done.17.refs_6_) | copy-start | bytes 983044
  161.5 38.1 %collective-permute-start.12 = (bf16[2,80,1024]{2,1,0:T(8,128)(2,1)S(1)}, bf16[2,80,1024]{2,1,0:T(8,128)(2,1)S(1)}, u32[]{:S(2)}, u32[]{:S(2)}) collective-permute-start(bf16[2,80,1024]{2,1,0:T(8,128)(2,1)S(1)} %pad_maximum_fusion.1), channel_id=1, source_target_pairs={{0,32},{16,240},{32,64},{48,16},{64,96},{80,48},{96,128},{112,80},... | collective-permute-start | bytes 983048 | tf_op jit(solution)/shard_map/ppermute | solution.py:226
  201.1 5.7 %copy-start.8 = (bf16[2,80,1024]{2,1,0:T(8,128)(2,1)S(1)}, bf16[2,80,1024]{2,1,0:T(8,128)(2,1)}, u32[]{:S(2)}) copy-start(bf16[2,80,1024]{2,1,0:T(8,128)(2,1)} %copy-done.7) | copy-start | bytes 983044
  201.1 5.7 %copy-start.10 = (bf16[2,80,1024]{2,1,0:T(8,128)(2,1)S(1)}, bf16[2,80,1024]{2,1,0:T(8,128)(2,1)}, u32[]{:S(2)}) copy-start(bf16[2,80,1024]{2,1,0:T(8,128)(2,1)} %copy-done.9) | copy-start | bytes 983044
  201.1 5.7 %copy-start.12 = (bf16[2,80,1024]{2,1,0:T(8,128)(2,1)S(1)}, bf16[2,80,1024]{2,1,0:T(8,128)(2,1)}, u32[]{:S(2)}) copy-start(bf16[2,80,1024]{2,1,0:T(8,128)(2,1)} %copy-done.11) | copy-start | bytes 983044
  201.1 17.1 %collective-permute-start.19 = (bf16[8,64,512]{2,1,0:T(8,128)(2,1)S(1)}, bf16[8,64,512]{2,1,0:T(8,128)(2,1)S(1)}, u32[]{:S(2)}, u32[]{:S(2)}) collective-permute-start(bf16[8,64,512]{2,1,0:T(8,128)(2,1)S(1)} %shard_map.45), channel_id=1, source_target_pairs={{0,256},{256,0},{1,257},{257,1},{2,258},{258,2},{3,259},{259,3},{4... | collective-permute-start | bytes 1572872 | tf_op jit(solution)/shard_map/ppermute | solution.py:329
  (20 other events, 42.4 us)

commit v4 on v3

--- a/solution.py
+++ b/solution.py
@@ -80,7 +80,7 @@
     pltpu.make_async_copy(own, own, sem).wait()
 
 
-def cols_to_rows(map_ref, map2_ref, inv_ref, arrived, taken, tail, own, swap, sem, sem_t):
+def cols_to_rows(map_ref, map2_ref, inv_ref, arrived, taken, own, swap, sem):
     sib = lax.axis_index("sib")
 
     @pl.loop(0, W)
@@ -92,19 +92,13 @@
             def _():
                 for j in range(W // 2):
                     pltpu.make_async_copy(
-                        arrived.at[col_landing(inv_ref, sib, j), q],
-                        ob.at[k, pl.ds(0, HA), pl.ds(j * B, B)], sem
+                        arrived.at[col_landing(inv_ref, sib, j), q], ob.at[k, :, pl.ds(j * B, B)], sem
                     ).start()
 
             @pl.when(e2 == side)
             def _():
-                pltpu.make_async_copy(taken.at[q], ob.at[k2, pl.ds(0, HA), pl.ds(PANEL, PANEL)], sem).start()
-            pltpu.make_async_copy(tail, ob.at[q, pl.ds(HA, TAIL), :], sem_t).start()
-    done = own.at[:, pl.ds(0, HA), :]
-    pltpu.make_async_copy(done, done, sem).wait()
-    for ob in (own, swap):
-        done = ob.at[:, pl.ds(HA, TAIL), :]
-        pltpu.make_async_copy(done, done, sem_t).wait()
+                pltpu.make_async_copy(taken.at[q], ob.at[k2, :, pl.ds(PANEL, PANEL)], sem).start()
+    pltpu.make_async_copy(own, own, sem).wait()
 
 
 def rows_to_cols(map_ref, inv_ref, *refs):
@@ -249,11 +243,11 @@
 
 def panel_piece(got, inv, inv2):
     sib, row = lax.axis_index("sib"), lax.axis_index("row")
-    parts = [
-        jnp.take(got, child * G + lax.dynamic_slice_in_dim(ref, row * W, W, 0) // W, axis=0, mode="clip").astype(jnp.float32)
-        for child, ref in ((sib, inv), (1 - sib, inv2))
+    slots = [
+        child * G + lax.dynamic_slice_in_dim(ref, row * W, W, 0) // W for child, ref in ((sib, inv), (1 - sib, inv2))
     ]
-    return (parts[0] + parts[1]).astype(jnp.bfloat16)
+    parts = jnp.take(got, jnp.concatenate(slots), axis=0, mode="clip").astype(jnp.float32)
+    return (parts[:W] + parts[W:]).astype(jnp.bfloat16)
 
 
 def tail_piece(piece):
@@ -276,11 +270,10 @@
     dma = pltpu.SemaphoreType.DMA
     MiB = 1 << 20
     exchange = [(0, 1), (1, 0)]
-    maps2 = lax.ppermute(maps, "sib", exchange)
     inv = inverse_of(maps)
     blocks = tile.reshape(W, B, W * B)
 
-    rows_a, rows_b = bf16(8, HA + TAIL, W * B), bf16(8, HB, W * B)
+    rows_a, rows_b = bf16(8, HA, W * B), bf16(8, HB, W * B)
     send_a = pl.pallas_call(
         pack_cols, out_shape=bf16(G, W + 1, HA, B), in_specs=[SMEM, ANY, ANY], out_specs=ANY,
         scratch_shapes=[dma, dma], **params(moved=2 * MiB),
@@ -290,7 +283,9 @@
         **params(moved=2 * MiB),
     )(maps, blocks)
     got_a = lax.all_to_all(send_a, "col", 0, 0, tiled=True)
-    got_b = z_ring(pairs_of(own, core_exchange(swap)))
+    other, maps_later = lax.optimization_barrier((core_exchange(swap), maps))
+    maps2 = lax.ppermute(maps_later, "sib", exchange)
+    got_b = z_ring(pairs_of(own, other))
     got_a, maps2, got_b[7], got_b[6], got_b[5] = lax.optimization_barrier(
         (got_a, maps2, got_b[7], got_b[6], got_b[5]))
 
@@ -306,20 +301,22 @@
         scratch_shapes=[dma], **params(moved=2 * MiB),
     )(maps, inv, *got_b)
     pieces = lax.all_to_all(pieces, ("sib", "row"), 0, 0, tiled=True)
-    pieces, taken_a, send_b = lax.optimization_barrier((pieces, taken_a, send_b))
+    own, swap = pl.pallas_call(
+        cols_to_rows, out_shape=(rows_a, rows_a), in_specs=[SMEM] * 3 + [ANY] * 2, out_specs=(ANY, ANY),
+        scratch_shapes=[dma], **params(moved=2 * MiB),
+    )(maps, maps2, inv, got_a, taken_a)
+    pieces, send_b = lax.optimization_barrier((pieces, send_b))
     piece = panel_piece(pieces, inv, inv2)
     tail = tail_piece(piece)
     send_b = pl.pallas_call(
         add_piece, out_shape=bf16(G, W + 4, HB, B), in_specs=[ANY, ANY], out_specs=ANY, scratch_shapes=[dma],
         input_output_aliases={1: 0}, **params(moved=MiB),
     )(jnp.transpose(piece, (1, 0, 2, 3)).reshape(4, W * 8, B), send_b)
-    send_b, tail = lax.optimization_barrier((send_b, tail))
+    send_b, tail, own, swap = lax.optimization_barrier((send_b, tail, own, swap))
     got_b = lax.all_to_all(send_b, "col", 0, 0, tiled=True)
-    own, swap = pl.pallas_call(
-        cols_to_rows, out_shape=(rows_a, rows_a), in_specs=[SMEM] * 3 + [ANY] * 3, out_specs=(ANY, ANY),
-        scratch_shapes=[dma, dma], **params(moved=2 * MiB),
-    )(maps, maps2, inv, got_a, taken_a, tail)
-    got_a = z_ring(pairs_of(own, core_exchange(swap)))
+    other = core_exchange(swap)
+    tails = jnp.stack([tail, core_exchange(tail)])
+    got_a = z_ring([jnp.concatenate([both, tails], axis=1) for both in pairs_of(own, other)])
     got_b, got_a = lax.optimization_barrier((got_b, got_a))
 
     hand_b = pl.pallas_call(

time: 221 us -> 219 us (level)
  waiting for transfers between devices: 59.2 us -> 47.1 us
  starting transfers between devices: 105 us -> 111 us
    ppermute x1, waiting for transfers between devices: 5.64 us -> 0.72 us  [tail_piece(): got = lax.ppermute(send, ('sib', 'row', 'col'), pairs)]
    all_to_all x1, starting transfers between devices: 7.63 us -> 12.3 us  [shards(): got_b = lax.all_to_all(send_b, 'col', 0, 0, tiled=True)]
    all_to_all x1, waiting for transfers between devices: 4.45 us -> 0.46 us  [shards(): pieces = lax.all_to_all(pieces, ('sib', 'row'), 0, 0, tiled=True)]
    ppermute x2 -> x3, waiting for transfers between devices: 4.66 us -> 1.8 us  [core_exchange(): return lax.ppermute(swap, 'row', [(i, i ^ 1) for i in range(G)])]
    all_to_all x1, waiting for transfers between devices: 0.01 us -> 2.43 us  [shards(): got_b = lax.all_to_all(send_b, 'col', 0, 0, tiled=True)]
    ppermute x2 -> x3, starting transfers between devices: 3.84 us -> 6.24 us  [core_exchange(): return lax.ppermute(swap, 'row', [(i, i ^ 1) for i in range(G)])]
    unnamed x58 -> x62, local copies, waits for them, and re-layouts: 15.8 us -> 17.5 us
  transfers between devices with their start and end apart: 23 -> 24, of which waited for: 11 -> 9; matrix products, arithmetic and copies ran while one was open for 5% -> 7% of each run, Pallas kernels for 8% -> 8%
where the time goes in v4:
time: 219 us; the launch traced here: 217 us
  starting transfers between devices  111 us (51%)
  waiting for transfers between devices  47.1 us (22%)
  local copies, waits for them, and re-layouts  28.8 us (13%)
  Pallas kernels  21.5 us (10%)
  other arithmetic  7.22 us (3%)
    ppermute x14, starting transfers between devices, z_ring(): arrived[k] = lax.ppermute(both[k], 'row', pairs)  56.8 us
    ppermute x14, waiting for transfers between devices, z_ring(): arrived[k] = lax.ppermute(both[k], 'row', pairs)  31.7 us
    unnamed x62, local copies, waits for them, and re-layouts  17.5 us
    all_to_all x1, starting transfers between devices, shards(): pieces = lax.all_to_all(pieces, ('sib', 'row'), 0, 0, tiled=True)  13.5 us
    all_to_all x1, starting transfers between devices, shards(): got_b = lax.all_to_all(send_b, 'col', 0, 0, tiled=True)  12.3 us
    all_to_all x1, starting transfers between devices, shards(): got_a = lax.all_to_all(send_a, 'col', 0, 0, tiled=True)  8.71 us
    ppermute x3, starting transfers between devices, core_exchange(): return lax.ppermute(swap, 'row', [(i, i ^ 1) for i in range(G)])  6.24 us
    pallas_call x1, Pallas kernels, shards(): pl.pallas_call(keep, out_shape=full, in_specs=[SMEM] * 2 + [ANY] * 9 + [V...  5.3 us
  transfers between devices with their start and end apart: 24, of which 9 were waited for; matrix products, arithmetic and copies ran while one was open for 7% of the time, Pallas kernels for 8%

profile of v4, /device:TPU:6, one launch (start us, length us, event | category | flops | bytes accessed | tf_op | source)
XLA Modules:
  0.0 216.9 jit_solution(3914418535806797650)
XLA Ops:
  7.6 8.7 %all-to-all-start = ((bf16[16,9,64,128]{3,2,1,0:T(8,128)(2,1)}), bf16[16,9,64,128]{3,2,1,0:T(8,128)(2,1)S(1)}, u32[]{:S(2)}, u32[]{:S(2)}) async-start(bf16[16,9,64,128]{3,2,1,0:T(8,128)(2,1)} %copy-done.5), calls=%async_computation | async-start | bytes 4718592 | tf_op jit(solution)/shard_map/all_to_all | solution.py:285
  17.9 2.1 shard_map.38
  20.0 1.9 collective-permute-start
  24.9 2.0 fusion.16
  26.9 10.9 %collective-permute-start.2 = (bf16[2,64,1024]{2,1,0:T(8,128)(2,1)S(1)}, bf16[2,64,1024]{2,1,0:T(8,128)(2,1)S(1)}, u32[]{:S(2)}, u32[]{:S(2)}) collective-permute-start(bf16[2,64,1024]{2,1,0:T(8,128)(2,1)S(1)} %pad_maximum_fusion.1), channel_id=1, source_target_pairs={{0,224},{16,48},{32,0},{48,80},{64,32},{80,112},{96,64},{112,144},... | collective-permute-start | bytes 786440 | tf_op jit(solution)/shard_map/ppermute | solution.py:220
  37.9 2.0 collective-permute-start.3
  39.9 2.4 %collective-permute-start.4 = (bf16[2,64,1024]{2,1,0:T(8,128)(2,1)S(1)}, bf16[2,64,1024]{2,1,0:T(8,128)(2,1)S(1)}, u32[]{:S(2)}, u32[]{:S(2)}) collective-permute-start(bf16[2,64,1024]{2,1,0:T(8,128)(2,1)S(1)} %pad_maximum_fusion.3), channel_id=1, source_target_pairs={{0,160},{16,112},{32,192},{48,144},{64,224},{80,176},{96,0},{112,2... | collective-permute-start | bytes 786440 | tf_op jit(solution)/shard_map/ppermute | solution.py:220
  42.4 3.3 %collective-permute-start.1 = (s32[128]{0:T(128)S(1)}, s32[128]{0:T(128)S(1)}, u32[]{:S(2)}, u32[]{:S(2)}) collective-permute-start(s32[128]{0:T(128)S(1)} %bitcast.35), channel_id=1, source_target_pairs={{0,256},{256,0},{1,257},{257,1},{2,258},{258,2},{3,259},{259,3},{4... | collective-permute-start | bytes 1544 | tf_op jit(solution)/shard_map/ppermute | solution.py:287
  46.4 3.4 %collective-permute-start.5 = (bf16[2,64,1024]{2,1,0:T(8,128)(2,1)}, bf16[2,64,1024]{2,1,0:T(8,128)(2,1)S(1)}, u32[]{:S(2)}, u32[]{:S(2)}) collective-permute-start(bf16[2,64,1024]{2,1,0:T(8,128)(2,1)} %pad_maximum_fusion.5), channel_id=1, source_target_pairs={{0,32},{16,240},{32,64},{48,16},{64,96},{80,48},{96,128},{112,80},... | collective-permute-start | bytes 786440 | tf_op jit(solution)/shard_map/ppermute | solution.py:220
  51.9 4.8 %collective-permute-start.6 = (bf16[2,64,1024]{2,1,0:T(8,128)(2,1)}, bf16[2,64,1024]{2,1,0:T(8,128)(2,1)}, u32[]{:S(2)}, u32[]{:S(2)}) collective-permute-start(bf16[2,64,1024]{2,1,0:T(8,128)(2,1)} %pad_maximum_fusion.6), channel_id=1, source_target_pairs={{0,64},{16,208},{32,96},{48,240},{64,128},{80,16},{96,160},{112,48... | collective-permute-start | bytes 786440 | tf_op jit(solution)/shard_map/ppermute | solution.py:220
  56.8 4.8 %collective-permute-start.7 = (bf16[2,64,1024]{2,1,0:T(8,128)(2,1)}, bf16[2,64,1024]{2,1,0:T(8,128)(2,1)}, u32[]{:S(2)}, u32[]{:S(2)}) collective-permute-start(bf16[2,64,1024]{2,1,0:T(8,128)(2,1)} %pad_maximum_fusion.7), channel_id=1, source_target_pairs={{0,96},{16,176},{32,128},{48,208},{64,160},{80,240},{96,192},{112,... | collective-permute-start | bytes 786440 | tf_op jit(solution)/shard_map/ppermute | solution.py:220
  61.6 3.9 %collective-permute-start.8 = (bf16[2,64,1024]{2,1,0:T(8,128)(2,1)}, bf16[2,64,1024]{2,1,0:T(8,128)(2,1)}, u32[]{:S(2)}, u32[]{:S(2)}) collective-permute-start(bf16[2,64,1024]{2,1,0:T(8,128)(2,1)} %pad_maximum_fusion.8), channel_id=1, source_target_pairs={{0,128},{16,144},{32,160},{48,176},{64,192},{80,208},{96,224},{112... | collective-permute-start | bytes 786440 | tf_op jit(solution)/shard_map/ppermute | solution.py:220
  65.5 5.3 %all-to-all-done.arrived = bf16[16,9,64,128]{3,2,1,0:T(8,128)(2,1)S(1)} async-done(((bf16[16,9,64,128]{3,2,1,0:T(8,128)(2,1)}), bf16[16,9,64,128]{3,2,1,0:T(8,128)(2,1)S(1)}, u32[]{:S(2)}, u32[]{:S(2)}) %all-to-all-start) | async-done | bytes 2359328 | tf_op jit(solution)/shard_map/all_to_all | solution.py:285
  74.5 13.5 %all-to-all-start.1 = ((bf16[32,4,8,128]{3,2,1,0:T(8,128)(2,1)}), bf16[32,4,8,128]{3,2,1,0:T(8,128)(2,1)}, u32[]{:S(2)}, u32[]{:S(2)}) async-start(bf16[32,4,8,128]{3,2,1,0:T(8,128)(2,1)} %gather_fusion.1), calls=%async_computation.1 | async-start | bytes 524288 | tf_op jit(solution)/shard_map/all_to_all | solution.py:303
  90.6 2.2 %collective-permute-start.10 = (bf16[8,64,512]{2,1,0:T(8,128)(2,1)}, bf16[8,64,512]{2,1,0:T(8,128)(2,1)}, u32[]{:S(2)}, u32[]{:S(2)}) collective-permute-start(bf16[8,64,512]{2,1,0:T(8,128)(2,1)} %shard_map.41), channel_id=1, source_target_pairs={{0,256},{256,0},{1,257},{257,1},{2,258},{258,2},{3,259},{259,3},{4... | collective-permute-start | bytes 1572872 | tf_op jit(solution)/shard_map/ppermute | solution.py:298
  96.4 2.9 %shard_map.39.a = bf16[16,12,64,128]{3,2,1,0:T(8,128)(2,1)S(1)} custom-call(s32[128]{0:T(128)S(1)} %bitcast.36, s32[128]{0:T(128)S(1)} %select_reduce_fusion.1.inv_ref, bf16[2,64,1024]{2,1,0:T(8,128)(2,1)S(1)} %pad_maximum_fusion.4.refs_0_, bf16[2,64,1024]{2,1,0:T(8,128)(2,1)S(1)} %copy-done.27, bf16[2,64,1024]{2,1,0:T(8,128)(2,1)} %collective-permute-done.6.refs_2_, ...), custom_call_target="tpu_custom_call" | custom-call | bytes 2097152 | tf_op jit(solution)/shard_map/pallas_call | solution.py:299
  100.0 2.2 gather_fusion.2
  103.2 3.7 %collective-permute-start.9 = (bf16[32,512]{1,0:T(8,128)(2,1)S(1)}, bf16[32,512]{1,0:T(8,128)(2,1)S(1)}, u32[]{:S(2)}, u32[]{:S(2)}) collective-permute-start(bf16[32,512]{1,0:T(8,128)(2,1)S(1)} %constant_dynamic-slice_fusion), channel_id=1, source_target_pairs={{0,0},{1,16},{2,32},{3,48},{4,64},{5,80},{6,96},{7,112},{8,128},{9... | collective-permute-start | bytes 98312 | tf_op jit(solution)/shard_map/ppermute | solution.py:263
  110.0 2.3 %shard_map.42 = (bf16[8,64,1024]{2,1,0:T(8,128)(2,1)S(1)}, bf16[8,64,1024]{2,1,0:T(8,128)(2,1)S(1)}) custom-call(s32[128]{0:T(128)S(1)} %bitcast.37, s32[128]{0:T(128)S(1)} %collective-permute-done.1.map2_ref, s32[128]{0:T(128)S(1)} %select_reduce_fusion.1.inv_ref, bf16[16,9,64,128]{3,2,1,0:T(8,128)(2,1)S(1)} %copy-done.2, ...), custom_call_target="tpu_custom_call" | custom-call | bytes 2097152 | tf_op jit(solution)/shard_map/pallas_call | solution.py:304
  115.0 12.3 %all-to-all-start.2 = ((bf16[16,12,64,128]{3,2,1,0:T(8,128)(2,1)}), bf16[16,12,64,128]{3,2,1,0:T(8,128)(2,1)S(1)}, u32[]{:S(2)}, u32[]{:S(2)}) async-start(bf16[16,12,64,128]{3,2,1,0:T(8,128)(2,1)} %copy-done), calls=%async_computation.2 | async-start | bytes 6291456 | tf_op jit(solution)/shard_map/all_to_all | solution.py:316
  129.2 2.4 %collective-permute-start.12 = (bf16[16,1024]{1,0:T(8,128)(2,1)S(1)}, bf16[16,1024]{1,0:T(8,128)(2,1)S(1)}, u32[]{:S(2)}, u32[]{:S(2)}) collective-permute-start(bf16[16,1024]{1,0:T(8,128)(2,1)S(1)} %pad_maximum_fusion.9), channel_id=1, source_target_pairs={{0,16},{16,0},{32,48},{48,32},{64,80},{80,64},{96,112},{112,96},{1... | collective-permute-start | bytes 98312 | tf_op jit(solution)/shard_map/ppermute | solution.py:209
  133.2 2.5 %collective-permute-start.13 = (bf16[2,80,1024]{2,1,0:T(8,128)(2,1)S(1)}, bf16[2,80,1024]{2,1,0:T(8,128)(2,1)S(1)}, u32[]{:S(2)}, u32[]{:S(2)}) collective-permute-start(bf16[2,80,1024]{2,1,0:T(8,128)(2,1)S(1)} %get-tuple-element.94), channel_id=1, source_target_pairs={{0,32},{16,240},{32,64},{48,16},{64,96},{80,48},{96,128},{112,80},... | collective-permute-start | bytes 983048 | tf_op jit(solution)/shard_map/ppermute | solution.py:220
  139.6 4.6 %collective-permute-start.19 = (bf16[2,80,1024]{2,1,0:T(8,128)(2,1)S(1)}, bf16[2,80,1024]{2,1,0:T(8,128)(2,1)S(1)}, u32[]{:S(2)}, u32[]{:S(2)}) collective-permute-start(bf16[2,80,1024]{2,1,0:T(8,128)(2,1)S(1)} %get-tuple-element.93), channel_id=1, source_target_pairs={{0,224},{16,48},{32,0},{48,80},{64,32},{80,112},{96,64},{112,144},... | collective-permute-start | bytes 983048 | tf_op jit(solution)/shard_map/ppermute | solution.py:220
  144.4 8.4 %collective-permute-start.16 = (bf16[2,80,1024]{2,1,0:T(8,128)(2,1)S(1)}, bf16[2,80,1024]{2,1,0:T(8,128)(2,1)S(1)}, u32[]{:S(2)}, u32[]{:S(2)}) collective-permute-start(bf16[2,80,1024]{2,1,0:T(8,128)(2,1)S(1)} %get-tuple-element.98), channel_id=1, source_target_pairs={{0,128},{16,144},{32,160},{48,176},{64,192},{80,208},{96,224},{112... | collective-permute-start | bytes 983048 | tf_op jit(solution)/shard_map/ppermute | solution.py:220
  156.1 3.4 %collective-permute-start.18 = (bf16[2,80,1024]{2,1,0:T(8,128)(2,1)S(1)}, bf16[2,80,1024]{2,1,0:T(8,128)(2,1)S(1)}, u32[]{:S(2)}, u32[]{:S(2)}) collective-permute-start(bf16[2,80,1024]{2,1,0:T(8,128)(2,1)S(1)} %get-tuple-element.97), channel_id=1, source_target_pairs={{0,192},{16,80},{32,224},{48,112},{64,0},{80,144},{96,32},{112,176... | collective-permute-start | bytes 983048 | tf_op jit(solution)/shard_map/ppermute | solution.py:220
  159.5 24.4 %collective-permute-done.15.refs_3_ = bf16[2,80,1024]{2,1,0:T(8,128)(2,1)S(1)} collective-permute-done((bf16[2,80,1024]{2,1,0:T(8,128)(2,1)S(1)}, bf16[2,80,1024]{2,1,0:T(8,128)(2,1)S(1)}, u32[]{:S(2)}, u32[]{:S(2)}) %collective-permute-start.15) | collective-permute-done | bytes 327712 | tf_op jit(solution)/shard_map/ppermute | solution.py:220
  188.2 5.9 %collective-permute-done.18.refs_6_ = bf16[2,80,1024]{2,1,0:T(8,128)(2,1)S(1)} collective-permute-done((bf16[2,80,1024]{2,1,0:T(8,128)(2,1)S(1)}, bf16[2,80,1024]{2,1,0:T(8,128)(2,1)S(1)}, u32[]{:S(2)}, u32[]{:S(2)}) %collective-permute-start.18) | collective-permute-done | bytes 327712 | tf_op jit(solution)/shard_map/ppermute | solution.py:220
  194.8 2.4 %all-to-all-done.2.arrived.refs_8_ = bf16[16,12,64,128]{3,2,1,0:T(8,128)(2,1)S(1)} async-done(((bf16[16,12,64,128]{3,2,1,0:T(8,128)(2,1)}), bf16[16,12,64,128]{3,2,1,0:T(8,128)(2,1)S(1)}, u32[]{:S(2)}, u32[]{:S(2)}) %all-to-all-start.2) | async-done | bytes 3145760 | tf_op jit(solution)/shard_map/all_to_all | solution.py:316
  198.0 4.2 %collective-permute-start.20 = (bf16[8,64,512]{2,1,0:T(8,128)(2,1)S(1)}, bf16[8,64,512]{2,1,0:T(8,128)(2,1)S(1)}, u32[]{:S(2)}, u32[]{:S(2)}) collective-permute-start(bf16[8,64,512]{2,1,0:T(8,128)(2,1)S(1)} %shard_map.45), channel_id=1, source_target_pairs={{0,256},{256,0},{1,257},{257,1},{2,258},{258,2},{3,259},{259,3},{4... | collective-permute-start | bytes 1572872 | tf_op jit(solution)/shard_map/ppermute | solution.py:326
  202.3 2.7 %shard_map.43.refs_9_ = bf16[1024,512]{1,0:T(8,128)(2,1)S(1)} custom-call(bf16[16,12,64,128]{3,2,1,0:T(8,128)(2,1)S(1)} %all-to-all-done.2.arrived.refs_8_, bf16[512,512]{1,0:T(8,128)(2,1)S(1)} %copy-done.6), custom_call_target="tpu_custom_call" | custom-call | flops 536870912 | bytes 2097152 | tf_op jit(solution)/shard_map/pallas_call | solution.py:327
  205.0 5.3 %shard_map.44.base = f32[8,128,512]{2,1,0:T(8,128)S(1)} custom-call(s32[128]{0:T(128)S(1)} %select_reduce_fusion.1.inv_ref, s32[128]{0:T(128)S(1)} %select_reduce_fusion.inv2_ref, bf16[2,80,1024]{2,1,0:T(8,128)(2,1)S(1)} %get-tuple-element.52.refs_0_, bf16[2,80,1024]{2,1,0:T(8,128)(2,1)S(1)} %copy-done.9, bf16[2,80,1024]{2,1,0:T(8,128)(2,1)S(1)} %copy-done.11, ...), custom_call_target="tpu_custom_call" | custom-call | flops 805306368 | bytes 6291456 | tf_op jit(solution)/shard_map/pallas_call | solution.py:333
  210.3 4.7 %collective-permute-done.20.got_b = bf16[8,64,512]{2,1,0:T(8,128)(2,1)S(1)} collective-permute-done((bf16[8,64,512]{2,1,0:T(8,128)(2,1)S(1)}, bf16[8,64,512]{2,1,0:T(8,128)(2,1)S(1)}, u32[]{:S(2)}, u32[]{:S(2)}) %collective-permute-start.20) | collective-permute-done | bytes 524320 | tf_op jit(solution)/shard_map/ppermute | solution.py:326
  (127 shorter events, 50.1 us)
Async XLA Ops:
  7.6 8.7 %copy-start.29 = (s32[1,128]{1,0:T(1,128)S(1)}, s32[1,128]{1,0:T(1,128)}, u32[]{:S(2)}) copy-start(s32[1,128]{1,0:T(1,128)} %param.4) | copy-start | bytes 1540
  7.6 63.2 %all-to-all-start = ((bf16[16,9,64,128]{3,2,1,0:T(8,128)(2,1)}), bf16[16,9,64,128]{3,2,1,0:T(8,128)(2,1)S(1)}, u32[]{:S(2)}, u32[]{:S(2)}) async-start(bf16[16,9,64,128]{3,2,1,0:T(8,128)(2,1)} %copy-done.5), calls=%async_computation | async-start | bytes 4718592 | tf_op jit(solution)/shard_map/all_to_all | solution.py:285
  20.0 4.9 %collective-permute-start = (bf16[8,64,1024]{2,1,0:T(8,128)(2,1)}, bf16[8,64,1024]{2,1,0:T(8,128)(2,1)}, u32[]{:S(2)}, u32[]{:S(2)}) collective-permute-start(bf16[8,64,1024]{2,1,0:T(8,128)(2,1)} %get-tuple-element.33), channel_id=1, source_target_pairs={{0,16},{16,0},{32,48},{48,32},{64,80},{80,64},{96,112},{112,96},{1... | collective-permute-start | bytes 3145736 | tf_op jit(solution)/shard_map/ppermute | solution.py:209
  26.9 29.8 %collective-permute-start.2 = (bf16[2,64,1024]{2,1,0:T(8,128)(2,1)S(1)}, bf16[2,64,1024]{2,1,0:T(8,128)(2,1)S(1)}, u32[]{:S(2)}, u32[]{:S(2)}) collective-permute-start(bf16[2,64,1024]{2,1,0:T(8,128)(2,1)S(1)} %pad_maximum_fusion.1), channel_id=1, source_target_pairs={{0,224},{16,48},{32,0},{48,80},{64,32},{80,112},{96,64},{112,144},... | collective-permute-start | bytes 786440 | tf_op jit(solution)/shard_map/ppermute | solution.py:220
  37.9 23.7 %collective-permute-start.3 = (bf16[2,64,1024]{2,1,0:T(8,128)(2,1)S(1)}, bf16[2,64,1024]{2,1,0:T(8,128)(2,1)S(1)}, u32[]{:S(2)}, u32[]{:S(2)}) collective-permute-start(bf16[2,64,1024]{2,1,0:T(8,128)(2,1)S(1)} %pad_maximum_fusion.2), channel_id=1, source_target_pairs={{0,192},{16,80},{32,224},{48,112},{64,0},{80,144},{96,32},{112,176... | collective-permute-start | bytes 786440 | tf_op jit(solution)/shard_map/ppermute | solution.py:220
  39.9 25.6 %collective-permute-start.4 = (bf16[2,64,1024]{2,1,0:T(8,128)(2,1)S(1)}, bf16[2,64,1024]{2,1,0:T(8,128)(2,1)S(1)}, u32[]{:S(2)}, u32[]{:S(2)}) collective-permute-start(bf16[2,64,1024]{2,1,0:T(8,128)(2,1)S(1)} %pad_maximum_fusion.3), channel_id=1, source_target_pairs={{0,160},{16,112},{32,192},{48,144},{64,224},{80,176},{96,0},{112,2... | collective-permute-start | bytes 786440 | tf_op jit(solution)/shard_map/ppermute | solution.py:220
  42.4 9.6 %collective-permute-start.1 = (s32[128]{0:T(128)S(1)}, s32[128]{0:T(128)S(1)}, u32[]{:S(2)}, u32[]{:S(2)}) collective-permute-start(s32[128]{0:T(128)S(1)} %bitcast.35), channel_id=1, source_target_pairs={{0,256},{256,0},{1,257},{257,1},{2,258},{258,2},{3,259},{259,3},{4... | collective-permute-start | bytes 1544 | tf_op jit(solution)/shard_map/ppermute | solution.py:287
  46.4 46.4 %collective-permute-start.5 = (bf16[2,64,1024]{2,1,0:T(8,128)(2,1)}, bf16[2,64,1024]{2,1,0:T(8,128)(2,1)S(1)}, u32[]{:S(2)}, u32[]{:S(2)}) collective-permute-start(bf16[2,64,1024]{2,1,0:T(8,128)(2,1)} %pad_maximum_fusion.5), channel_id=1, source_target_pairs={{0,32},{16,240},{32,64},{48,16},{64,96},{80,48},{96,128},{112,80},... | collective-permute-start | bytes 786440 | tf_op jit(solution)/shard_map/ppermute | solution.py:220
  51.9 41.6 %collective-permute-start.6 = (bf16[2,64,1024]{2,1,0:T(8,128)(2,1)}, bf16[2,64,1024]{2,1,0:T(8,128)(2,1)}, u32[]{:S(2)}, u32[]{:S(2)}) collective-permute-start(bf16[2,64,1024]{2,1,0:T(8,128)(2,1)} %pad_maximum_fusion.6), channel_id=1, source_target_pairs={{0,64},{16,208},{32,96},{48,240},{64,128},{80,16},{96,160},{112,48... | collective-permute-start | bytes 786440 | tf_op jit(solution)/shard_map/ppermute | solution.py:220
  56.8 36.7 %collective-permute-start.7 = (bf16[2,64,1024]{2,1,0:T(8,128)(2,1)}, bf16[2,64,1024]{2,1,0:T(8,128)(2,1)}, u32[]{:S(2)}, u32[]{:S(2)}) collective-permute-start(bf16[2,64,1024]{2,1,0:T(8,128)(2,1)} %pad_maximum_fusion.7), channel_id=1, source_target_pairs={{0,96},{16,176},{32,128},{48,208},{64,160},{80,240},{96,192},{112,... | collective-permute-start | bytes 786440 | tf_op jit(solution)/shard_map/ppermute | solution.py:220
  61.6 29.0 %copy-start.22 = (bf16[2,64,1024]{2,1,0:T(8,128)(2,1)}, bf16[2,64,1024]{2,1,0:T(8,128)(2,1)S(1)}, u32[]{:S(2)}) copy-start(bf16[2,64,1024]{2,1,0:T(8,128)(2,1)S(1)} %collective-permute-done.3.refs_6_) | copy-start | bytes 786436
  61.6 31.9 %collective-permute-start.8 = (bf16[2,64,1024]{2,1,0:T(8,128)(2,1)}, bf16[2,64,1024]{2,1,0:T(8,128)(2,1)}, u32[]{:S(2)}, u32[]{:S(2)}) collective-permute-start(bf16[2,64,1024]{2,1,0:T(8,128)(2,1)} %pad_maximum_fusion.8), channel_id=1, source_target_pairs={{0,128},{16,144},{32,160},{48,176},{64,192},{80,208},{96,224},{112... | collective-permute-start | bytes 786440 | tf_op jit(solution)/shard_map/ppermute | solution.py:220
  65.5 25.1 %copy-start.24 = (bf16[2,64,1024]{2,1,0:T(8,128)(2,1)}, bf16[2,64,1024]{2,1,0:T(8,128)(2,1)S(1)}, u32[]{:S(2)}) copy-start(bf16[2,64,1024]{2,1,0:T(8,128)(2,1)S(1)} %collective-permute-done.4.refs_5_) | copy-start | bytes 786436
  70.8 19.8 %copy-start.1 = (bf16[16,9,64,128]{3,2,1,0:T(8,128)(2,1)}, bf16[16,9,64,128]{3,2,1,0:T(8,128)(2,1)S(1)}, u32[]{:S(2)}) copy-start(bf16[16,9,64,128]{3,2,1,0:T(8,128)(2,1)S(1)} %all-to-all-done.arrived) | copy-start | bytes 7077892
  74.5 25.5 %all-to-all-start.1 = ((bf16[32,4,8,128]{3,2,1,0:T(8,128)(2,1)}), bf16[32,4,8,128]{3,2,1,0:T(8,128)(2,1)}, u32[]{:S(2)}, u32[]{:S(2)}) async-start(bf16[32,4,8,128]{3,2,1,0:T(8,128)(2,1)} %gather_fusion.1), calls=%async_computation.1 | async-start | bytes 524288 | tf_op jit(solution)/shard_map/all_to_all | solution.py:303
  90.6 19.4 %collective-permute-start.10 = (bf16[8,64,512]{2,1,0:T(8,128)(2,1)}, bf16[8,64,512]{2,1,0:T(8,128)(2,1)}, u32[]{:S(2)}, u32[]{:S(2)}) collective-permute-start(bf16[8,64,512]{2,1,0:T(8,128)(2,1)} %shard_map.41), channel_id=1, source_target_pairs={{0,256},{256,0},{1,257},{257,1},{2,258},{258,2},{3,259},{259,3},{4... | collective-permute-start | bytes 1572872 | tf_op jit(solution)/shard_map/ppermute | solution.py:298
  103.2 11.8 %collective-permute-start.9 = (bf16[32,512]{1,0:T(8,128)(2,1)S(1)}, bf16[32,512]{1,0:T(8,128)(2,1)S(1)}, u32[]{:S(2)}, u32[]{:S(2)}) collective-permute-start(bf16[32,512]{1,0:T(8,128)(2,1)S(1)} %constant_dynamic-slice_fusion), channel_id=1, source_target_pairs={{0,0},{1,16},{2,32},{3,48},{4,64},{5,80},{6,96},{7,112},{8,128},{9... | collective-permute-start | bytes 98312 | tf_op jit(solution)/shard_map/ppermute | solution.py:263
  115.0 82.3 %all-to-all-start.2 = ((bf16[16,12,64,128]{3,2,1,0:T(8,128)(2,1)}), bf16[16,12,64,128]{3,2,1,0:T(8,128)(2,1)S(1)}, u32[]{:S(2)}, u32[]{:S(2)}) async-start(bf16[16,12,64,128]{3,2,1,0:T(8,128)(2,1)} %copy-done), calls=%async_computation.2 | async-start | bytes 6291456 | tf_op jit(solution)/shard_map/all_to_all | solution.py:316
  127.2 5.7 %collective-permute-start.11 = (bf16[8,64,1024]{2,1,0:T(8,128)(2,1)}, bf16[8,64,1024]{2,1,0:T(8,128)(2,1)S(1)}, u32[]{:S(2)}, u32[]{:S(2)}) collective-permute-start(bf16[8,64,1024]{2,1,0:T(8,128)(2,1)} %copy-done.30), channel_id=1, source_target_pairs={{0,16},{16,0},{32,48},{48,32},{64,80},{80,64},{96,112},{112,96},{1... | collective-permute-start | bytes 3145736 | tf_op jit(solution)/shard_map/ppermute | solution.py:209
  129.2 3.9 %collective-permute-start.12 = (bf16[16,1024]{1,0:T(8,128)(2,1)S(1)}, bf16[16,1024]{1,0:T(8,128)(2,1)S(1)}, u32[]{:S(2)}, u32[]{:S(2)}) collective-permute-start(bf16[16,1024]{1,0:T(8,128)(2,1)S(1)} %pad_maximum_fusion.9), channel_id=1, source_target_pairs={{0,16},{16,0},{32,48},{48,32},{64,80},{80,64},{96,112},{112,96},{1... | collective-permute-start | bytes 98312 | tf_op jit(solution)/shard_map/ppermute | solution.py:209
  133.2 19.5 %collective-permute-start.13 = (bf16[2,80,1024]{2,1,0:T(8,128)(2,1)S(1)}, bf16[2,80,1024]{2,1,0:T(8,128)(2,1)S(1)}, u32[]{:S(2)}, u32[]{:S(2)}) collective-permute-start(bf16[2,80,1024]{2,1,0:T(8,128)(2,1)S(1)} %get-tuple-element.94), channel_id=1, source_target_pairs={{0,32},{16,240},{32,64},{48,16},{64,96},{80,48},{96,128},{112,80},... | collective-permute-start | bytes 983048 | tf_op jit(solution)/shard_map/ppermute | solution.py:220
  135.8 19.6 %collective-permute-start.14 = (bf16[2,80,1024]{2,1,0:T(8,128)(2,1)S(1)}, bf16[2,80,1024]{2,1,0:T(8,128)(2,1)S(1)}, u32[]{:S(2)}, u32[]{:S(2)}) collective-permute-start(bf16[2,80,1024]{2,1,0:T(8,128)(2,1)S(1)} %get-tuple-element.95), channel_id=1, source_target_pairs={{0,64},{16,208},{32,96},{48,240},{64,128},{80,16},{96,160},{112,48... | collective-permute-start | bytes 983048 | tf_op jit(solution)/shard_map/ppermute | solution.py:220
  137.7 46.2 %collective-permute-start.15 = (bf16[2,80,1024]{2,1,0:T(8,128)(2,1)S(1)}, bf16[2,80,1024]{2,1,0:T(8,128)(2,1)S(1)}, u32[]{:S(2)}, u32[]{:S(2)}) collective-permute-start(bf16[2,80,1024]{2,1,0:T(8,128)(2,1)S(1)} %get-tuple-element.96), channel_id=1, source_target_pairs={{0,96},{16,176},{32,128},{48,208},{64,160},{80,240},{96,192},{112,... | collective-permute-start | bytes 983048 | tf_op jit(solution)/shard_map/ppermute | solution.py:220
  139.6 45.0 %collective-permute-start.19 = (bf16[2,80,1024]{2,1,0:T(8,128)(2,1)S(1)}, bf16[2,80,1024]{2,1,0:T(8,128)(2,1)S(1)}, u32[]{:S(2)}, u32[]{:S(2)}) collective-permute-start(bf16[2,80,1024]{2,1,0:T(8,128)(2,1)S(1)} %get-tuple-element.93), channel_id=1, source_target_pairs={{0,224},{16,48},{32,0},{48,80},{64,32},{80,112},{96,64},{112,144},... | collective-permute-start | bytes 983048 | tf_op jit(solution)/shard_map/ppermute | solution.py:220
  144.4 41.0 %collective-permute-start.16 = (bf16[2,80,1024]{2,1,0:T(8,128)(2,1)S(1)}, bf16[2,80,1024]{2,1,0:T(8,128)(2,1)S(1)}, u32[]{:S(2)}, u32[]{:S(2)}) collective-permute-start(bf16[2,80,1024]{2,1,0:T(8,128)(2,1)S(1)} %get-tuple-element.98), channel_id=1, source_target_pairs={{0,128},{16,144},{32,160},{48,176},{64,192},{80,208},{96,224},{112... | collective-permute-start | bytes 983048 | tf_op jit(solution)/shard_map/ppermute | solution.py:220
  153.5 34.0 %collective-permute-start.17 = (bf16[2,80,1024]{2,1,0:T(8,128)(2,1)S(1)}, bf16[2,80,1024]{2,1,0:T(8,128)(2,1)S(1)}, u32[]{:S(2)}, u32[]{:S(2)}) collective-permute-start(bf16[2,80,1024]{2,1,0:T(8,128)(2,1)S(1)} %get-tuple-element.99), channel_id=1, source_target_pairs={{0,160},{16,112},{32,192},{48,144},{64,224},{80,176},{96,0},{112,2... | collective-permute-start | bytes 983048 | tf_op jit(solution)/shard_map/ppermute | solution.py:220
  156.1 38.0 %collective-permute-start.18 = (bf16[2,80,1024]{2,1,0:T(8,128)(2,1)S(1)}, bf16[2,80,1024]{2,1,0:T(8,128)(2,1)S(1)}, u32[]{:S(2)}, u32[]{:S(2)}) collective-permute-start(bf16[2,80,1024]{2,1,0:T(8,128)(2,1)S(1)} %get-tuple-element.97), channel_id=1, source_target_pairs={{0,192},{16,80},{32,224},{48,112},{64,0},{80,144},{96,32},{112,176... | collective-permute-start | bytes 983048 | tf_op jit(solution)/shard_map/ppermute | solution.py:220
  198.0 7.0 %copy-start.9 = (bf16[2,80,1024]{2,1,0:T(8,128)(2,1)S(1)}, bf16[2,80,1024]{2,1,0:T(8,128)(2,1)}, u32[]{:S(2)}) copy-start(bf16[2,80,1024]{2,1,0:T(8,128)(2,1)} %copy-done.8) | copy-start | bytes 983044
  198.0 7.0 %copy-start.11 = (bf16[2,80,1024]{2,1,0:T(8,128)(2,1)S(1)}, bf16[2,80,1024]{2,1,0:T(8,128)(2,1)}, u32[]{:S(2)}) copy-start(bf16[2,80,1024]{2,1,0:T(8,128)(2,1)} %copy-done.10) | copy-start | bytes 983044
  198.0 7.0 %copy-start.13 = (bf16[2,80,1024]{2,1,0:T(8,128)(2,1)S(1)}, bf16[2,80,1024]{2,1,0:T(8,128)(2,1)}, u32[]{:S(2)}) copy-start(bf16[2,80,1024]{2,1,0:T(8,128)(2,1)} %copy-done.12) | copy-start | bytes 983044
  198.0 7.0 %copy-start.15 = (bf16[2,80,1024]{2,1,0:T(8,128)(2,1)S(1)}, bf16[2,80,1024]{2,1,0:T(8,128)(2,1)}, u32[]{:S(2)}) copy-start(bf16[2,80,1024]{2,1,0:T(8,128)(2,1)} %copy-done.14) | copy-start | bytes 983044
  198.0 17.0 %collective-permute-start.20 = (bf16[8,64,512]{2,1,0:T(8,128)(2,1)S(1)}, bf16[8,64,512]{2,1,0:T(8,128)(2,1)S(1)}, u32[]{:S(2)}, u32[]{:S(2)}) collective-permute-start(bf16[8,64,512]{2,1,0:T(8,128)(2,1)S(1)} %shard_map.45), channel_id=1, source_target_pairs={{0,256},{256,0},{1,257},{257,1},{2,258},{258,2},{3,259},{259,3},{4... | collective-permute-start | bytes 1572872 | tf_op jit(solution)/shard_map/ppermute | solution.py:326
  (23 other events, 46.7 us)

commit v5 on v4

--- a/solution.py
+++ b/solution.py
@@ -275,7 +275,7 @@
 
     rows_a, rows_b = bf16(8, HA, W * B), bf16(8, HB, W * B)
     send_a = pl.pallas_call(
-        pack_cols, out_shape=bf16(G, W + 1, HA, B), in_specs=[SMEM, ANY, ANY], out_specs=ANY,
+        pack_cols, out_shape=pltpu.HBM((G, W + 1, HA, B), jnp.bfloat16), in_specs=[SMEM, ANY, ANY], out_specs=ANY,
         scratch_shapes=[dma, dma], **params(moved=2 * MiB),
     )(maps, blocks, panel_column(tile, maps))
     own, swap = pl.pallas_call(
@@ -286,8 +286,7 @@
     other, maps_later = lax.optimization_barrier((core_exchange(swap), maps))
     maps2 = lax.ppermute(maps_later, "sib", exchange)
     got_b = z_ring(pairs_of(own, other))
-    got_a, maps2, got_b[7], got_b[6], got_b[5] = lax.optimization_barrier(
-        (got_a, maps2, got_b[7], got_b[6], got_b[5]))
+    got_a, maps2, got_b[7], got_b[6] = lax.optimization_barrier((got_a, maps2, got_b[7], got_b[6]))
 
     inv2 = inverse_of(maps2)
     pieces, got_a = lax.optimization_barrier((panel_slots(got_a[:, W].reshape(G, W, 8, B), maps, inv), got_a))

time: 219 us -> 219 us (level)
    unnamed x62 -> x60, local copies, waits for them, and re-layouts: 17.5 us -> 16.8 us
  transfers between devices with their start and end apart: 24 -> 24, of which waited for: 9 -> 9; matrix products, arithmetic and copies ran while one was open for 7% -> 8% of each run, Pallas kernels for 8% -> 8%
where the time goes in v5:
time: 219 us; the launch traced here: 217 us
  starting transfers between devices  112 us (51%)
  waiting for transfers between devices  45.4 us (21%)
  local copies, waits for them, and re-layouts  28 us (13%)
  Pallas kernels  21.7 us (10%)
  other arithmetic  7.95 us (4%)
    ppermute x14, starting transfers between devices, z_ring(): arrived[k] = lax.ppermute(both[k], 'row', pairs)  56.9 us
    ppermute x14, waiting for transfers between devices, z_ring(): arrived[k] = lax.ppermute(both[k], 'row', pairs)  30.5 us
    unnamed x60, local copies, waits for them, and re-layouts  16.8 us
    all_to_all x1, starting transfers between devices, shards(): pieces = lax.all_to_all(pieces, ('sib', 'row'), 0, 0, tiled=True)  13.5 us
    all_to_all x1, starting transfers between devices, shards(): got_b = lax.all_to_all(send_b, 'col', 0, 0, tiled=True)  12.9 us
    all_to_all x1, starting transfers between devices, shards(): got_a = lax.all_to_all(send_a, 'col', 0, 0, tiled=True)  8.6 us
    ppermute x3, starting transfers between devices, core_exchange(): return lax.ppermute(swap, 'row', [(i, i ^ 1) for i in range(G)])  6.24 us
    pallas_call x1, Pallas kernels, shards(): pl.pallas_call(keep, out_shape=full, in_specs=[SMEM] * 2 + [ANY] * 9 + [V...  5.3 us
  transfers between devices with their start and end apart: 24, of which 9 were waited for; matrix products, arithmetic and copies ran while one was open for 8% of the time, Pallas kernels for 8%

profile of v5, /device:TPU:6, one launch (start us, length us, event | category | flops | bytes accessed | tf_op | source)
XLA Modules:
  0.0 216.5 jit_solution(17758976908349380109)
XLA Ops:
  7.0 8.6 %all-to-all-start = ((bf16[16,9,64,128]{3,2,1,0:T(8,128)(2,1)}), bf16[16,9,64,128]{3,2,1,0:T(8,128)(2,1)S(1)}, u32[]{:S(2)}, u32[]{:S(2)}) async-start(bf16[16,9,64,128]{3,2,1,0:T(8,128)(2,1)} %shard_map.37), calls=%async_computation | async-start | bytes 4718592 | tf_op jit(solution)/shard_map/all_to_all | solution.py:285
  19.1 1.9 collective-permute-start
  24.0 2.0 fusion.16
  26.0 10.5 %collective-permute-start.2 = (bf16[2,64,1024]{2,1,0:T(8,128)(2,1)S(1)}, bf16[2,64,1024]{2,1,0:T(8,128)(2,1)S(1)}, u32[]{:S(2)}, u32[]{:S(2)}) collective-permute-start(bf16[2,64,1024]{2,1,0:T(8,128)(2,1)S(1)} %pad_maximum_fusion.1), channel_id=1, source_target_pairs={{0,224},{16,48},{32,0},{48,80},{64,32},{80,112},{96,64},{112,144},... | collective-permute-start | bytes 786440 | tf_op jit(solution)/shard_map/ppermute | solution.py:220
  36.5 2.7 %collective-permute-start.3 = (bf16[2,64,1024]{2,1,0:T(8,128)(2,1)S(1)}, bf16[2,64,1024]{2,1,0:T(8,128)(2,1)S(1)}, u32[]{:S(2)}, u32[]{:S(2)}) collective-permute-start(bf16[2,64,1024]{2,1,0:T(8,128)(2,1)S(1)} %pad_maximum_fusion.2), channel_id=1, source_target_pairs={{0,192},{16,80},{32,224},{48,112},{64,0},{80,144},{96,32},{112,176... | collective-permute-start | bytes 786440 | tf_op jit(solution)/shard_map/ppermute | solution.py:220
  39.3 3.5 %collective-permute-start.1 = (s32[128]{0:T(128)S(1)}, s32[128]{0:T(128)S(1)}, u32[]{:S(2)}, u32[]{:S(2)}) collective-permute-start(s32[128]{0:T(128)S(1)} %bitcast.35), channel_id=1, source_target_pairs={{0,256},{256,0},{1,257},{257,1},{2,258},{258,2},{3,259},{259,3},{4... | collective-permute-start | bytes 1544 | tf_op jit(solution)/shard_map/ppermute | solution.py:287
  43.5 3.3 %collective-permute-start.4 = (bf16[2,64,1024]{2,1,0:T(8,128)(2,1)}, bf16[2,64,1024]{2,1,0:T(8,128)(2,1)S(1)}, u32[]{:S(2)}, u32[]{:S(2)}) collective-permute-start(bf16[2,64,1024]{2,1,0:T(8,128)(2,1)} %pad_maximum_fusion.4), channel_id=1, source_target_pairs={{0,32},{16,240},{32,64},{48,16},{64,96},{80,48},{96,128},{112,80},... | collective-permute-start | bytes 786440 | tf_op jit(solution)/shard_map/ppermute | solution.py:220
  47.6 3.0 %collective-permute-start.5 = (bf16[2,64,1024]{2,1,0:T(8,128)(2,1)}, bf16[2,64,1024]{2,1,0:T(8,128)(2,1)S(1)}, u32[]{:S(2)}, u32[]{:S(2)}) collective-permute-start(bf16[2,64,1024]{2,1,0:T(8,128)(2,1)} %pad_maximum_fusion.5), channel_id=1, source_target_pairs={{0,64},{16,208},{32,96},{48,240},{64,128},{80,16},{96,160},{112,48... | collective-permute-start | bytes 786440 | tf_op jit(solution)/shard_map/ppermute | solution.py:220
  52.8 2.5 %collective-permute-start.6 = (bf16[2,64,1024]{2,1,0:T(8,128)(2,1)}, bf16[2,64,1024]{2,1,0:T(8,128)(2,1)}, u32[]{:S(2)}, u32[]{:S(2)}) collective-permute-start(bf16[2,64,1024]{2,1,0:T(8,128)(2,1)} %pad_maximum_fusion.6), channel_id=1, source_target_pairs={{0,96},{16,176},{32,128},{48,208},{64,160},{80,240},{96,192},{112,... | collective-permute-start | bytes 786440 | tf_op jit(solution)/shard_map/ppermute | solution.py:220
  55.3 7.8 %collective-permute-start.7 = (bf16[2,64,1024]{2,1,0:T(8,128)(2,1)}, bf16[2,64,1024]{2,1,0:T(8,128)(2,1)}, u32[]{:S(2)}, u32[]{:S(2)}) collective-permute-start(bf16[2,64,1024]{2,1,0:T(8,128)(2,1)} %pad_maximum_fusion.7), channel_id=1, source_target_pairs={{0,128},{16,144},{32,160},{48,176},{64,192},{80,208},{96,224},{112... | collective-permute-start | bytes 786440 | tf_op jit(solution)/shard_map/ppermute | solution.py:220
  63.2 2.5 %collective-permute-start.8 = (bf16[2,64,1024]{2,1,0:T(8,128)(2,1)}, bf16[2,64,1024]{2,1,0:T(8,128)(2,1)}, u32[]{:S(2)}, u32[]{:S(2)}) collective-permute-start(bf16[2,64,1024]{2,1,0:T(8,128)(2,1)} %pad_maximum_fusion.8), channel_id=1, source_target_pairs={{0,160},{16,112},{32,192},{48,144},{64,224},{80,176},{96,0},{112,2... | collective-permute-start | bytes 786440 | tf_op jit(solution)/shard_map/ppermute | solution.py:220
  65.6 4.4 %all-to-all-done.arrived = bf16[16,9,64,128]{3,2,1,0:T(8,128)(2,1)S(1)} async-done(((bf16[16,9,64,128]{3,2,1,0:T(8,128)(2,1)}), bf16[16,9,64,128]{3,2,1,0:T(8,128)(2,1)S(1)}, u32[]{:S(2)}, u32[]{:S(2)}) %all-to-all-start) | async-done | bytes 2359328 | tf_op jit(solution)/shard_map/all_to_all | solution.py:285
  73.9 13.5 %all-to-all-start.1 = ((bf16[32,4,8,128]{3,2,1,0:T(8,128)(2,1)}), bf16[32,4,8,128]{3,2,1,0:T(8,128)(2,1)}, u32[]{:S(2)}, u32[]{:S(2)}) async-start(bf16[32,4,8,128]{3,2,1,0:T(8,128)(2,1)} %gather_fusion.1), calls=%async_computation.1 | async-start | bytes 524288 | tf_op jit(solution)/shard_map/all_to_all | solution.py:302
  90.6 2.2 %collective-permute-start.10 = (bf16[8,64,512]{2,1,0:T(8,128)(2,1)}, bf16[8,64,512]{2,1,0:T(8,128)(2,1)}, u32[]{:S(2)}, u32[]{:S(2)}) collective-permute-start(bf16[8,64,512]{2,1,0:T(8,128)(2,1)} %shard_map.41), channel_id=1, source_target_pairs={{0,256},{256,0},{1,257},{257,1},{2,258},{258,2},{3,259},{259,3},{4... | collective-permute-start | bytes 1572872 | tf_op jit(solution)/shard_map/ppermute | solution.py:297
  96.4 2.4 %shard_map.39.a = bf16[16,12,64,128]{3,2,1,0:T(8,128)(2,1)S(1)} custom-call(s32[128]{0:T(128)S(1)} %bitcast.36, s32[128]{0:T(128)S(1)} %select_reduce_fusion.1.inv_ref, bf16[2,64,1024]{2,1,0:T(8,128)(2,1)S(1)} %pad_maximum_fusion.3.refs_0_, bf16[2,64,1024]{2,1,0:T(8,128)(2,1)S(1)} %copy-done.24, bf16[2,64,1024]{2,1,0:T(8,128)(2,1)S(1)} %copy-done.26, ...), custom_call_target="tpu_custom_call" | custom-call | bytes 2097152 | tf_op jit(solution)/shard_map/pallas_call | solution.py:298
  99.4 2.2 gather_fusion.2
  102.6 4.1 %collective-permute-start.9 = (bf16[32,512]{1,0:T(8,128)(2,1)S(1)}, bf16[32,512]{1,0:T(8,128)(2,1)S(1)}, u32[]{:S(2)}, u32[]{:S(2)}) collective-permute-start(bf16[32,512]{1,0:T(8,128)(2,1)S(1)} %constant_dynamic-slice_fusion), channel_id=1, source_target_pairs={{0,0},{1,16},{2,32},{3,48},{4,64},{5,80},{6,96},{7,112},{8,128},{9... | collective-permute-start | bytes 98312 | tf_op jit(solution)/shard_map/ppermute | solution.py:263
  109.8 2.4 %shard_map.42 = (bf16[8,64,1024]{2,1,0:T(8,128)(2,1)S(1)}, bf16[8,64,1024]{2,1,0:T(8,128)(2,1)S(1)}) custom-call(s32[128]{0:T(128)S(1)} %bitcast.37, s32[128]{0:T(128)S(1)} %collective-permute-done.1.map2_ref, s32[128]{0:T(128)S(1)} %select_reduce_fusion.1.inv_ref, bf16[16,9,64,128]{3,2,1,0:T(8,128)(2,1)S(1)} %copy-done.2, ...), custom_call_target="tpu_custom_call" | custom-call | bytes 2097152 | tf_op jit(solution)/shard_map/pallas_call | solution.py:303
  114.5 12.9 %all-to-all-start.2 = ((bf16[16,12,64,128]{3,2,1,0:T(8,128)(2,1)}), bf16[16,12,64,128]{3,2,1,0:T(8,128)(2,1)S(1)}, u32[]{:S(2)}, u32[]{:S(2)}) async-start(bf16[16,12,64,128]{3,2,1,0:T(8,128)(2,1)} %copy-done), calls=%async_computation.2 | async-start | bytes 6291456 | tf_op jit(solution)/shard_map/all_to_all | solution.py:315
  129.3 2.4 %collective-permute-start.12 = (bf16[16,1024]{1,0:T(8,128)(2,1)S(1)}, bf16[16,1024]{1,0:T(8,128)(2,1)S(1)}, u32[]{:S(2)}, u32[]{:S(2)}) collective-permute-start(bf16[16,1024]{1,0:T(8,128)(2,1)S(1)} %pad_maximum_fusion.9), channel_id=1, source_target_pairs={{0,16},{16,0},{32,48},{48,32},{64,80},{80,64},{96,112},{112,96},{1... | collective-permute-start | bytes 98312 | tf_op jit(solution)/shard_map/ppermute | solution.py:209
  133.4 2.0 collective-permute-start.13
  137.3 2.0 collective-permute-start.15
  139.3 5.1 %collective-permute-start.19 = (bf16[2,80,1024]{2,1,0:T(8,128)(2,1)S(1)}, bf16[2,80,1024]{2,1,0:T(8,128)(2,1)S(1)}, u32[]{:S(2)}, u32[]{:S(2)}) collective-permute-start(bf16[2,80,1024]{2,1,0:T(8,128)(2,1)S(1)} %get-tuple-element.91), channel_id=1, source_target_pairs={{0,224},{16,48},{32,0},{48,80},{64,32},{80,112},{96,64},{112,144},... | collective-permute-start | bytes 983048 | tf_op jit(solution)/shard_map/ppermute | solution.py:220
  144.6 7.8 %collective-permute-start.16 = (bf16[2,80,1024]{2,1,0:T(8,128)(2,1)S(1)}, bf16[2,80,1024]{2,1,0:T(8,128)(2,1)S(1)}, u32[]{:S(2)}, u32[]{:S(2)}) collective-permute-start(bf16[2,80,1024]{2,1,0:T(8,128)(2,1)S(1)} %get-tuple-element.96), channel_id=1, source_target_pairs={{0,128},{16,144},{32,160},{48,176},{64,192},{80,208},{96,224},{112... | collective-permute-start | bytes 983048 | tf_op jit(solution)/shard_map/ppermute | solution.py:220
  155.7 3.8 %collective-permute-start.18 = (bf16[2,80,1024]{2,1,0:T(8,128)(2,1)S(1)}, bf16[2,80,1024]{2,1,0:T(8,128)(2,1)S(1)}, u32[]{:S(2)}, u32[]{:S(2)}) collective-permute-start(bf16[2,80,1024]{2,1,0:T(8,128)(2,1)S(1)} %get-tuple-element.95), channel_id=1, source_target_pairs={{0,192},{16,80},{32,224},{48,112},{64,0},{80,144},{96,32},{112,176... | collective-permute-start | bytes 983048 | tf_op jit(solution)/shard_map/ppermute | solution.py:220
  159.6 25.0 %collective-permute-done.15.refs_3_ = bf16[2,80,1024]{2,1,0:T(8,128)(2,1)S(1)} collective-permute-done((bf16[2,80,1024]{2,1,0:T(8,128)(2,1)S(1)}, bf16[2,80,1024]{2,1,0:T(8,128)(2,1)S(1)}, u32[]{:S(2)}, u32[]{:S(2)}) %collective-permute-start.15) | collective-permute-done | bytes 327712 | tf_op jit(solution)/shard_map/ppermute | solution.py:220
  187.9 5.0 %collective-permute-done.18.refs_6_ = bf16[2,80,1024]{2,1,0:T(8,128)(2,1)S(1)} collective-permute-done((bf16[2,80,1024]{2,1,0:T(8,128)(2,1)S(1)}, bf16[2,80,1024]{2,1,0:T(8,128)(2,1)S(1)}, u32[]{:S(2)}, u32[]{:S(2)}) %collective-permute-start.18) | collective-permute-done | bytes 327712 | tf_op jit(solution)/shard_map/ppermute | solution.py:220
  193.7 3.7 %all-to-all-done.2.arrived.refs_8_ = bf16[16,12,64,128]{3,2,1,0:T(8,128)(2,1)S(1)} async-done(((bf16[16,12,64,128]{3,2,1,0:T(8,128)(2,1)}), bf16[16,12,64,128]{3,2,1,0:T(8,128)(2,1)S(1)}, u32[]{:S(2)}, u32[]{:S(2)}) %all-to-all-start.2) | async-done | bytes 3145760 | tf_op jit(solution)/shard_map/all_to_all | solution.py:315
  198.1 4.2 %collective-permute-start.20 = (bf16[8,64,512]{2,1,0:T(8,128)(2,1)S(1)}, bf16[8,64,512]{2,1,0:T(8,128)(2,1)S(1)}, u32[]{:S(2)}, u32[]{:S(2)}) collective-permute-start(bf16[8,64,512]{2,1,0:T(8,128)(2,1)S(1)} %shard_map.45), channel_id=1, source_target_pairs={{0,256},{256,0},{1,257},{257,1},{2,258},{258,2},{3,259},{259,3},{4... | collective-permute-start | bytes 1572872 | tf_op jit(solution)/shard_map/ppermute | solution.py:325
  202.4 2.7 %shard_map.43.refs_9_ = bf16[1024,512]{1,0:T(8,128)(2,1)S(1)} custom-call(bf16[16,12,64,128]{3,2,1,0:T(8,128)(2,1)S(1)} %all-to-all-done.2.arrived.refs_8_, bf16[512,512]{1,0:T(8,128)(2,1)S(1)} %copy-done.5), custom_call_target="tpu_custom_call" | custom-call | flops 536870912 | bytes 2097152 | tf_op jit(solution)/shard_map/pallas_call | solution.py:326
  205.1 5.3 %shard_map.44.base = f32[8,128,512]{2,1,0:T(8,128)S(1)} custom-call(s32[128]{0:T(128)S(1)} %select_reduce_fusion.1.inv_ref, s32[128]{0:T(128)S(1)} %select_reduce_fusion.inv2_ref, bf16[2,80,1024]{2,1,0:T(8,128)(2,1)S(1)} %get-tuple-element.50.refs_0_, bf16[2,80,1024]{2,1,0:T(8,128)(2,1)S(1)} %copy-done.8, bf16[2,80,1024]{2,1,0:T(8,128)(2,1)S(1)} %copy-done.10, ...), custom_call_target="tpu_custom_call" | custom-call | flops 805306368 | bytes 6291456 | tf_op jit(solution)/shard_map/pallas_call | solution.py:332
  210.4 4.2 %collective-permute-done.20.got_b = bf16[8,64,512]{2,1,0:T(8,128)(2,1)S(1)} collective-permute-done((bf16[8,64,512]{2,1,0:T(8,128)(2,1)S(1)}, bf16[8,64,512]{2,1,0:T(8,128)(2,1)S(1)}, u32[]{:S(2)}, u32[]{:S(2)}) %collective-permute-start.20) | collective-permute-done | bytes 524320 | tf_op jit(solution)/shard_map/ppermute | solution.py:325
  (125 shorter events, 49.5 us)
Async XLA Ops:
  7.0 8.6 %copy-start.28 = (s32[1,128]{1,0:T(1,128)S(1)}, s32[1,128]{1,0:T(1,128)}, u32[]{:S(2)}) copy-start(s32[1,128]{1,0:T(1,128)} %param.4) | copy-start | bytes 1540
  7.0 63.1 %all-to-all-start = ((bf16[16,9,64,128]{3,2,1,0:T(8,128)(2,1)}), bf16[16,9,64,128]{3,2,1,0:T(8,128)(2,1)S(1)}, u32[]{:S(2)}, u32[]{:S(2)}) async-start(bf16[16,9,64,128]{3,2,1,0:T(8,128)(2,1)} %shard_map.37), calls=%async_computation | async-start | bytes 4718592 | tf_op jit(solution)/shard_map/all_to_all | solution.py:285
  19.1 4.9 %collective-permute-start = (bf16[8,64,1024]{2,1,0:T(8,128)(2,1)}, bf16[8,64,1024]{2,1,0:T(8,128)(2,1)}, u32[]{:S(2)}, u32[]{:S(2)}) collective-permute-start(bf16[8,64,1024]{2,1,0:T(8,128)(2,1)} %get-tuple-element.32), channel_id=1, source_target_pairs={{0,16},{16,0},{32,48},{48,32},{64,80},{80,64},{96,112},{112,96},{1... | collective-permute-start | bytes 3145736 | tf_op jit(solution)/shard_map/ppermute | solution.py:209
  26.0 29.3 %collective-permute-start.2 = (bf16[2,64,1024]{2,1,0:T(8,128)(2,1)S(1)}, bf16[2,64,1024]{2,1,0:T(8,128)(2,1)S(1)}, u32[]{:S(2)}, u32[]{:S(2)}) collective-permute-start(bf16[2,64,1024]{2,1,0:T(8,128)(2,1)S(1)} %pad_maximum_fusion.1), channel_id=1, source_target_pairs={{0,224},{16,48},{32,0},{48,80},{64,32},{80,112},{96,64},{112,144},... | collective-permute-start | bytes 786440 | tf_op jit(solution)/shard_map/ppermute | solution.py:220
  36.5 26.6 %collective-permute-start.3 = (bf16[2,64,1024]{2,1,0:T(8,128)(2,1)S(1)}, bf16[2,64,1024]{2,1,0:T(8,128)(2,1)S(1)}, u32[]{:S(2)}, u32[]{:S(2)}) collective-permute-start(bf16[2,64,1024]{2,1,0:T(8,128)(2,1)S(1)} %pad_maximum_fusion.2), channel_id=1, source_target_pairs={{0,192},{16,80},{32,224},{48,112},{64,0},{80,144},{96,32},{112,176... | collective-permute-start | bytes 786440 | tf_op jit(solution)/shard_map/ppermute | solution.py:220
  39.3 13.6 %collective-permute-start.1 = (s32[128]{0:T(128)S(1)}, s32[128]{0:T(128)S(1)}, u32[]{:S(2)}, u32[]{:S(2)}) collective-permute-start(s32[128]{0:T(128)S(1)} %bitcast.35), channel_id=1, source_target_pairs={{0,256},{256,0},{1,257},{257,1},{2,258},{258,2},{3,259},{259,3},{4... | collective-permute-start | bytes 1544 | tf_op jit(solution)/shard_map/ppermute | solution.py:287
  43.5 46.4 %collective-permute-start.4 = (bf16[2,64,1024]{2,1,0:T(8,128)(2,1)}, bf16[2,64,1024]{2,1,0:T(8,128)(2,1)S(1)}, u32[]{:S(2)}, u32[]{:S(2)}) collective-permute-start(bf16[2,64,1024]{2,1,0:T(8,128)(2,1)} %pad_maximum_fusion.4), channel_id=1, source_target_pairs={{0,32},{16,240},{32,64},{48,16},{64,96},{80,48},{96,128},{112,80},... | collective-permute-start | bytes 786440 | tf_op jit(solution)/shard_map/ppermute | solution.py:220
  47.6 45.2 %collective-permute-start.5 = (bf16[2,64,1024]{2,1,0:T(8,128)(2,1)}, bf16[2,64,1024]{2,1,0:T(8,128)(2,1)S(1)}, u32[]{:S(2)}, u32[]{:S(2)}) collective-permute-start(bf16[2,64,1024]{2,1,0:T(8,128)(2,1)} %pad_maximum_fusion.5), channel_id=1, source_target_pairs={{0,64},{16,208},{32,96},{48,240},{64,128},{80,16},{96,160},{112,48... | collective-permute-start | bytes 786440 | tf_op jit(solution)/shard_map/ppermute | solution.py:220
  52.8 40.7 %collective-permute-start.6 = (bf16[2,64,1024]{2,1,0:T(8,128)(2,1)}, bf16[2,64,1024]{2,1,0:T(8,128)(2,1)}, u32[]{:S(2)}, u32[]{:S(2)}) collective-permute-start(bf16[2,64,1024]{2,1,0:T(8,128)(2,1)} %pad_maximum_fusion.6), channel_id=1, source_target_pairs={{0,96},{16,176},{32,128},{48,208},{64,160},{80,240},{96,192},{112,... | collective-permute-start | bytes 786440 | tf_op jit(solution)/shard_map/ppermute | solution.py:220
  55.3 38.2 %collective-permute-start.7 = (bf16[2,64,1024]{2,1,0:T(8,128)(2,1)}, bf16[2,64,1024]{2,1,0:T(8,128)(2,1)}, u32[]{:S(2)}, u32[]{:S(2)}) collective-permute-start(bf16[2,64,1024]{2,1,0:T(8,128)(2,1)} %pad_maximum_fusion.7), channel_id=1, source_target_pairs={{0,128},{16,144},{32,160},{48,176},{64,192},{80,208},{96,224},{112... | collective-permute-start | bytes 786440 | tf_op jit(solution)/shard_map/ppermute | solution.py:220
  63.1 26.7 %copy-start.21 = (bf16[2,64,1024]{2,1,0:T(8,128)(2,1)}, bf16[2,64,1024]{2,1,0:T(8,128)(2,1)S(1)}, u32[]{:S(2)}) copy-start(bf16[2,64,1024]{2,1,0:T(8,128)(2,1)S(1)} %collective-permute-done.3.refs_6_) | copy-start | bytes 786436
  63.2 30.4 %collective-permute-start.8 = (bf16[2,64,1024]{2,1,0:T(8,128)(2,1)}, bf16[2,64,1024]{2,1,0:T(8,128)(2,1)}, u32[]{:S(2)}, u32[]{:S(2)}) collective-permute-start(bf16[2,64,1024]{2,1,0:T(8,128)(2,1)} %pad_maximum_fusion.8), channel_id=1, source_target_pairs={{0,160},{16,112},{32,192},{48,144},{64,224},{80,176},{96,0},{112,2... | collective-permute-start | bytes 786440 | tf_op jit(solution)/shard_map/ppermute | solution.py:220
  70.1 19.8 %copy-start.1 = (bf16[16,9,64,128]{3,2,1,0:T(8,128)(2,1)}, bf16[16,9,64,128]{3,2,1,0:T(8,128)(2,1)S(1)}, u32[]{:S(2)}) copy-start(bf16[16,9,64,128]{3,2,1,0:T(8,128)(2,1)S(1)} %all-to-all-done.arrived) | copy-start | bytes 7077892
  73.9 25.6 %all-to-all-start.1 = ((bf16[32,4,8,128]{3,2,1,0:T(8,128)(2,1)}), bf16[32,4,8,128]{3,2,1,0:T(8,128)(2,1)}, u32[]{:S(2)}, u32[]{:S(2)}) async-start(bf16[32,4,8,128]{3,2,1,0:T(8,128)(2,1)} %gather_fusion.1), calls=%async_computation.1 | async-start | bytes 524288 | tf_op jit(solution)/shard_map/all_to_all | solution.py:302
  90.6 19.2 %collective-permute-start.10 = (bf16[8,64,512]{2,1,0:T(8,128)(2,1)}, bf16[8,64,512]{2,1,0:T(8,128)(2,1)}, u32[]{:S(2)}, u32[]{:S(2)}) collective-permute-start(bf16[8,64,512]{2,1,0:T(8,128)(2,1)} %shard_map.41), channel_id=1, source_target_pairs={{0,256},{256,0},{1,257},{257,1},{2,258},{258,2},{3,259},{259,3},{4... | collective-permute-start | bytes 1572872 | tf_op jit(solution)/shard_map/ppermute | solution.py:297
  102.6 11.9 %collective-permute-start.9 = (bf16[32,512]{1,0:T(8,128)(2,1)S(1)}, bf16[32,512]{1,0:T(8,128)(2,1)S(1)}, u32[]{:S(2)}, u32[]{:S(2)}) collective-permute-start(bf16[32,512]{1,0:T(8,128)(2,1)S(1)} %constant_dynamic-slice_fusion), channel_id=1, source_target_pairs={{0,0},{1,16},{2,32},{3,48},{4,64},{5,80},{6,96},{7,112},{8,128},{9... | collective-permute-start | bytes 98312 | tf_op jit(solution)/shard_map/ppermute | solution.py:263
  114.5 82.9 %all-to-all-start.2 = ((bf16[16,12,64,128]{3,2,1,0:T(8,128)(2,1)}), bf16[16,12,64,128]{3,2,1,0:T(8,128)(2,1)S(1)}, u32[]{:S(2)}, u32[]{:S(2)}) async-start(bf16[16,12,64,128]{3,2,1,0:T(8,128)(2,1)} %copy-done), calls=%async_computation.2 | async-start | bytes 6291456 | tf_op jit(solution)/shard_map/all_to_all | solution.py:315
  127.4 5.7 %collective-permute-start.11 = (bf16[8,64,1024]{2,1,0:T(8,128)(2,1)}, bf16[8,64,1024]{2,1,0:T(8,128)(2,1)S(1)}, u32[]{:S(2)}, u32[]{:S(2)}) collective-permute-start(bf16[8,64,1024]{2,1,0:T(8,128)(2,1)} %copy-done.29), channel_id=1, source_target_pairs={{0,16},{16,0},{32,48},{48,32},{64,80},{80,64},{96,112},{112,96},{1... | collective-permute-start | bytes 3145736 | tf_op jit(solution)/shard_map/ppermute | solution.py:209
  129.3 3.9 %collective-permute-start.12 = (bf16[16,1024]{1,0:T(8,128)(2,1)S(1)}, bf16[16,1024]{1,0:T(8,128)(2,1)S(1)}, u32[]{:S(2)}, u32[]{:S(2)}) collective-permute-start(bf16[16,1024]{1,0:T(8,128)(2,1)S(1)} %pad_maximum_fusion.9), channel_id=1, source_target_pairs={{0,16},{16,0},{32,48},{48,32},{64,80},{80,64},{96,112},{112,96},{1... | collective-permute-start | bytes 98312 | tf_op jit(solution)/shard_map/ppermute | solution.py:209
  133.4 19.0 %collective-permute-start.13 = (bf16[2,80,1024]{2,1,0:T(8,128)(2,1)S(1)}, bf16[2,80,1024]{2,1,0:T(8,128)(2,1)S(1)}, u32[]{:S(2)}, u32[]{:S(2)}) collective-permute-start(bf16[2,80,1024]{2,1,0:T(8,128)(2,1)S(1)} %get-tuple-element.92), channel_id=1, source_target_pairs={{0,32},{16,240},{32,64},{48,16},{64,96},{80,48},{96,128},{112,80},... | collective-permute-start | bytes 983048 | tf_op jit(solution)/shard_map/ppermute | solution.py:220
  135.4 19.6 %collective-permute-start.14 = (bf16[2,80,1024]{2,1,0:T(8,128)(2,1)S(1)}, bf16[2,80,1024]{2,1,0:T(8,128)(2,1)S(1)}, u32[]{:S(2)}, u32[]{:S(2)}) collective-permute-start(bf16[2,80,1024]{2,1,0:T(8,128)(2,1)S(1)} %get-tuple-element.93), channel_id=1, source_target_pairs={{0,64},{16,208},{32,96},{48,240},{64,128},{80,16},{96,160},{112,48... | collective-permute-start | bytes 983048 | tf_op jit(solution)/shard_map/ppermute | solution.py:220
  137.3 47.2 %collective-permute-start.15 = (bf16[2,80,1024]{2,1,0:T(8,128)(2,1)S(1)}, bf16[2,80,1024]{2,1,0:T(8,128)(2,1)S(1)}, u32[]{:S(2)}, u32[]{:S(2)}) collective-permute-start(bf16[2,80,1024]{2,1,0:T(8,128)(2,1)S(1)} %get-tuple-element.94), channel_id=1, source_target_pairs={{0,96},{16,176},{32,128},{48,208},{64,160},{80,240},{96,192},{112,... | collective-permute-start | bytes 983048 | tf_op jit(solution)/shard_map/ppermute | solution.py:220
  139.3 46.0 %collective-permute-start.19 = (bf16[2,80,1024]{2,1,0:T(8,128)(2,1)S(1)}, bf16[2,80,1024]{2,1,0:T(8,128)(2,1)S(1)}, u32[]{:S(2)}, u32[]{:S(2)}) collective-permute-start(bf16[2,80,1024]{2,1,0:T(8,128)(2,1)S(1)} %get-tuple-element.91), channel_id=1, source_target_pairs={{0,224},{16,48},{32,0},{48,80},{64,32},{80,112},{96,64},{112,144},... | collective-permute-start | bytes 983048 | tf_op jit(solution)/shard_map/ppermute | solution.py:220
  144.6 41.4 %collective-permute-start.16 = (bf16[2,80,1024]{2,1,0:T(8,128)(2,1)S(1)}, bf16[2,80,1024]{2,1,0:T(8,128)(2,1)S(1)}, u32[]{:S(2)}, u32[]{:S(2)}) collective-permute-start(bf16[2,80,1024]{2,1,0:T(8,128)(2,1)S(1)} %get-tuple-element.96), channel_id=1, source_target_pairs={{0,128},{16,144},{32,160},{48,176},{64,192},{80,208},{96,224},{112... | collective-permute-start | bytes 983048 | tf_op jit(solution)/shard_map/ppermute | solution.py:220
  153.1 34.1 %collective-permute-start.17 = (bf16[2,80,1024]{2,1,0:T(8,128)(2,1)S(1)}, bf16[2,80,1024]{2,1,0:T(8,128)(2,1)S(1)}, u32[]{:S(2)}, u32[]{:S(2)}) collective-permute-start(bf16[2,80,1024]{2,1,0:T(8,128)(2,1)S(1)} %get-tuple-element.97), channel_id=1, source_target_pairs={{0,160},{16,112},{32,192},{48,144},{64,224},{80,176},{96,0},{112,2... | collective-permute-start | bytes 983048 | tf_op jit(solution)/shard_map/ppermute | solution.py:220
  155.7 37.2 %collective-permute-start.18 = (bf16[2,80,1024]{2,1,0:T(8,128)(2,1)S(1)}, bf16[2,80,1024]{2,1,0:T(8,128)(2,1)S(1)}, u32[]{:S(2)}, u32[]{:S(2)}) collective-permute-start(bf16[2,80,1024]{2,1,0:T(8,128)(2,1)S(1)} %get-tuple-element.95), channel_id=1, source_target_pairs={{0,192},{16,80},{32,224},{48,112},{64,0},{80,144},{96,32},{112,176... | collective-permute-start | bytes 983048 | tf_op jit(solution)/shard_map/ppermute | solution.py:220
  198.1 7.0 %copy-start.8 = (bf16[2,80,1024]{2,1,0:T(8,128)(2,1)S(1)}, bf16[2,80,1024]{2,1,0:T(8,128)(2,1)}, u32[]{:S(2)}) copy-start(bf16[2,80,1024]{2,1,0:T(8,128)(2,1)} %copy-done.7) | copy-start | bytes 983044
  198.1 7.0 %copy-start.10 = (bf16[2,80,1024]{2,1,0:T(8,128)(2,1)S(1)}, bf16[2,80,1024]{2,1,0:T(8,128)(2,1)}, u32[]{:S(2)}) copy-start(bf16[2,80,1024]{2,1,0:T(8,128)(2,1)} %copy-done.9) | copy-start | bytes 983044
  198.1 7.0 %copy-start.12 = (bf16[2,80,1024]{2,1,0:T(8,128)(2,1)S(1)}, bf16[2,80,1024]{2,1,0:T(8,128)(2,1)}, u32[]{:S(2)}) copy-start(bf16[2,80,1024]{2,1,0:T(8,128)(2,1)} %copy-done.11) | copy-start | bytes 983044
  198.1 7.0 %copy-start.14 = (bf16[2,80,1024]{2,1,0:T(8,128)(2,1)S(1)}, bf16[2,80,1024]{2,1,0:T(8,128)(2,1)}, u32[]{:S(2)}) copy-start(bf16[2,80,1024]{2,1,0:T(8,128)(2,1)} %copy-done.13) | copy-start | bytes 983044
  198.1 7.0 %copy-start.16 = (bf16[2,80,1024]{2,1,0:T(8,128)(2,1)S(1)}, bf16[2,80,1024]{2,1,0:T(8,128)(2,1)}, u32[]{:S(2)}) copy-start(bf16[2,80,1024]{2,1,0:T(8,128)(2,1)} %copy-done.15) | copy-start | bytes 983044
  198.1 16.5 %collective-permute-start.20 = (bf16[8,64,512]{2,1,0:T(8,128)(2,1)S(1)}, bf16[8,64,512]{2,1,0:T(8,128)(2,1)S(1)}, u32[]{:S(2)}, u32[]{:S(2)}) collective-permute-start(bf16[8,64,512]{2,1,0:T(8,128)(2,1)S(1)} %shard_map.45), channel_id=1, source_target_pairs={{0,256},{256,0},{1,257},{257,1},{2,258},{258,2},{3,259},{259,3},{4... | collective-permute-start | bytes 1572872 | tf_op jit(solution)/shard_map/ppermute | solution.py:325
  (22 other events, 38.8 us)

commit v6 on v4

--- a/solution.py
+++ b/solution.py
@@ -275,7 +275,7 @@
 
     rows_a, rows_b = bf16(8, HA, W * B), bf16(8, HB, W * B)
     send_a = pl.pallas_call(
-        pack_cols, out_shape=bf16(G, W + 1, HA, B), in_specs=[SMEM, ANY, ANY], out_specs=ANY,
+        pack_cols, out_shape=pltpu.HBM((G, W + 1, HA, B), jnp.bfloat16), in_specs=[SMEM, ANY, ANY], out_specs=ANY,
         scratch_shapes=[dma, dma], **params(moved=2 * MiB),
     )(maps, blocks, panel_column(tile, maps))
     own, swap = pl.pallas_call(

time: 219 us -> 218 us (level)
    unnamed x62 -> x60, local copies, waits for them, and re-layouts: 17.5 us -> 16.1 us
where the time goes in v6:
time: 218 us; the launch traced here: 216 us
  starting transfers between devices  112 us (51%)
  waiting for transfers between devices  47 us (22%)
  local copies, waits for them, and re-layouts  27.4 us (13%)
  Pallas kernels  21.6 us (10%)
  other arithmetic  7.25 us (3%)
    ppermute x14, starting transfers between devices, z_ring(): arrived[k] = lax.ppermute(both[k], 'row', pairs)  57.3 us
    ppermute x14, waiting for transfers between devices, z_ring(): arrived[k] = lax.ppermute(both[k], 'row', pairs)  30.4 us
    unnamed x60, local copies, waits for them, and re-layouts  16.1 us
    all_to_all x1, starting transfers between devices, shards(): pieces = lax.all_to_all(pieces, ('sib', 'row'), 0, 0, tiled=True)  13.5 us
    all_to_all x1, starting transfers between devices, shards(): got_b = lax.all_to_all(send_b, 'col', 0, 0, tiled=True)  12.4 us
    all_to_all x1, starting transfers between devices, shards(): got_a = lax.all_to_all(send_a, 'col', 0, 0, tiled=True)  8.6 us
    ppermute x3, starting transfers between devices, core_exchange(): return lax.ppermute(swap, 'row', [(i, i ^ 1) for i in range(G)])  6.24 us
    all_to_all x1, waiting for transfers between devices, shards(): got_a = lax.all_to_all(send_a, 'col', 0, 0, tiled=True)  5.46 us
  transfers between devices with their start and end apart: 24, of which 9 were waited for; matrix products, arithmetic and copies ran while one was open for 7% of the time, Pallas kernels for 8%

profile of v6, /device:TPU:6, one launch (start us, length us, event | category | flops | bytes accessed | tf_op | source)
XLA Modules:
  0.0 216.2 jit_solution(4841054737043556004)
XLA Ops:
  7.0 8.6 %all-to-all-start = ((bf16[16,9,64,128]{3,2,1,0:T(8,128)(2,1)}), bf16[16,9,64,128]{3,2,1,0:T(8,128)(2,1)S(1)}, u32[]{:S(2)}, u32[]{:S(2)}) async-start(bf16[16,9,64,128]{3,2,1,0:T(8,128)(2,1)} %shard_map.37), calls=%async_computation | async-start | bytes 4718592 | tf_op jit(solution)/shard_map/all_to_all | solution.py:285
  18.7 1.9 collective-permute-start
  23.6 2.0 fusion.16
  25.6 11.5 %collective-permute-start.2 = (bf16[2,64,1024]{2,1,0:T(8,128)(2,1)S(1)}, bf16[2,64,1024]{2,1,0:T(8,128)(2,1)S(1)}, u32[]{:S(2)}, u32[]{:S(2)}) collective-permute-start(bf16[2,64,1024]{2,1,0:T(8,128)(2,1)S(1)} %pad_maximum_fusion.1), channel_id=1, source_target_pairs={{0,224},{16,48},{32,0},{48,80},{64,32},{80,112},{96,64},{112,144},... | collective-permute-start | bytes 786440 | tf_op jit(solution)/shard_map/ppermute | solution.py:220
  37.2 2.3 %collective-permute-start.3 = (bf16[2,64,1024]{2,1,0:T(8,128)(2,1)S(1)}, bf16[2,64,1024]{2,1,0:T(8,128)(2,1)S(1)}, u32[]{:S(2)}, u32[]{:S(2)}) collective-permute-start(bf16[2,64,1024]{2,1,0:T(8,128)(2,1)S(1)} %pad_maximum_fusion.2), channel_id=1, source_target_pairs={{0,192},{16,80},{32,224},{48,112},{64,0},{80,144},{96,32},{112,176... | collective-permute-start | bytes 786440 | tf_op jit(solution)/shard_map/ppermute | solution.py:220
  39.5 2.1 collective-permute-start.4
  41.6 3.1 %collective-permute-start.1 = (s32[128]{0:T(128)S(1)}, s32[128]{0:T(128)S(1)}, u32[]{:S(2)}, u32[]{:S(2)}) collective-permute-start(s32[128]{0:T(128)S(1)} %bitcast.35), channel_id=1, source_target_pairs={{0,256},{256,0},{1,257},{257,1},{2,258},{258,2},{3,259},{259,3},{4... | collective-permute-start | bytes 1544 | tf_op jit(solution)/shard_map/ppermute | solution.py:287
  45.5 3.6 %collective-permute-start.5 = (bf16[2,64,1024]{2,1,0:T(8,128)(2,1)}, bf16[2,64,1024]{2,1,0:T(8,128)(2,1)S(1)}, u32[]{:S(2)}, u32[]{:S(2)}) collective-permute-start(bf16[2,64,1024]{2,1,0:T(8,128)(2,1)} %pad_maximum_fusion.5), channel_id=1, source_target_pairs={{0,32},{16,240},{32,64},{48,16},{64,96},{80,48},{96,128},{112,80},... | collective-permute-start | bytes 786440 | tf_op jit(solution)/shard_map/ppermute | solution.py:220
  51.3 4.6 %collective-permute-start.6 = (bf16[2,64,1024]{2,1,0:T(8,128)(2,1)}, bf16[2,64,1024]{2,1,0:T(8,128)(2,1)}, u32[]{:S(2)}, u32[]{:S(2)}) collective-permute-start(bf16[2,64,1024]{2,1,0:T(8,128)(2,1)} %pad_maximum_fusion.6), channel_id=1, source_target_pairs={{0,64},{16,208},{32,96},{48,240},{64,128},{80,16},{96,160},{112,48... | collective-permute-start | bytes 786440 | tf_op jit(solution)/shard_map/ppermute | solution.py:220
  55.9 5.2 %collective-permute-start.7 = (bf16[2,64,1024]{2,1,0:T(8,128)(2,1)}, bf16[2,64,1024]{2,1,0:T(8,128)(2,1)}, u32[]{:S(2)}, u32[]{:S(2)}) collective-permute-start(bf16[2,64,1024]{2,1,0:T(8,128)(2,1)} %pad_maximum_fusion.7), channel_id=1, source_target_pairs={{0,96},{16,176},{32,128},{48,208},{64,160},{80,240},{96,192},{112,... | collective-permute-start | bytes 786440 | tf_op jit(solution)/shard_map/ppermute | solution.py:220
  61.1 3.5 %collective-permute-start.8 = (bf16[2,64,1024]{2,1,0:T(8,128)(2,1)}, bf16[2,64,1024]{2,1,0:T(8,128)(2,1)}, u32[]{:S(2)}, u32[]{:S(2)}) collective-permute-start(bf16[2,64,1024]{2,1,0:T(8,128)(2,1)} %pad_maximum_fusion.8), channel_id=1, source_target_pairs={{0,128},{16,144},{32,160},{48,176},{64,192},{80,208},{96,224},{112... | collective-permute-start | bytes 786440 | tf_op jit(solution)/shard_map/ppermute | solution.py:220
  64.6 5.5 %all-to-all-done.arrived = bf16[16,9,64,128]{3,2,1,0:T(8,128)(2,1)S(1)} async-done(((bf16[16,9,64,128]{3,2,1,0:T(8,128)(2,1)}), bf16[16,9,64,128]{3,2,1,0:T(8,128)(2,1)S(1)}, u32[]{:S(2)}, u32[]{:S(2)}) %all-to-all-start) | async-done | bytes 2359328 | tf_op jit(solution)/shard_map/all_to_all | solution.py:285
  73.8 13.5 %all-to-all-start.1 = ((bf16[32,4,8,128]{3,2,1,0:T(8,128)(2,1)}), bf16[32,4,8,128]{3,2,1,0:T(8,128)(2,1)}, u32[]{:S(2)}, u32[]{:S(2)}) async-start(bf16[32,4,8,128]{3,2,1,0:T(8,128)(2,1)} %gather_fusion.1), calls=%async_computation.1 | async-start | bytes 524288 | tf_op jit(solution)/shard_map/all_to_all | solution.py:303
  89.9 2.2 %collective-permute-start.10 = (bf16[8,64,512]{2,1,0:T(8,128)(2,1)}, bf16[8,64,512]{2,1,0:T(8,128)(2,1)}, u32[]{:S(2)}, u32[]{:S(2)}) collective-permute-start(bf16[8,64,512]{2,1,0:T(8,128)(2,1)} %shard_map.41), channel_id=1, source_target_pairs={{0,256},{256,0},{1,257},{257,1},{2,258},{258,2},{3,259},{259,3},{4... | collective-permute-start | bytes 1572872 | tf_op jit(solution)/shard_map/ppermute | solution.py:298
  95.7 2.7 %shard_map.39.a = bf16[16,12,64,128]{3,2,1,0:T(8,128)(2,1)S(1)} custom-call(s32[128]{0:T(128)S(1)} %bitcast.36, s32[128]{0:T(128)S(1)} %select_reduce_fusion.1.inv_ref, bf16[2,64,1024]{2,1,0:T(8,128)(2,1)S(1)} %pad_maximum_fusion.4.refs_0_, bf16[2,64,1024]{2,1,0:T(8,128)(2,1)S(1)} %copy-done.26, bf16[2,64,1024]{2,1,0:T(8,128)(2,1)} %collective-permute-done.6.refs_2_, ...), custom_call_target="tpu_custom_call" | custom-call | bytes 2097152 | tf_op jit(solution)/shard_map/pallas_call | solution.py:299
  99.3 2.2 gather_fusion.2
  102.5 4.2 %collective-permute-start.9 = (bf16[32,512]{1,0:T(8,128)(2,1)S(1)}, bf16[32,512]{1,0:T(8,128)(2,1)S(1)}, u32[]{:S(2)}, u32[]{:S(2)}) collective-permute-start(bf16[32,512]{1,0:T(8,128)(2,1)S(1)} %constant_dynamic-slice_fusion), channel_id=1, source_target_pairs={{0,0},{1,16},{2,32},{3,48},{4,64},{5,80},{6,96},{7,112},{8,128},{9... | collective-permute-start | bytes 98312 | tf_op jit(solution)/shard_map/ppermute | solution.py:263
  109.7 2.4 %shard_map.42 = (bf16[8,64,1024]{2,1,0:T(8,128)(2,1)S(1)}, bf16[8,64,1024]{2,1,0:T(8,128)(2,1)S(1)}) custom-call(s32[128]{0:T(128)S(1)} %bitcast.37, s32[128]{0:T(128)S(1)} %collective-permute-done.1.map2_ref, s32[128]{0:T(128)S(1)} %select_reduce_fusion.1.inv_ref, bf16[16,9,64,128]{3,2,1,0:T(8,128)(2,1)S(1)} %copy-done.2, ...), custom_call_target="tpu_custom_call" | custom-call | bytes 2097152 | tf_op jit(solution)/shard_map/pallas_call | solution.py:304
  114.4 12.4 %all-to-all-start.2 = ((bf16[16,12,64,128]{3,2,1,0:T(8,128)(2,1)}), bf16[16,12,64,128]{3,2,1,0:T(8,128)(2,1)S(1)}, u32[]{:S(2)}, u32[]{:S(2)}) async-start(bf16[16,12,64,128]{3,2,1,0:T(8,128)(2,1)} %copy-done), calls=%async_computation.2 | async-start | bytes 6291456 | tf_op jit(solution)/shard_map/all_to_all | solution.py:316
  128.7 2.4 %collective-permute-start.12 = (bf16[16,1024]{1,0:T(8,128)(2,1)S(1)}, bf16[16,1024]{1,0:T(8,128)(2,1)S(1)}, u32[]{:S(2)}, u32[]{:S(2)}) collective-permute-start(bf16[16,1024]{1,0:T(8,128)(2,1)S(1)} %pad_maximum_fusion.9), channel_id=1, source_target_pairs={{0,16},{16,0},{32,48},{48,32},{64,80},{80,64},{96,112},{112,96},{1... | collective-permute-start | bytes 98312 | tf_op jit(solution)/shard_map/ppermute | solution.py:209
  132.8 2.2 %collective-permute-start.13 = (bf16[2,80,1024]{2,1,0:T(8,128)(2,1)S(1)}, bf16[2,80,1024]{2,1,0:T(8,128)(2,1)S(1)}, u32[]{:S(2)}, u32[]{:S(2)}) collective-permute-start(bf16[2,80,1024]{2,1,0:T(8,128)(2,1)S(1)} %get-tuple-element.94), channel_id=1, source_target_pairs={{0,32},{16,240},{32,64},{48,16},{64,96},{80,48},{96,128},{112,80},... | collective-permute-start | bytes 983048 | tf_op jit(solution)/shard_map/ppermute | solution.py:220
  135.1 1.9 collective-permute-start.14
  138.9 4.9 %collective-permute-start.19 = (bf16[2,80,1024]{2,1,0:T(8,128)(2,1)S(1)}, bf16[2,80,1024]{2,1,0:T(8,128)(2,1)S(1)}, u32[]{:S(2)}, u32[]{:S(2)}) collective-permute-start(bf16[2,80,1024]{2,1,0:T(8,128)(2,1)S(1)} %get-tuple-element.93), channel_id=1, source_target_pairs={{0,224},{16,48},{32,0},{48,80},{64,32},{80,112},{96,64},{112,144},... | collective-permute-start | bytes 983048 | tf_op jit(solution)/shard_map/ppermute | solution.py:220
  144.0 8.0 %collective-permute-start.16 = (bf16[2,80,1024]{2,1,0:T(8,128)(2,1)S(1)}, bf16[2,80,1024]{2,1,0:T(8,128)(2,1)S(1)}, u32[]{:S(2)}, u32[]{:S(2)}) collective-permute-start(bf16[2,80,1024]{2,1,0:T(8,128)(2,1)S(1)} %get-tuple-element.98), channel_id=1, source_target_pairs={{0,128},{16,144},{32,160},{48,176},{64,192},{80,208},{96,224},{112... | collective-permute-start | bytes 983048 | tf_op jit(solution)/shard_map/ppermute | solution.py:220
  155.4 3.6 %collective-permute-start.18 = (bf16[2,80,1024]{2,1,0:T(8,128)(2,1)S(1)}, bf16[2,80,1024]{2,1,0:T(8,128)(2,1)S(1)}, u32[]{:S(2)}, u32[]{:S(2)}) collective-permute-start(bf16[2,80,1024]{2,1,0:T(8,128)(2,1)S(1)} %get-tuple-element.97), channel_id=1, source_target_pairs={{0,192},{16,80},{32,224},{48,112},{64,0},{80,144},{96,32},{112,176... | collective-permute-start | bytes 983048 | tf_op jit(solution)/shard_map/ppermute | solution.py:220
  159.0 25.1 %collective-permute-done.15.refs_3_ = bf16[2,80,1024]{2,1,0:T(8,128)(2,1)S(1)} collective-permute-done((bf16[2,80,1024]{2,1,0:T(8,128)(2,1)S(1)}, bf16[2,80,1024]{2,1,0:T(8,128)(2,1)S(1)}, u32[]{:S(2)}, u32[]{:S(2)}) %collective-permute-start.15) | collective-permute-done | bytes 327712 | tf_op jit(solution)/shard_map/ppermute | solution.py:220
  188.2 4.2 %collective-permute-done.18.refs_6_ = bf16[2,80,1024]{2,1,0:T(8,128)(2,1)S(1)} collective-permute-done((bf16[2,80,1024]{2,1,0:T(8,128)(2,1)S(1)}, bf16[2,80,1024]{2,1,0:T(8,128)(2,1)S(1)}, u32[]{:S(2)}, u32[]{:S(2)}) %collective-permute-start.18) | collective-permute-done | bytes 327712 | tf_op jit(solution)/shard_map/ppermute | solution.py:220
  193.1 3.7 %all-to-all-done.2.arrived.refs_8_ = bf16[16,12,64,128]{3,2,1,0:T(8,128)(2,1)S(1)} async-done(((bf16[16,12,64,128]{3,2,1,0:T(8,128)(2,1)}), bf16[16,12,64,128]{3,2,1,0:T(8,128)(2,1)S(1)}, u32[]{:S(2)}, u32[]{:S(2)}) %all-to-all-start.2) | async-done | bytes 3145760 | tf_op jit(solution)/shard_map/all_to_all | solution.py:316
  197.6 4.1 %collective-permute-start.20 = (bf16[8,64,512]{2,1,0:T(8,128)(2,1)S(1)}, bf16[8,64,512]{2,1,0:T(8,128)(2,1)S(1)}, u32[]{:S(2)}, u32[]{:S(2)}) collective-permute-start(bf16[8,64,512]{2,1,0:T(8,128)(2,1)S(1)} %shard_map.45), channel_id=1, source_target_pairs={{0,256},{256,0},{1,257},{257,1},{2,258},{258,2},{3,259},{259,3},{4... | collective-permute-start | bytes 1572872 | tf_op jit(solution)/shard_map/ppermute | solution.py:326
  201.7 2.7 %shard_map.43.refs_9_ = bf16[1024,512]{1,0:T(8,128)(2,1)S(1)} custom-call(bf16[16,12,64,128]{3,2,1,0:T(8,128)(2,1)S(1)} %all-to-all-done.2.arrived.refs_8_, bf16[512,512]{1,0:T(8,128)(2,1)S(1)} %copy-done.5), custom_call_target="tpu_custom_call" | custom-call | flops 536870912 | bytes 2097152 | tf_op jit(solution)/shard_map/pallas_call | solution.py:327
  204.5 5.3 %shard_map.44.base = f32[8,128,512]{2,1,0:T(8,128)S(1)} custom-call(s32[128]{0:T(128)S(1)} %select_reduce_fusion.1.inv_ref, s32[128]{0:T(128)S(1)} %select_reduce_fusion.inv2_ref, bf16[2,80,1024]{2,1,0:T(8,128)(2,1)S(1)} %get-tuple-element.52.refs_0_, bf16[2,80,1024]{2,1,0:T(8,128)(2,1)S(1)} %copy-done.8, bf16[2,80,1024]{2,1,0:T(8,128)(2,1)S(1)} %copy-done.10, ...), custom_call_target="tpu_custom_call" | custom-call | flops 805306368 | bytes 6291456 | tf_op jit(solution)/shard_map/pallas_call | solution.py:333
  209.8 4.6 %collective-permute-done.20.got_b = bf16[8,64,512]{2,1,0:T(8,128)(2,1)S(1)} collective-permute-done((bf16[8,64,512]{2,1,0:T(8,128)(2,1)S(1)}, bf16[8,64,512]{2,1,0:T(8,128)(2,1)S(1)}, u32[]{:S(2)}, u32[]{:S(2)}) %collective-permute-start.20) | collective-permute-done | bytes 524320 | tf_op jit(solution)/shard_map/ppermute | solution.py:326
  (125 shorter events, 48.7 us)
Async XLA Ops:
  7.0 8.6 %copy-start.28 = (s32[1,128]{1,0:T(1,128)S(1)}, s32[1,128]{1,0:T(1,128)}, u32[]{:S(2)}) copy-start(s32[1,128]{1,0:T(1,128)} %param.4) | copy-start | bytes 1540
  7.0 63.1 %all-to-all-start = ((bf16[16,9,64,128]{3,2,1,0:T(8,128)(2,1)}), bf16[16,9,64,128]{3,2,1,0:T(8,128)(2,1)S(1)}, u32[]{:S(2)}, u32[]{:S(2)}) async-start(bf16[16,9,64,128]{3,2,1,0:T(8,128)(2,1)} %shard_map.37), calls=%async_computation | async-start | bytes 4718592 | tf_op jit(solution)/shard_map/all_to_all | solution.py:285
  18.7 4.9 %collective-permute-start = (bf16[8,64,1024]{2,1,0:T(8,128)(2,1)}, bf16[8,64,1024]{2,1,0:T(8,128)(2,1)}, u32[]{:S(2)}, u32[]{:S(2)}) collective-permute-start(bf16[8,64,1024]{2,1,0:T(8,128)(2,1)} %get-tuple-element.33), channel_id=1, source_target_pairs={{0,16},{16,0},{32,48},{48,32},{64,80},{80,64},{96,112},{112,96},{1... | collective-permute-start | bytes 3145736 | tf_op jit(solution)/shard_map/ppermute | solution.py:209
  25.6 30.2 %collective-permute-start.2 = (bf16[2,64,1024]{2,1,0:T(8,128)(2,1)S(1)}, bf16[2,64,1024]{2,1,0:T(8,128)(2,1)S(1)}, u32[]{:S(2)}, u32[]{:S(2)}) collective-permute-start(bf16[2,64,1024]{2,1,0:T(8,128)(2,1)S(1)} %pad_maximum_fusion.1), channel_id=1, source_target_pairs={{0,224},{16,48},{32,0},{48,80},{64,32},{80,112},{96,64},{112,144},... | collective-permute-start | bytes 786440 | tf_op jit(solution)/shard_map/ppermute | solution.py:220
  37.2 23.9 %collective-permute-start.3 = (bf16[2,64,1024]{2,1,0:T(8,128)(2,1)S(1)}, bf16[2,64,1024]{2,1,0:T(8,128)(2,1)S(1)}, u32[]{:S(2)}, u32[]{:S(2)}) collective-permute-start(bf16[2,64,1024]{2,1,0:T(8,128)(2,1)S(1)} %pad_maximum_fusion.2), channel_id=1, source_target_pairs={{0,192},{16,80},{32,224},{48,112},{64,0},{80,144},{96,32},{112,176... | collective-permute-start | bytes 786440 | tf_op jit(solution)/shard_map/ppermute | solution.py:220
  39.5 25.1 %collective-permute-start.4 = (bf16[2,64,1024]{2,1,0:T(8,128)(2,1)S(1)}, bf16[2,64,1024]{2,1,0:T(8,128)(2,1)S(1)}, u32[]{:S(2)}, u32[]{:S(2)}) collective-permute-start(bf16[2,64,1024]{2,1,0:T(8,128)(2,1)S(1)} %pad_maximum_fusion.3), channel_id=1, source_target_pairs={{0,160},{16,112},{32,192},{48,144},{64,224},{80,176},{96,0},{112,2... | collective-permute-start | bytes 786440 | tf_op jit(solution)/shard_map/ppermute | solution.py:220
  41.6 9.6 %collective-permute-start.1 = (s32[128]{0:T(128)S(1)}, s32[128]{0:T(128)S(1)}, u32[]{:S(2)}, u32[]{:S(2)}) collective-permute-start(s32[128]{0:T(128)S(1)} %bitcast.35), channel_id=1, source_target_pairs={{0,256},{256,0},{1,257},{257,1},{2,258},{258,2},{3,259},{259,3},{4... | collective-permute-start | bytes 1544 | tf_op jit(solution)/shard_map/ppermute | solution.py:287
  45.5 46.6 %collective-permute-start.5 = (bf16[2,64,1024]{2,1,0:T(8,128)(2,1)}, bf16[2,64,1024]{2,1,0:T(8,128)(2,1)S(1)}, u32[]{:S(2)}, u32[]{:S(2)}) collective-permute-start(bf16[2,64,1024]{2,1,0:T(8,128)(2,1)} %pad_maximum_fusion.5), channel_id=1, source_target_pairs={{0,32},{16,240},{32,64},{48,16},{64,96},{80,48},{96,128},{112,80},... | collective-permute-start | bytes 786440 | tf_op jit(solution)/shard_map/ppermute | solution.py:220
  51.3 41.5 %collective-permute-start.6 = (bf16[2,64,1024]{2,1,0:T(8,128)(2,1)}, bf16[2,64,1024]{2,1,0:T(8,128)(2,1)}, u32[]{:S(2)}, u32[]{:S(2)}) collective-permute-start(bf16[2,64,1024]{2,1,0:T(8,128)(2,1)} %pad_maximum_fusion.6), channel_id=1, source_target_pairs={{0,64},{16,208},{32,96},{48,240},{64,128},{80,16},{96,160},{112,48... | collective-permute-start | bytes 786440 | tf_op jit(solution)/shard_map/ppermute | solution.py:220
  55.9 36.9 %collective-permute-start.7 = (bf16[2,64,1024]{2,1,0:T(8,128)(2,1)}, bf16[2,64,1024]{2,1,0:T(8,128)(2,1)}, u32[]{:S(2)}, u32[]{:S(2)}) collective-permute-start(bf16[2,64,1024]{2,1,0:T(8,128)(2,1)} %pad_maximum_fusion.7), channel_id=1, source_target_pairs={{0,96},{16,176},{32,128},{48,208},{64,160},{80,240},{96,192},{112,... | collective-permute-start | bytes 786440 | tf_op jit(solution)/shard_map/ppermute | solution.py:220
  61.1 28.8 %copy-start.21 = (bf16[2,64,1024]{2,1,0:T(8,128)(2,1)}, bf16[2,64,1024]{2,1,0:T(8,128)(2,1)S(1)}, u32[]{:S(2)}) copy-start(bf16[2,64,1024]{2,1,0:T(8,128)(2,1)S(1)} %collective-permute-done.3.refs_6_) | copy-start | bytes 786436
  61.1 31.7 %collective-permute-start.8 = (bf16[2,64,1024]{2,1,0:T(8,128)(2,1)}, bf16[2,64,1024]{2,1,0:T(8,128)(2,1)}, u32[]{:S(2)}, u32[]{:S(2)}) collective-permute-start(bf16[2,64,1024]{2,1,0:T(8,128)(2,1)} %pad_maximum_fusion.8), channel_id=1, source_target_pairs={{0,128},{16,144},{32,160},{48,176},{64,192},{80,208},{96,224},{112... | collective-permute-start | bytes 786440 | tf_op jit(solution)/shard_map/ppermute | solution.py:220
  64.6 25.3 %copy-start.23 = (bf16[2,64,1024]{2,1,0:T(8,128)(2,1)}, bf16[2,64,1024]{2,1,0:T(8,128)(2,1)S(1)}, u32[]{:S(2)}) copy-start(bf16[2,64,1024]{2,1,0:T(8,128)(2,1)S(1)} %collective-permute-done.4.refs_5_) | copy-start | bytes 786436
  70.1 19.8 %copy-start.1 = (bf16[16,9,64,128]{3,2,1,0:T(8,128)(2,1)}, bf16[16,9,64,128]{3,2,1,0:T(8,128)(2,1)S(1)}, u32[]{:S(2)}) copy-start(bf16[16,9,64,128]{3,2,1,0:T(8,128)(2,1)S(1)} %all-to-all-done.arrived) | copy-start | bytes 7077892
  73.8 25.5 %all-to-all-start.1 = ((bf16[32,4,8,128]{3,2,1,0:T(8,128)(2,1)}), bf16[32,4,8,128]{3,2,1,0:T(8,128)(2,1)}, u32[]{:S(2)}, u32[]{:S(2)}) async-start(bf16[32,4,8,128]{3,2,1,0:T(8,128)(2,1)} %gather_fusion.1), calls=%async_computation.1 | async-start | bytes 524288 | tf_op jit(solution)/shard_map/all_to_all | solution.py:303
  89.9 19.9 %collective-permute-start.10 = (bf16[8,64,512]{2,1,0:T(8,128)(2,1)}, bf16[8,64,512]{2,1,0:T(8,128)(2,1)}, u32[]{:S(2)}, u32[]{:S(2)}) collective-permute-start(bf16[8,64,512]{2,1,0:T(8,128)(2,1)} %shard_map.41), channel_id=1, source_target_pairs={{0,256},{256,0},{1,257},{257,1},{2,258},{258,2},{3,259},{259,3},{4... | collective-permute-start | bytes 1572872 | tf_op jit(solution)/shard_map/ppermute | solution.py:298
  102.5 11.9 %collective-permute-start.9 = (bf16[32,512]{1,0:T(8,128)(2,1)S(1)}, bf16[32,512]{1,0:T(8,128)(2,1)S(1)}, u32[]{:S(2)}, u32[]{:S(2)}) collective-permute-start(bf16[32,512]{1,0:T(8,128)(2,1)S(1)} %constant_dynamic-slice_fusion), channel_id=1, source_target_pairs={{0,0},{1,16},{2,32},{3,48},{4,64},{5,80},{6,96},{7,112},{8,128},{9... | collective-permute-start | bytes 98312 | tf_op jit(solution)/shard_map/ppermute | solution.py:263
  114.4 82.4 %all-to-all-start.2 = ((bf16[16,12,64,128]{3,2,1,0:T(8,128)(2,1)}), bf16[16,12,64,128]{3,2,1,0:T(8,128)(2,1)S(1)}, u32[]{:S(2)}, u32[]{:S(2)}) async-start(bf16[16,12,64,128]{3,2,1,0:T(8,128)(2,1)} %copy-done), calls=%async_computation.2 | async-start | bytes 6291456 | tf_op jit(solution)/shard_map/all_to_all | solution.py:316
  126.8 5.7 %collective-permute-start.11 = (bf16[8,64,1024]{2,1,0:T(8,128)(2,1)}, bf16[8,64,1024]{2,1,0:T(8,128)(2,1)S(1)}, u32[]{:S(2)}, u32[]{:S(2)}) collective-permute-start(bf16[8,64,1024]{2,1,0:T(8,128)(2,1)} %copy-done.29), channel_id=1, source_target_pairs={{0,16},{16,0},{32,48},{48,32},{64,80},{80,64},{96,112},{112,96},{1... | collective-permute-start | bytes 3145736 | tf_op jit(solution)/shard_map/ppermute | solution.py:209
  128.7 3.9 %collective-permute-start.12 = (bf16[16,1024]{1,0:T(8,128)(2,1)S(1)}, bf16[16,1024]{1,0:T(8,128)(2,1)S(1)}, u32[]{:S(2)}, u32[]{:S(2)}) collective-permute-start(bf16[16,1024]{1,0:T(8,128)(2,1)S(1)} %pad_maximum_fusion.9), channel_id=1, source_target_pairs={{0,16},{16,0},{32,48},{48,32},{64,80},{80,64},{96,112},{112,96},{1... | collective-permute-start | bytes 98312 | tf_op jit(solution)/shard_map/ppermute | solution.py:209
  132.8 19.2 %collective-permute-start.13 = (bf16[2,80,1024]{2,1,0:T(8,128)(2,1)S(1)}, bf16[2,80,1024]{2,1,0:T(8,128)(2,1)S(1)}, u32[]{:S(2)}, u32[]{:S(2)}) collective-permute-start(bf16[2,80,1024]{2,1,0:T(8,128)(2,1)S(1)} %get-tuple-element.94), channel_id=1, source_target_pairs={{0,32},{16,240},{32,64},{48,16},{64,96},{80,48},{96,128},{112,80},... | collective-permute-start | bytes 983048 | tf_op jit(solution)/shard_map/ppermute | solution.py:220
  135.1 19.6 %collective-permute-start.14 = (bf16[2,80,1024]{2,1,0:T(8,128)(2,1)S(1)}, bf16[2,80,1024]{2,1,0:T(8,128)(2,1)S(1)}, u32[]{:S(2)}, u32[]{:S(2)}) collective-permute-start(bf16[2,80,1024]{2,1,0:T(8,128)(2,1)S(1)} %get-tuple-element.95), channel_id=1, source_target_pairs={{0,64},{16,208},{32,96},{48,240},{64,128},{80,16},{96,160},{112,48... | collective-permute-start | bytes 983048 | tf_op jit(solution)/shard_map/ppermute | solution.py:220
  137.0 47.1 %collective-permute-start.15 = (bf16[2,80,1024]{2,1,0:T(8,128)(2,1)S(1)}, bf16[2,80,1024]{2,1,0:T(8,128)(2,1)S(1)}, u32[]{:S(2)}, u32[]{:S(2)}) collective-permute-start(bf16[2,80,1024]{2,1,0:T(8,128)(2,1)S(1)} %get-tuple-element.96), channel_id=1, source_target_pairs={{0,96},{16,176},{32,128},{48,208},{64,160},{80,240},{96,192},{112,... | collective-permute-start | bytes 983048 | tf_op jit(solution)/shard_map/ppermute | solution.py:220
  138.9 45.9 %collective-permute-start.19 = (bf16[2,80,1024]{2,1,0:T(8,128)(2,1)S(1)}, bf16[2,80,1024]{2,1,0:T(8,128)(2,1)S(1)}, u32[]{:S(2)}, u32[]{:S(2)}) collective-permute-start(bf16[2,80,1024]{2,1,0:T(8,128)(2,1)S(1)} %get-tuple-element.93), channel_id=1, source_target_pairs={{0,224},{16,48},{32,0},{48,80},{64,32},{80,112},{96,64},{112,144},... | collective-permute-start | bytes 983048 | tf_op jit(solution)/shard_map/ppermute | solution.py:220
  144.0 41.6 %collective-permute-start.16 = (bf16[2,80,1024]{2,1,0:T(8,128)(2,1)S(1)}, bf16[2,80,1024]{2,1,0:T(8,128)(2,1)S(1)}, u32[]{:S(2)}, u32[]{:S(2)}) collective-permute-start(bf16[2,80,1024]{2,1,0:T(8,128)(2,1)S(1)} %get-tuple-element.98), channel_id=1, source_target_pairs={{0,128},{16,144},{32,160},{48,176},{64,192},{80,208},{96,224},{112... | collective-permute-start | bytes 983048 | tf_op jit(solution)/shard_map/ppermute | solution.py:220
  152.8 34.7 %collective-permute-start.17 = (bf16[2,80,1024]{2,1,0:T(8,128)(2,1)S(1)}, bf16[2,80,1024]{2,1,0:T(8,128)(2,1)S(1)}, u32[]{:S(2)}, u32[]{:S(2)}) collective-permute-start(bf16[2,80,1024]{2,1,0:T(8,128)(2,1)S(1)} %get-tuple-element.99), channel_id=1, source_target_pairs={{0,160},{16,112},{32,192},{48,144},{64,224},{80,176},{96,0},{112,2... | collective-permute-start | bytes 983048 | tf_op jit(solution)/shard_map/ppermute | solution.py:220
  155.4 36.9 %collective-permute-start.18 = (bf16[2,80,1024]{2,1,0:T(8,128)(2,1)S(1)}, bf16[2,80,1024]{2,1,0:T(8,128)(2,1)S(1)}, u32[]{:S(2)}, u32[]{:S(2)}) collective-permute-start(bf16[2,80,1024]{2,1,0:T(8,128)(2,1)S(1)} %get-tuple-element.97), channel_id=1, source_target_pairs={{0,192},{16,80},{32,224},{48,112},{64,0},{80,144},{96,32},{112,176... | collective-permute-start | bytes 983048 | tf_op jit(solution)/shard_map/ppermute | solution.py:220
  197.5 6.9 %copy-start.8 = (bf16[2,80,1024]{2,1,0:T(8,128)(2,1)S(1)}, bf16[2,80,1024]{2,1,0:T(8,128)(2,1)}, u32[]{:S(2)}) copy-start(bf16[2,80,1024]{2,1,0:T(8,128)(2,1)} %copy-done.7) | copy-start | bytes 983044
  197.5 6.9 %copy-start.10 = (bf16[2,80,1024]{2,1,0:T(8,128)(2,1)S(1)}, bf16[2,80,1024]{2,1,0:T(8,128)(2,1)}, u32[]{:S(2)}) copy-start(bf16[2,80,1024]{2,1,0:T(8,128)(2,1)} %copy-done.9) | copy-start | bytes 983044
  197.5 6.9 %copy-start.12 = (bf16[2,80,1024]{2,1,0:T(8,128)(2,1)S(1)}, bf16[2,80,1024]{2,1,0:T(8,128)(2,1)}, u32[]{:S(2)}) copy-start(bf16[2,80,1024]{2,1,0:T(8,128)(2,1)} %copy-done.11) | copy-start | bytes 983044
  197.5 6.9 %copy-start.14 = (bf16[2,80,1024]{2,1,0:T(8,128)(2,1)S(1)}, bf16[2,80,1024]{2,1,0:T(8,128)(2,1)}, u32[]{:S(2)}) copy-start(bf16[2,80,1024]{2,1,0:T(8,128)(2,1)} %copy-done.13) | copy-start | bytes 983044
  197.6 16.8 %collective-permute-start.20 = (bf16[8,64,512]{2,1,0:T(8,128)(2,1)S(1)}, bf16[8,64,512]{2,1,0:T(8,128)(2,1)S(1)}, u32[]{:S(2)}, u32[]{:S(2)}) collective-permute-start(bf16[8,64,512]{2,1,0:T(8,128)(2,1)S(1)} %shard_map.45), channel_id=1, source_target_pairs={{0,256},{256,0},{1,257},{257,1},{2,258},{258,2},{3,259},{259,3},{4... | collective-permute-start | bytes 1572872 | tf_op jit(solution)/shard_map/ppermute | solution.py:326
  (22 other events, 44.8 us)
